TPU v7x, 32 devices: a whole 2x2x4 slice. The times are simulated.
32 devices in a mesh: dp: 8 (over z, y), mp: 4 (over x, core).
Axes of the slice: x: 2, y: 2, z: 4, core: 2. Of those that a mesh axis runs over, the one named last changes fastest.
Arguments:
- tokens: bfloat16 [2, 8192, 1024], P(None, 'dp'), may hold values from -6 to 6
- cotangent: bfloat16 [2, 8192, 1024], P(None, 'dp'), may hold values from -6 to 6
- lengths: int32 [2, 8, 4], P(None, 'dp'), may hold values from 1 to 768, 1024 in all within a row
- placement_ids: int32 [2, 8192], replicated, may hold values from 0 to 8191, as said below
- block_slot_index: int32 [12], replicated, may hold values from 0 to 15, as said below
- matrices: float32 [1024, 12, 1024], P('dp', None, 'mp')
- norm_vectors: float32 [6, 1024], P(None, 'dp')
- head_vectors: float32 [6, 1024], P(None, 'mp'), may hold values from -3 to 3
- left_stats: float32 [16, 1024, 1024], P('dp', 'mp'), as said below
- right_stats: float32 [16, 1024, 1024], P('dp', 'mp'), as said below
- left_roots: float32 [16, 1024, 1024], P('dp'), as said below
- right_roots: float32 [16, 1024, 1024], P('dp', 'mp'), as said below
- norm_state: float32 [6, 1024], P(None, 'dp'), may hold values from 16384 to 65536
- head_state: float32 [6, 1024], P(None, 'mp'), may hold values from 2048 to 32768
Outputs:
- block_output: bfloat16 [2, 8192, 1024], P(None, 'dp')
- input_grad: bfloat16 [2, 8192, 1024], P(None, 'dp')
- slot_block_grads: float32 [1024, 16, 1024], P(None, 'dp', 'mp')
- new_left: float32 [16, 1024, 1024], P('dp', 'mp')
- new_right: float32 [16, 1024, 1024], P('dp', 'mp')
- updated_blocks: float32 [1024, 16, 1024], P(None, 'dp', 'mp')
- norm_grads: float32 [6, 1024], P(None, 'dp')
- new_norm_state: float32 [6, 1024], P(None, 'dp')
- new_norm_vectors: float32 [6, 1024], P(None, 'dp')
- head_grads: float32 [6, 1024], P(None, 'mp')
- new_head_state: float32 [6, 1024], P(None, 'mp')
- new_head_vectors: float32 [6, 1024], P(None, 'mp')
Inputs may be any that keep to these rules, and one draw needn't show every extreme that they name: `placement_ids`: for each micro-batch a permutation of the rows; balanced rows q * 1024 to q * 1024 + 1023 belong to dp device q, and of the 1024 given rows that dp device p holds exactly 128 go to each dp device. `block_slot_index`: distinct slots; slot o belongs to dp device o // 2. `right_roots`: symmetric in its last two dimensions. `left_roots`: symmetric in its last two dimensions. `left_stats`: symmetric in its last two dimensions. `right_stats`: symmetric in its last two dimensions.
All inputs are finite; a program needn't handle non-finite values.
Results may differ from a plain program's by a relative error of at most 0.01.
The roundings to bfloat16 on the way count: a program that leaves them out, or rounds other values in their place, can miss the bound.
Values may be sent and summed in bfloat16 or wider, within the bound.
No kernel may reach another device: no remote copies, remote signals or barrier semaphores. Data moves between devices by JAX's collectives and lax.ppermute only.
A program may use at most 256 MiB of HBM per device.

v0:
```python
import math

import jax
import jax.numpy as jnp
from jax import lax
from jax.sharding import PartitionSpec as P

HEAD_DIM = 64


stat_decay = 0.5
matrix_rate = 0.02
vector_rate = 0.3
norm_eps = 1e-05
mean_eps = 1e-06
diag_eps = 1e-08
masked_score = -1000000000.0


def layer_norm(values, gain, shift):
    center = values - jnp.mean(values, axis=-1, keepdims=True)
    spread = jnp.mean(center * center, axis=-1, keepdims=True)
    return center * lax.rsqrt(spread + norm_eps) * gain + shift


def norm_back(values, gain, grad_normed):
    center = values - jnp.mean(values, axis=-1, keepdims=True)
    spread = jnp.mean(center * center, axis=-1, keepdims=True)
    scale_rows = lax.rsqrt(spread + norm_eps)
    unit_rows = center * scale_rows
    grad_unit = grad_normed * gain
    grad_values = scale_rows * (
        grad_unit
        - jnp.mean(grad_unit, axis=-1, keepdims=True)
        - unit_rows * jnp.mean(grad_unit * unit_rows, axis=-1, keepdims=True)
    )
    return (grad_values, grad_normed * unit_rows)


def model_rows(left, right):
    return lax.psum(jnp.einsum("qk,mk->qm", left, right, preferred_element_type=jnp.float32), "mp")


def on_device(
    tokens,
    cotangent,
    lengths,
    placement_ids,
    block_slot_index,
    matrices,
    norm_vectors,
    head_vectors,
    left_stats,
    right_stats,
    left_roots,
    right_roots,
    norm_state,
    head_state,
):
    f32 = jnp.float32
    low_type = jnp.bfloat16
    data_count = lax.axis_size("dp")
    data_index = lax.axis_index("dp")
    model_count = lax.axis_size("mp")
    model_index = lax.axis_index("mp")
    micro_count, rows_here, model_width = tokens.shape
    piece_rows = rows_here // data_count
    share_rows = rows_here // model_count
    row_start = 0
    stat_offset = model_index * share_rows - row_start

    def share_sum(values):
        return jnp.sum(lax.dynamic_slice_in_dim(values, stat_offset, share_rows, 0), axis=0)

    blocks = matrices.shape[1]
    local_cols = matrices.shape[2]
    ffn_count = (blocks - 4) // 2
    local_heads = local_cols // HEAD_DIM
    score_scale = 1.0 / math.sqrt(HEAD_DIM)
    positions = jnp.arange(rows_here)
    causal = positions[:, None] >= positions[None, :]
    shipped = (matrices.astype(low_type), norm_vectors.astype(low_type))
    weight_grads = jnp.zeros((model_width, blocks, local_cols), f32)
    norm_grads_local = jnp.zeros((6, model_width), f32)
    head_grads_local = jnp.zeros(head_vectors.shape, f32)
    outputs_given = []
    inputs_given = []
    for micro_index in range(micro_count):
        weights_now, norms_now = (
            lax.all_gather(shipped[0], "dp", axis=0, tiled=True),
            lax.all_gather(shipped[1], "dp", axis=1, tiled=True),
        )
        dest_all = placement_ids[micro_index]
        dest_mine = lax.dynamic_slice_in_dim(dest_all, data_index * rows_here, rows_here)
        send_order = jnp.argsort(dest_mine)
        sent_rows = tokens[micro_index][send_order].reshape(data_count, piece_rows, model_width)
        sent_grads = cotangent[micro_index][send_order].reshape(data_count, piece_rows, model_width)
        got_rows, got_grads = (
            lax.all_to_all(sent_rows, "dp", split_axis=0, concat_axis=0, tiled=True),
            lax.all_to_all(sent_grads, "dp", split_axis=0, concat_axis=0, tiled=True),
        )
        source_rows = jnp.argsort(dest_all)
        source_mine = (
            lax.dynamic_slice_in_dim(source_rows, data_index * rows_here, rows_here) // rows_here
        )
        arrival_order = jnp.argsort(source_mine * rows_here + positions)
        arrival_rank = jnp.argsort(arrival_order)
        rows_bal = got_rows.reshape(rows_here, model_width)[arrival_rank]
        grads_bal = got_grads.reshape(rows_here, model_width)[arrival_rank]
        bounds = jnp.cumsum(lengths[micro_index, 0])
        segment = jnp.sum((positions[:, None] >= bounds[None, :]).astype(jnp.int32), axis=1)
        keep_rows = (segment < lengths.shape[2] - 1).astype(f32)
        allowed = causal & (segment[:, None] == segment[None, :])
        rows_float = rows_bal.astype(f32)
        normed_low = layer_norm(
            rows_float, norms_now[0].astype(f32), norms_now[1].astype(f32)
        ).astype(low_type)
        w_qkv = weights_now[:, 0:3, :].reshape(model_width, 3 * local_cols)
        qkv_all = jnp.dot(normed_low, w_qkv, preferred_element_type=f32)
        queries = (qkv_all[:, :local_cols] + head_vectors[0]).astype(low_type)
        keys_all = qkv_all[:, local_cols : 2 * local_cols].astype(low_type)
        values = (qkv_all[:, 2 * local_cols :] + head_vectors[1]).astype(low_type)
        query_heads = queries.reshape(rows_here, local_heads, HEAD_DIM)
        key_heads = keys_all.reshape(rows_here, local_heads, HEAD_DIM)
        value_heads = values.reshape(rows_here, local_heads, HEAD_DIM)
        scores = (
            jnp.einsum("qhd,khd->hqk", query_heads, key_heads, preferred_element_type=f32)
            * score_scale
        )
        scores = jnp.where(allowed[None], scores, masked_score)
        attention = jax.nn.softmax(scores, axis=-1)
        attention_low = attention.astype(low_type)
        attended = jnp.einsum(
            "hqk,khd->qhd", attention_low, value_heads, preferred_element_type=f32
        )
        attended = attended.reshape(rows_here, local_cols).astype(low_type)
        branch_own = model_rows(attended, weights_now[:, 3, :])
        hidden_own = rows_float + branch_own + norms_now[2].astype(f32)
        normed_two = layer_norm(
            hidden_own, norms_now[3].astype(f32), norms_now[4].astype(f32)
        ).astype(low_type)
        w_up = weights_now[:, 4 : 4 + ffn_count, :].reshape(model_width, ffn_count * local_cols)
        w_down = weights_now[:, 4 + ffn_count :, :].reshape(model_width, ffn_count * local_cols)
        up_in = jnp.dot(normed_two, w_up, preferred_element_type=f32) + head_vectors[2:].reshape(-1)
        active, gelu_pull = jax.vjp(lambda v: jax.nn.gelu(v, approximate=True), up_in)
        active_low = active.astype(low_type)
        feed_own = model_rows(active_low, w_down)
        output_own = (hidden_own + feed_own + norms_now[5].astype(f32)).astype(low_type)
        weights_back, norms_back = (
            lax.all_gather(shipped[0], "dp", axis=0, tiled=True),
            lax.all_gather(shipped[1], "dp", axis=1, tiled=True),
        )
        w_qkv_back = weights_back[:, 0:3, :].reshape(model_width, 3 * local_cols)
        w_out_back = weights_back[:, 3, :]
        w_up_back = weights_back[:, 4 : 4 + ffn_count, :].reshape(
            model_width, ffn_count * local_cols
        )
        w_down_back = weights_back[:, 4 + ffn_count :, :].reshape(
            model_width, ffn_count * local_cols
        )
        grad_out = grads_bal.astype(f32) * keep_rows[:, None]
        grad_low = grad_out.astype(low_type)
        down_bias_grad = share_sum(grad_out)
        down_grad = jnp.einsum("qm,qf->mf", grad_low, active_low, preferred_element_type=f32)
        grad_active = jnp.dot(grad_low, w_down_back, preferred_element_type=f32)
        grad_up = gelu_pull(grad_active)[0].astype(low_type)
        up_bias_grad = jnp.sum(grad_up.astype(f32), axis=0)
        up_grad = jnp.einsum("qm,qf->mf", normed_two, grad_up, preferred_element_type=f32)
        grad_normed_two = model_rows(grad_up, w_up_back)
        hidden_part, gain_two_rows = norm_back(
            hidden_own, norms_back[3].astype(f32), grad_normed_two
        )
        gain_two_grad = share_sum(gain_two_rows)
        shift_two_grad = share_sum(grad_normed_two)
        grad_hidden_own = grad_out + hidden_part
        out_bias_grad = share_sum(grad_hidden_own)
        grad_hidden_low = grad_hidden_own.astype(low_type)
        out_grad = jnp.einsum("qm,ql->ml", grad_hidden_low, attended, preferred_element_type=f32)
        grad_attended = jnp.dot(grad_hidden_low, w_out_back, preferred_element_type=f32).astype(
            low_type
        )
        grad_attended = grad_attended.reshape(rows_here, local_heads, HEAD_DIM)
        grad_attention = jnp.einsum(
            "qhd,khd->hqk", grad_attended, value_heads, preferred_element_type=f32
        )
        row_total = jnp.sum(grad_attention * attention, axis=-1, keepdims=True)
        grad_scores = (attention * (grad_attention - row_total)).astype(low_type)
        grad_values = jnp.einsum(
            "hqk,qhd->khd", attention_low, grad_attended, preferred_element_type=f32
        ).astype(low_type)
        grad_queries = (
            jnp.einsum("hqk,khd->qhd", grad_scores, key_heads, preferred_element_type=f32)
            * score_scale
        ).astype(low_type)
        grad_keys = (
            jnp.einsum("hqk,qhd->khd", grad_scores, query_heads, preferred_element_type=f32)
            * score_scale
        ).astype(low_type)
        grad_queries = grad_queries.reshape(rows_here, local_cols)
        grad_values = grad_values.reshape(rows_here, local_cols)
        grad_qkv = jnp.concatenate(
            [grad_queries, grad_keys.reshape(rows_here, local_cols), grad_values], axis=1
        )
        qkv_grad = jnp.einsum("qm,ql->ml", normed_low, grad_qkv, preferred_element_type=f32)
        grad_normed_one = model_rows(grad_qkv, w_qkv_back)
        rows_part, gain_one_rows = norm_back(rows_float, norms_back[0].astype(f32), grad_normed_one)
        gain_one_grad = share_sum(gain_one_rows)
        shift_one_grad = share_sum(grad_normed_one)
        grad_input_own = (grad_hidden_own + rows_part).astype(low_type)
        finished = jnp.stack([output_own, grad_input_own], axis=1)
        output_bal = finished[:, 0, :]
        grad_input = finished[:, 1, :]
        weight_grads = weight_grads + jnp.concatenate(
            [
                qkv_grad.reshape(model_width, 3, local_cols),
                out_grad[:, None, :],
                up_grad.reshape(model_width, ffn_count, local_cols),
                down_grad.reshape(model_width, ffn_count, local_cols),
            ],
            axis=1,
        )
        norm_grads_local = norm_grads_local + jnp.stack(
            [
                gain_one_grad,
                shift_one_grad,
                out_bias_grad,
                gain_two_grad,
                shift_two_grad,
                down_bias_grad,
            ]
        )
        head_grads_local = head_grads_local + jnp.concatenate(
            [
                jnp.sum(grad_queries.astype(f32), axis=0)[None],
                jnp.sum(grad_values.astype(f32), axis=0)[None],
                up_bias_grad.reshape(ffn_count, local_cols),
            ],
            axis=0,
        )
        back_rows, back_grads = (
            lax.all_to_all(
                output_bal[arrival_order].reshape(data_count, piece_rows, model_width),
                "dp",
                split_axis=0,
                concat_axis=0,
                tiled=True,
            ),
            lax.all_to_all(
                grad_input[arrival_order].reshape(data_count, piece_rows, model_width),
                "dp",
                split_axis=0,
                concat_axis=0,
                tiled=True,
            ),
        )
        outputs_given.append(
            jnp.zeros((rows_here, model_width), low_type)
            .at[send_order]
            .set(back_rows.reshape(rows_here, model_width))
        )
        inputs_given.append(
            jnp.zeros((rows_here, model_width), low_type)
            .at[send_order]
            .set(back_grads.reshape(rows_here, model_width))
        )
    head_total = lax.psum(head_grads_local, "dp")
    slot_count = left_stats.shape[0]
    all_slots = slot_count * data_count
    slot_match = block_slot_index[None, :] == jnp.arange(all_slots)[:, None]
    filled = jnp.any(slot_match, axis=1)
    block_of = jnp.sum(jnp.where(slot_match, jnp.arange(blocks)[None, :], 0), axis=1)

    def to_slots(per_block):
        return jnp.where(filled[None, :, None], per_block[:, block_of, :], 0.0)

    summed_rows, norm_part = (
        lax.psum_scatter(weight_grads, "dp", scatter_dimension=0, tiled=True),
        lax.psum_scatter(norm_grads_local, "dp", scatter_dimension=1, tiled=True),
    )
    owned_grads, owned_weights = (
        lax.all_to_all(to_slots(summed_rows), "dp", split_axis=1, concat_axis=0, tiled=True),
        lax.all_to_all(to_slots(matrices), "dp", split_axis=1, concat_axis=0, tiled=True),
    )
    highest = lax.Precision.HIGHEST
    whole_grads = lax.all_gather(owned_grads.astype(jnp.bfloat16), "mp", axis=2, tiled=True).astype(
        owned_grads.dtype
    )
    row_total_count = left_stats.shape[1]
    my_rows = lax.dynamic_slice_in_dim(
        whole_grads, model_index * row_total_count, row_total_count, 0
    )
    new_left = stat_decay * left_stats + jnp.einsum(
        "asb,csb->sac", my_rows, whole_grads, precision=highest
    )
    new_right = stat_decay * right_stats + jnp.einsum(
        "dsa,dsb->sab", owned_grads, whole_grads, precision=highest
    )
    halfway = jnp.einsum("dsb,scb->dsc", whole_grads, right_roots, precision=highest)
    direction = jnp.einsum("sad,dsc->asc", left_roots, halfway, precision=highest)
    squares, norm_total = lax.psum((jnp.sum(direction * direction, axis=(0, 2)), norm_part), "mp")
    factor = lax.rsqrt(squares / (whole_grads.shape[0] * whole_grads.shape[2]) + mean_eps)
    updated_blocks = owned_weights - matrix_rate * factor[None, :, None] * direction
    new_norm_state = stat_decay * norm_state + norm_total * norm_total
    new_norm_vectors = norm_vectors - vector_rate * norm_total / (
        jnp.sqrt(new_norm_state) + diag_eps
    )
    new_head_state = stat_decay * head_state + head_total * head_total
    new_head_vectors = head_vectors - vector_rate * head_total / (
        jnp.sqrt(new_head_state) + diag_eps
    )
    return (
        jnp.stack(outputs_given),
        jnp.stack(inputs_given),
        owned_grads,
        new_left,
        new_right,
        updated_blocks,
        norm_total,
        new_norm_state,
        new_norm_vectors,
        head_total,
        new_head_state,
        new_head_vectors,
    )


def solution(mesh):
    placed = (
        P(None, "dp", None),
        P(None, "dp", None),
        P(None, "dp", None),
        P(),
        P(),
        P("dp", None, "mp"),
        P(None, "dp"),
        P(None, "mp"),
        P("dp", "mp", None),
        P("dp", "mp", None),
        P("dp", None, None),
        P("dp", "mp", None),
        P(None, "dp"),
        P(None, "mp"),
    )
    return jax.shard_map(
        on_device,
        mesh=mesh,
        in_specs=placed,
        out_specs=(
            P(None, "dp", None),
            P(None, "dp", None),
            P(None, "dp", "mp"),
            P("dp", "mp", None),
            P("dp", "mp", None),
            P(None, "dp", "mp"),
            P(None, "dp"),
            P(None, "dp"),
            P(None, "dp"),
            P(None, "mp"),
            P(None, "mp"),
            P(None, "mp"),
        ),
        check_vma=False,
    )
```

profile of v0, /device:TPU:0, one launch (start us, length us, event | category | flops | bytes accessed | tf_op | source)
XLA Modules:
  0.0 1637.3 jit_solution(7794623200670585256)
XLA Ops:
  20.6 8.1 gather_fusion.3
  48.7 77.4 %all-to-all-done.2 = bf16[8,128,1024]{2,1,0:T(8,128)(2,1)} async-done(((bf16[8,128,1024]{2,1,0:T(8,128)(2,1)}), bf16[8,128,1024]{2,1,0:T(8,128)(2,1)}, u32[]{:S(2)}, u32[]{:S(2)}) %all-to-all-start.2) | async-done | bytes 2097184 | tf_op jit(solution)/shard_map/all_to_all | solution.py:99
  135.7 7.9 gather_fusion.6
  174.7 38.4 %all_gather.6 = bf16[6,1024]{1,0:T(8,128)(2,1)S(1)} all-gather(bf16[6,128]{1,0:T(8,128)(2,1)S(1)} %convert_element_type.225), channel_id=1, replica_groups=mesh['dp'=8,'mp'=4] {'dp'}, dimensions={1}, use_global_device_ids=true | all-gather | bytes 13824 | tf_op jit(solution)/shard_map/all_gather | solution.py:91
  254.3 11.5 fusion.143
  277.4 11.0 fusion.144
  314.4 7.9 gather_fusion.7
  322.3 35.6 %all-to-all-done.6 = bf16[8,128,1024]{2,1,0:T(8,128)(2,1)} async-done(((bf16[8,128,1024]{2,1,0:T(8,128)(2,1)}), bf16[8,128,1024]{2,1,0:T(8,128)(2,1)}, u32[]{:S(2)}, u32[]{:S(2)}) %all-to-all-start.6) | async-done | bytes 2097184 | tf_op jit(solution)/shard_map/all_to_all | solution.py:100
  357.9 8.0 gather_fusion.10
  370.6 84.6 %all-reduce.12.cloned.1.call-done = (f32[1024,1024]{1,0:T(8,128)}, f32[1024,1024]{1,0:T(8,128)}) async-done(((f32[1024,1024]{1,0:T(8,128)}, f32[1024,1024]{1,0:T(8,128)}), (f32[1024,1024]{1,0:T(8,128)}, f32[1024,1024]{1,0:T(8,128)})) %all-reduce.12.cloned.1.call-update) | async-done | bytes 8388624 | tf_op jit(solution)/shard_map/psum | solution.py:41
  509.9 140.8 %all-reduce.10.cloned.1.call-done = (f32[1024,1024]{1,0:T(8,128)}, f32[1024,1024]{1,0:T(8,128)}) async-done(((f32[1024,1024]{1,0:T(8,128)}, f32[1024,1024]{1,0:T(8,128)}), (f32[1024,1024]{1,0:T(8,128)}, f32[1024,1024]{1,0:T(8,128)})) %all-reduce.10.cloned.1.call-update) | async-done | bytes 8388624 | tf_op jit(solution)/shard_map/psum | solution.py:41
  650.8 8.0 multiply_reduce_fusion.11
  668.2 10.1 convert_reduce_fusion.6
  678.4 8.7 multiply_reduce_fusion.1
  687.1 7.9 multiply_convert_fusion.1
  709.9 10.1 convert_reduce_fusion.4
  720.0 8.7 multiply_reduce_fusion
  728.8 7.9 multiply_convert_fusion
  788.4 7.9 fusion.83
  826.1 10.4 maximum_add_fusion
  837.2 202.1 %all-reduce.8.cloned.1.call-done = (f32[1024,1024]{1,0:T(8,128)}, f32[1024,1024]{1,0:T(8,128)}, f32[1024,1024]{1,0:T(8,128)}, f32[1024,1024]{1,0:T(8,128)}) async-done(((f32[1024,1024]{1,0:T(8,128)}, f32[1024,1024]{1,0:T(8,128)}, f32[1024,1024]{1,0:T(8,128)}, f32[1024,1024]{1,0:T(8,128)}), (f32[1024,1024]{1,0:T(8,128)}, f32[1024,1024]{1,0:T(8,128)}, f32[1024,1024]{1,0:T(8,128)}, ...) | async-done | bytes 16777232 | tf_op jit(solution)/shard_map/psum | solution.py:41
  1039.4 16.8 %multiply_reduce_fusion.10 = (f32[1024]{0:T(1024)S(1)}, f32[1024]{0:T(1024)S(1)}, f32[1024]{0:T(1024)S(1)}, f32[1024]{0:T(1024)S(1)}, f32[1024,1024]{1,0:T(8,128...) fusion(f32[1024,1024]{1,0:T(8,128)} %get-tuple-element.93, ...), kind=kLoop, calls=%fused_computation.110 | loop fusion | flops 25161728 | bytes 41988096 | tf_op jit(solution)/shard_map/reduce_sum | solution.py:34
  1056.3 8.6 add_convert_fusion.1
  1064.8 7.9 gather_fusion.8
  1086.2 93.8 %all-to-all-done.5 = bf16[8,128,1024]{2,1,0:T(8,128)(2,1)} async-done(((bf16[8,128,1024]{2,1,0:T(8,128)(2,1)}), bf16[8,128,1024]{2,1,0:T(8,128)(2,1)}, u32[]{:S(2)}, u32[]{:S(2)}) %all-to-all-start.5) | async-done | bytes 2097184 | tf_op jit(solution)/shard_map/all_to_all | solution.py:248
  1184.6 7.9 gather_fusion.11
  1192.5 52.2 %all-to-all-done.1 = bf16[8,128,1024]{2,1,0:T(8,128)(2,1)} async-done(((bf16[8,128,1024]{2,1,0:T(8,128)(2,1)}), bf16[8,128,1024]{2,1,0:T(8,128)(2,1)}, u32[]{:S(2)}, u32[]{:S(2)}) %all-to-all-start.1) | async-done | bytes 2097184 | tf_op jit(solution)/shard_map/all_to_all | solution.py:241
  1252.7 100.4 %reduce-scatter.3.cloned.1.call-done = f32[128,12,256]{2,0,1:T(8,128)} async-done(((f32[1024,12,256]{2,0,1:T(8,128)}), f32[128,12,256]{2,0,1:T(8,128)}) %reduce-scatter.3.cloned.1.call-update) | async-done | bytes 1572880 | tf_op jit(solution)/shard_map/reduce_scatter | solution.py:277
  1373.6 40.7 %all-to-all-done.8 = f32[128,16,256]{2,0,1:T(8,128)} async-done(((f32[128,16,256]{2,0,1:T(8,128)}), f32[128,16,256]{2,0,1:T(8,128)}, u32[]{:S(2)}, u32[]{:S(2)}) %all-to-all-start.8) | async-done | bytes 2097184 | tf_op jit(solution)/shard_map/all_to_all | solution.py:281
  1422.9 43.5 %all-to-all-done.3 = bf16[8,128,1024]{2,1,0:T(8,128)(2,1)} async-done(((bf16[8,128,1024]{2,1,0:T(8,128)(2,1)}), bf16[8,128,1024]{2,1,0:T(8,128)(2,1)}, u32[]{:S(2)}, u32[]{:S(2)}) %all-to-all-start.3) | async-done | bytes 2097184 | tf_op jit(solution)/shard_map/all_to_all | solution.py:241
  1471.2 48.9 %psum.87 = f32[6,256]{1,0:T(8,128)S(1)} all-reduce(f32[6,256]{1,0:T(8,128)S(1)} %maximum_add_fusion.1), channel_id=1, replica_groups=mesh['dp'=8,'mp'=4] {'dp'}, use_global_device_ids=true, to_apply=%region_71.72 | all-reduce | flops 1536 | bytes 12288 | tf_op jit(solution)/shard_map/psum | solution.py:266
  1586.9 17.5 %multiply_reduce_fusion.12 = (f32[2]{0:T(128)S(1)}, f32[2,256,1024]{2,1,0:T(8,128)}) fusion(f32[2,1024,1024]{2,1,0:T(8,128)} %param.24, f32[2,1024,256]{2,1,0:T(8,128)S(1)} %fusion.147), kind=kOutput, calls=%fused_computation.117 | convolution fusion | flops 6443499520 | bytes 12582920 | tf_op jit(solution)/shard_map/sad,dsc->asc/dot_general | solution.py:299
  (423 shorter events, 470.1 us)
Async XLA Ops:
  7.2 1574.3 %copy-start = (f32[2,256,1024]{2,1,0:T(8,128)S(1)}, f32[2,256,1024]{2,1,0:T(8,128)}, u32[]{:S(2)}) copy-start(f32[2,256,1024]{2,1,0:T(8,128)} %param.25) | copy-start | bytes 6291460
  7.2 236.2 %all-gather.3.cloned.1.call-start = ((), (), s32[]{:S(2)}) async-start(), calls=%async_computation.12 | async-start | bytes 7077888 | tf_op jit(solution)/shard_map/all_gather | solution.py:90
  28.7 97.4 %all-to-all-start.2 = ((bf16[8,128,1024]{2,1,0:T(8,128)(2,1)}), bf16[8,128,1024]{2,1,0:T(8,128)(2,1)}, u32[]{:S(2)}, u32[]{:S(2)}) async-start(bf16[8,128,1024]{2,1,0:T(8,128)(2,1)} %bitcast.207), calls=%async_computation.2 | async-start | bytes 4194304 | tf_op jit(solution)/shard_map/all_to_all | solution.py:99
  48.7 82.0 %copy-start.99 = (s32[2,1,4]{2,1,0:T(1,128)S(1)}, s32[2,1,4]{2,1,0:T(1,128)}, u32[]{:S(2)}) copy-start(s32[2,1,4]{2,1,0:T(1,128)} %param.16) | copy-start | bytes 100
  48.7 82.4 %copy-start.76 = (f32[6,128]{1,0:T(8,128)S(1)}, f32[6,128]{1,0:T(8,128)}, u32[]{:S(2)}) copy-start(f32[6,128]{1,0:T(8,128)} %param.20) | copy-start | bytes 9220
  126.1 98.9 %all-to-all-start = ((bf16[8,128,1024]{2,1,0:T(8,128)(2,1)}), bf16[8,128,1024]{2,1,0:T(8,128)(2,1)}, u32[]{:S(2)}, u32[]{:S(2)}) async-start(bf16[8,128,1024]{2,1,0:T(8,128)(2,1)} %bitcast.203), calls=%async_computation | async-start | bytes 4194304 | tf_op jit(solution)/shard_map/all_to_all | solution.py:99
  135.7 77.6 %copy-start.68 = (f32[6,256]{1,0:T(8,128)S(1)}, f32[6,256]{1,0:T(8,128)}, u32[]{:S(2)}) copy-start(f32[6,256]{1,0:T(8,128)} %param.21) | copy-start | bytes 18436
  214.0 251.8 %copy-start.55 = (f32[1,1024]{1,0:T(1,128)}, f32[1,1024]{1,0:T(1,128)S(1)}, u32[]{:S(2)}) copy-start(f32[1,1024]{1,0:T(1,128)S(1)} %get-tuple-element.125) | copy-start | bytes 12292
  214.0 255.9 %copy-start.90 = (f32[1,1024]{1,0:T(1,128)}, f32[1,1024]{1,0:T(1,128)S(1)}, u32[]{:S(2)}) copy-start(f32[1,1024]{1,0:T(1,128)S(1)} %get-tuple-element.123) | copy-start | bytes 12292
  225.0 83.4 %all-to-all-start.4 = ((bf16[8,128,1024]{2,1,0:T(8,128)(2,1)}), bf16[8,128,1024]{2,1,0:T(8,128)(2,1)}, u32[]{:S(2)}, u32[]{:S(2)}) async-start(bf16[8,128,1024]{2,1,0:T(8,128)(2,1)} %bitcast.202), calls=%async_computation.4 | async-start | bytes 4194304 | tf_op jit(solution)/shard_map/all_to_all | solution.py:100
  229.9 225.3 %all-reduce.12.cloned.1.call-start = ((), (), s32[]{:S(2)}) async-start(), calls=%async_computation.18 | async-start | bytes 16777216 | tf_op jit(solution)/shard_map/psum | solution.py:41
  308.4 49.5 %all-to-all-start.6 = ((bf16[8,128,1024]{2,1,0:T(8,128)(2,1)}), bf16[8,128,1024]{2,1,0:T(8,128)(2,1)}, u32[]{:S(2)}, u32[]{:S(2)}) async-start(bf16[8,128,1024]{2,1,0:T(8,128)(2,1)} %bitcast.206), calls=%async_computation.6 | async-start | bytes 4194304 | tf_op jit(solution)/shard_map/all_to_all | solution.py:100
  314.3 336.5 %all-reduce.10.cloned.1.call-start = ((), (), s32[]{:S(2)}) async-start(), calls=%async_computation.17 | async-start | bytes 16777216 | tf_op jit(solution)/shard_map/psum | solution.py:41
  314.4 190.8 %copy-start.95 = (f32[1,2,4,128]{3,1,2,0:T(2,128)}, f32[1,2,4,128]{3,1,2,0:T(2,128)S(1)}, u32[]{:S(2)}) copy-start(f32[1,2,4,128]{3,1,2,0:T(2,128)S(1)} %copy.92) | copy-start | bytes 12292
  314.4 344.4 %copy-start.72 = (f32[1024]{0:T(1024)}, f32[1024]{0:T(1024)S(1)}, u32[]{:S(2)}) copy-start(f32[1024]{0:T(1024)S(1)} %compare_convert_fusion.1) | copy-start | bytes 12292
  314.4 158.8 %copy-start.74 = (f32[1024]{0:T(1024)}, f32[1024]{0:T(1024)S(1)}, u32[]{:S(2)}) copy-start(f32[1024]{0:T(1024)S(1)} %compare_convert_fusion) | copy-start | bytes 12292
  497.3 542.1 %all-reduce.8.cloned.1.call-start = ((), (), s32[]{:S(2)}) async-start(), calls=%async_computation.16 | async-start | bytes 33554432 | tf_op jit(solution)/shard_map/psum | solution.py:41
  749.2 603.8 %reduce-scatter.3.cloned.1.call-start = ((), (), s32[]{:S(2)}) async-start(), calls=%async_computation.13 | async-start | bytes 14155776 | tf_op jit(solution)/shard_map/reduce_scatter | solution.py:277
  836.5 202.8 %copy-start.56 = (f32[1,1024]{1,0:T(1,128)S(1)}, f32[1,1024]{1,0:T(1,128)}, u32[]{:S(2)}) copy-start(f32[1,1024]{1,0:T(1,128)} %copy-done.55) | copy-start | bytes 12292
  836.5 202.8 %copy-start.84 = (f32[1,1024]{1,0:T(1,128)S(1)}, f32[1,1024]{1,0:T(1,128)}, u32[]{:S(2)}) copy-start(f32[1,1024]{1,0:T(1,128)} %get-tuple-element.122) | copy-start | bytes 12292
  1072.7 107.2 %all-to-all-start.5 = ((bf16[8,128,1024]{2,1,0:T(8,128)(2,1)}), bf16[8,128,1024]{2,1,0:T(8,128)(2,1)}, u32[]{:S(2)}, u32[]{:S(2)}) async-start(bf16[8,128,1024]{2,1,0:T(8,128)(2,1)} %bitcast.209), calls=%async_computation.5 | async-start | bytes 4194304 | tf_op jit(solution)/shard_map/all_to_all | solution.py:248
  1086.2 98.3 %copy-start.79 = (s32[1024]{0:T(1024)S(1)}, s32[1024]{0:T(1024)}, u32[]{:S(2)}) copy-start(s32[1024]{0:T(1024)} %copy-done.78) | copy-start | bytes 12292
  1180.0 64.6 %all-to-all-start.1 = ((bf16[8,128,1024]{2,1,0:T(8,128)(2,1)}), bf16[8,128,1024]{2,1,0:T(8,128)(2,1)}, u32[]{:S(2)}, u32[]{:S(2)}) async-start(bf16[8,128,1024]{2,1,0:T(8,128)(2,1)} %bitcast.208), calls=%async_computation.1 | async-start | bytes 4194304 | tf_op jit(solution)/shard_map/all_to_all | solution.py:241
  1192.5 56.5 %copy-start.100 = (s32[12]{0:T(128)S(1)}, s32[12]{0:T(128)}, u32[]{:S(2)}) copy-start(s32[12]{0:T(128)} %param.18) | copy-start | bytes 148
  1244.6 116.7 %all-to-all-start.7 = ((bf16[8,128,1024]{2,1,0:T(8,128)(2,1)}), bf16[8,128,1024]{2,1,0:T(8,128)(2,1)}, u32[]{:S(2)}, u32[]{:S(2)}) async-start(bf16[8,128,1024]{2,1,0:T(8,128)(2,1)} %bitcast.204), calls=%async_computation.7 | async-start | bytes 4194304 | tf_op jit(solution)/shard_map/all_to_all | solution.py:248
  1361.3 52.9 %all-to-all-start.8 = ((f32[128,16,256]{2,0,1:T(8,128)}), f32[128,16,256]{2,0,1:T(8,128)}, u32[]{:S(2)}, u32[]{:S(2)}) async-start(f32[128,16,256]{2,0,1:T(8,128)} %get-tuple-element.143), calls=%async_computation.9 | async-start | bytes 4194304 | tf_op jit(solution)/shard_map/all_to_all | solution.py:281
  1414.3 52.2 %all-to-all-start.3 = ((bf16[8,128,1024]{2,1,0:T(8,128)(2,1)}), bf16[8,128,1024]{2,1,0:T(8,128)(2,1)}, u32[]{:S(2)}, u32[]{:S(2)}) async-start(bf16[8,128,1024]{2,1,0:T(8,128)(2,1)} %bitcast.205), calls=%async_computation.3 | async-start | bytes 4194304 | tf_op jit(solution)/shard_map/all_to_all | solution.py:241
  1418.6 162.9 %all-gather.5.cloned.1.call-start = ((), (), s32[]{:S(2)}) async-start(), calls=%async_computation.14 | async-start | bytes 5242880 | tf_op jit(solution)/shard_map/all_gather | solution.py:285
  1421.8 49.2 %copy-start.97 = (f32[4,64]{1,0:T(4,128)S(1)}, f32[4,64]{1,0:T(4,128)}, u32[]{:S(2)}) copy-start(f32[4,64]{1,0:T(4,128)} %get-tuple-element.156) | copy-start | bytes 3076
  1421.8 49.3 %copy-start.85 = (f32[4,64]{1,0:T(4,128)S(1)}, f32[4,64]{1,0:T(4,128)}, u32[]{:S(2)}) copy-start(f32[4,64]{1,0:T(4,128)} %get-tuple-element.158) | copy-start | bytes 3076
  1466.4 104.9 %all-to-all-start.9 = ((f32[128,16,256]{2,0,1:T(8,128)}), f32[128,16,256]{2,0,1:T(8,128)}, u32[]{:S(2)}, u32[]{:S(2)}) async-start(f32[128,16,256]{2,0,1:T(8,128)} %get-tuple-element.142), calls=%async_computation.10 | async-start | bytes 4194304 | tf_op jit(solution)/shard_map/all_to_all | solution.py:282
  1470.8 133.7 %reduce-scatter.5.cloned.1.call-start = ((), (), s32[]{:S(2)}) async-start(), calls=%async_computation.15 | async-start | bytes 36864 | tf_op jit(solution)/shard_map/reduce_scatter | solution.py:278
  (101 other events, 858.8 us)
Sparse Core Ops, SparseCore 0:
  10.6 154.1 all-gather.2
  300.7 154.4 all-reduce.11
  497.4 153.3 all-reduce.9
  749.3 289.9 all-reduce.7
  1042.8 310.1 reduce-scatter.2
  1423.0 36.2 all-gather.4
  1533.8 59.4 reduce-scatter.4
where the time goes:
time: 1650 us; the launch traced here: 1640 us
  waiting for transfers between devices  871 us (53%)
  matrix products  231 us (14%)
  local copies, waits for them, and re-layouts  216 us (13%)
  other arithmetic  160 us (10%)
  blocking collectives  93.3 us (6%)
  starting transfers between devices  50.7 us (3%)
    psum x3, waiting for transfers between devices, model_rows(): lax.psum(jnp.einsum('qk,mk->qm', left, right, preferred_element_type=jnp....  428 us
    reduce_scatter x1, waiting for transfers between devices, on_device(): lax.psum_scatter(weight_grads, 'dp', scatter_dimension=0, tiled=True)  100 us
    all_to_all x2, waiting for transfers between devices, on_device(): lax.all_to_all(output_bal[arrival_order].reshape(data_count, piece_rows,...  95.7 us
    all_to_all x2, waiting for transfers between devices, on_device(): lax.all_to_all(grad_input[arrival_order].reshape(data_count, piece_rows,...  93.8 us
    all_to_all x2, waiting for transfers between devices, on_device(): lax.all_to_all(sent_rows, 'dp', split_axis=0, concat_axis=0, tiled=True)  77.4 us
    psum x1, blocking collectives, on_device(): head_total = lax.psum(head_grads_local, 'dp')  48.9 us
    all_to_all x1, waiting for transfers between devices, on_device(): lax.all_to_all(to_slots(summed_rows), 'dp', split_axis=1, concat_axis=0,...  40.7 us
    all_gather x1, blocking collectives, on_device(): lax.all_gather(shipped[1], 'dp', axis=1, tiled=True)  38.4 us
  transfers between devices with their start and end apart: 17, of which 10 were waited for; matrix products, arithmetic and copies ran while one was open for 27% of the time, Pallas kernels for 0%

commit v1 on v0

v1 whole, which is shorter than its diff:
```python
import math

import jax
import jax.numpy as jnp
from jax import lax
from jax.sharding import PartitionSpec as P

HEAD_DIM = 64


stat_decay = 0.5
matrix_rate = 0.02
vector_rate = 0.3
norm_eps = 1e-05
mean_eps = 1e-06
diag_eps = 1e-08
masked_score = -1000000000.0

f32 = jnp.float32
low_type = jnp.bfloat16


def unit_rows_of(values):
    center = values - jnp.mean(values, axis=-1, keepdims=True)
    spread = jnp.mean(center * center, axis=-1, keepdims=True)
    scale_rows = lax.rsqrt(spread + norm_eps)
    return center * scale_rows, scale_rows


def layer_norm(values, gain, shift):
    unit_rows, _ = unit_rows_of(values)
    return unit_rows * gain + shift


def norm_back(values, gain, grad_normed):
    unit_rows, scale_rows = unit_rows_of(values)
    grad_unit = grad_normed * gain
    grad_values = scale_rows * (
        grad_unit
        - jnp.mean(grad_unit, axis=-1, keepdims=True)
        - unit_rows * jnp.mean(grad_unit * unit_rows, axis=-1, keepdims=True)
    )
    return (grad_values, grad_normed * unit_rows)


def dot(left, right):
    return lax.dot_general(left, right, (((1,), (0,)), ((), ())), preferred_element_type=f32)


def dot_nt(left, right):
    return lax.dot_general(left, right, (((1,), (1,)), ((), ())), preferred_element_type=f32)


def dot_tn(left, right):
    return lax.dot_general(left, right, (((0,), (0,)), ((), ())), preferred_element_type=f32)


def swap(values, axis, bit):
    count = lax.axis_size(axis)
    return lax.ppermute(values, axis, [(i, i ^ bit) for i in range(count)])


def gather_parts(share, axis):
    parts = {0: share}
    bit = lax.axis_size(axis) // 2
    while bit >= 1:
        parts.update({j | bit: swap(part, axis, bit) for j, part in list(parts.items())})
        bit //= 2
    return [parts[j] for j in range(len(parts))]


def gather_rows(share):
    return jnp.concatenate(gather_parts(share, "mp"), axis=0)


def scatter_rows(values):
    count = lax.axis_size("mp")
    own = values.shape[0] // count
    parts = {j: values[j * own : (j + 1) * own] for j in range(count)}
    bit = 1
    while bit < count:
        parts = {
            j: part + swap(parts[j ^ bit].astype(low_type), "mp", bit).astype(f32)
            for j, part in parts.items()
            if not j & bit
        }
        bit *= 2
    return parts[0]


def sum_over(values, axis):
    bit = 1
    while bit < lax.axis_size(axis):
        values = values + swap(values, axis, bit)
        bit *= 2
    return values


def gather_columns(share, axis):
    index = lax.axis_index(axis)
    bit = 1
    while bit < lax.axis_size(axis):
        other = swap(share, axis, bit)
        share = jnp.where(
            (index & bit) != 0,
            jnp.concatenate([other, share], axis=-1),
            jnp.concatenate([share, other], axis=-1),
        )
        bit *= 2
    return share


def exchange(rows):
    return lax.all_to_all(rows, "dp", split_axis=0, concat_axis=0, tiled=True)


def on_device(
    tokens,
    cotangent,
    lengths,
    placement_ids,
    block_slot_index,
    matrices,
    norm_vectors,
    head_vectors,
    left_stats,
    right_stats,
    left_roots,
    right_roots,
    norm_state,
    head_state,
):
    data_count = lax.axis_size("dp")
    data_index = lax.axis_index("dp")
    model_count = lax.axis_size("mp")
    model_index = lax.axis_index("mp")
    micro_count, rows_here, model_width = tokens.shape
    piece_rows = rows_here // data_count
    sub_rows = piece_rows // model_count
    own_rows = rows_here // model_count
    blocks = matrices.shape[1]
    local_cols = matrices.shape[2]
    shard_rows = matrices.shape[0]
    ffn_count = (blocks - 4) // 2
    ffn_cols = ffn_count * local_cols
    local_heads = local_cols // HEAD_DIM
    score_scale = 1.0 / math.sqrt(HEAD_DIM)

    matrices_low = matrices.astype(low_type)
    shipped_one = matrices_low[:, :4, :].reshape(shard_rows, 4 * local_cols)
    shipped_two = matrices_low[:, 4:, :].reshape(shard_rows, 2 * ffn_cols)
    norm_parts = jnp.stack(gather_parts(norm_vectors.astype(low_type), "dp"))
    norms = norm_parts[data_index ^ jnp.arange(data_count)]
    norms = jnp.swapaxes(norms, 0, 1).reshape(6, model_width).astype(f32)
    weights_one = lax.all_gather(shipped_one, "dp", axis=0, tiled=True)
    weights_two = lax.all_gather(shipped_two, "dp", axis=0, tiled=True)
    w_qkv = weights_one[:, : 3 * local_cols]
    w_out = weights_one[:, 3 * local_cols :]
    w_up = weights_two[:, :ffn_cols]
    w_down = weights_two[:, ffn_cols:]

    order = jnp.arange(rows_here)
    earlier = (order[:, None] < order[None, :]).astype(low_type)
    device_ids = jnp.arange(data_count)[:, None]
    slots_mine = []
    positions = []
    for micro in range(micro_count):
        dest_all = placement_ids[micro].reshape(data_count, rows_here)
        dest_mine = lax.dynamic_slice_in_dim(dest_all, data_index, 1, 0)
        target = dest_mine // rows_here
        to_each = target == device_ids
        to_me = (dest_all // rows_here) == data_index
        rank_both = dot(jnp.concatenate([to_each, to_me]).astype(low_type), earlier).astype(
            jnp.int32
        )
        rank_out = jnp.sum(jnp.where(to_each, rank_both[:data_count], 0), axis=0)
        slots_mine.append((rank_out, target[0]))
        rank_in = jnp.where(to_me, rank_both[data_count:], -1)
        place = jnp.sum(
            jnp.where(
                rank_in[:, None, :] == jnp.arange(piece_rows)[None, :, None],
                (dest_all - data_index * rows_here)[:, None, :],
                0,
            ),
            axis=2,
        )
        place = place.reshape(data_count, model_count, sub_rows).transpose(1, 0, 2)
        place = place.reshape(model_count, own_rows)[model_index ^ jnp.arange(model_count)]
        positions.append(place.reshape(rows_here))

    def send_rows(given, micro):
        rank, target = slots_mine[micro]
        wanted = jnp.arange(own_rows)
        here = (rank // sub_rows) == model_index
        slot = jnp.where(here, target * sub_rows + rank % sub_rows, -1)
        pick = (slot[None, :] == wanted[:, None]).astype(low_type)
        picked = dot(pick, given).astype(low_type)
        return exchange(picked.reshape(data_count, sub_rows, model_width)).reshape(
            own_rows, model_width
        )

    def return_rows(own, micro):
        rank, target = slots_mine[micro]
        slot = ((rank // sub_rows) ^ model_index) * own_rows + target * sub_rows + rank % sub_rows
        back = exchange(own.reshape(data_count, sub_rows, model_width))
        back = gather_rows(back.reshape(own_rows, model_width))
        pick = (slot[:, None] == order[None, :]).astype(low_type)
        return dot(pick, back).astype(low_type)

    micros = range(micro_count)
    rows_own = [send_rows(tokens[i], i).astype(f32) for i in micros]
    segments = []
    for i in micros:
        bounds = jnp.cumsum(lengths[i, 0])
        segments.append(
            jnp.sum((positions[i][:, None] >= bounds[None, :]).astype(jnp.int32), axis=1)
        )
    normed_one = [
        gather_rows(layer_norm(rows_own[i], norms[0], norms[1]).astype(low_type)) for i in micros
    ]
    keep = [
        (segments[i][:own_rows] < lengths.shape[2] - 1).astype(f32)[:, None] for i in micros
    ]
    grad_out_own = [send_rows(cotangent[i], i).astype(f32) * keep[i] for i in micros]
    grad_low = [gather_rows(grad_out_own[i].astype(low_type)) for i in micros]

    saved = []
    hidden_own = []
    for i in micros:
        qkv = dot(normed_one[i], w_qkv)
        queries = (qkv[:, :local_cols] + head_vectors[0]).astype(low_type)
        keys_all = qkv[:, local_cols : 2 * local_cols].astype(low_type)
        values = (qkv[:, 2 * local_cols :] + head_vectors[1]).astype(low_type)
        query_heads = queries.reshape(rows_here, local_heads, HEAD_DIM)
        key_heads = keys_all.reshape(rows_here, local_heads, HEAD_DIM)
        value_heads = values.reshape(rows_here, local_heads, HEAD_DIM)
        place, segment = positions[i], segments[i]
        allowed = (place[:, None] >= place[None, :]) & (segment[:, None] == segment[None, :])
        scores = (
            jnp.einsum("qhd,khd->hqk", query_heads, key_heads, preferred_element_type=f32)
            * score_scale
        )
        scores = jnp.where(allowed[None], scores, masked_score)
        attention = jax.nn.softmax(scores, axis=-1)
        attention_low = attention.astype(low_type)
        attended = jnp.einsum(
            "hqk,khd->qhd", attention_low, value_heads, preferred_element_type=f32
        )
        attended = attended.reshape(rows_here, local_cols).astype(low_type)
        branch = scatter_rows(dot_nt(attended, w_out))
        hidden_own.append(rows_own[i] + branch + norms[2])
        saved.append((query_heads, key_heads, value_heads, attention, attention_low, attended))

    normed_two = []
    active = []
    grad_up = []
    outputs_given = []
    grad_normed_two = []
    for i in micros:
        normed_two.append(
            gather_rows(layer_norm(hidden_own[i], norms[3], norms[4]).astype(low_type))
        )
        up_in = dot(normed_two[i], w_up) + head_vectors[2:].reshape(-1)
        active_full, gelu_pull = jax.vjp(lambda v: jax.nn.gelu(v, approximate=True), up_in)
        active.append(active_full.astype(low_type))
        grad_up.append(gelu_pull(dot(grad_low[i], w_down))[0].astype(low_type))
        grad_normed_two.append(scatter_rows(dot_nt(grad_up[i], w_up)))
        feed = scatter_rows(dot_nt(active[i], w_down))
        output_own = (hidden_own[i] + feed + norms[5]).astype(low_type)
        outputs_given.append(return_rows(output_own, i))

    up_grad = dot_tn(normed_two[0], grad_up[0])
    down_grad = dot_tn(grad_low[0], active[0])
    for i in micros[1:]:
        up_grad = up_grad + dot_tn(normed_two[i], grad_up[i])
        down_grad = down_grad + dot_tn(grad_low[i], active[i])
    summed_two = lax.psum_scatter(
        jnp.concatenate([up_grad, down_grad], axis=1).astype(low_type),
        "dp",
        scatter_dimension=0,
        tiled=True,
    )

    inputs_given = []
    grad_qkv = []
    grad_hidden_low = []
    norm_grads_own = 0.0
    for i in micros:
        query_heads, key_heads, value_heads, attention, attention_low, attended = saved[i]
        hidden_part, gain_two_rows = norm_back(hidden_own[i], norms[3], grad_normed_two[i])
        grad_hidden = grad_out_own[i] + hidden_part
        grad_hidden_low.append(gather_rows(grad_hidden.astype(low_type)))
        grad_attended = dot(grad_hidden_low[i], w_out).astype(low_type)
        grad_attended = grad_attended.reshape(rows_here, local_heads, HEAD_DIM)
        grad_attention = jnp.einsum(
            "qhd,khd->hqk", grad_attended, value_heads, preferred_element_type=f32
        )
        row_total = jnp.sum(grad_attention * attention, axis=-1, keepdims=True)
        grad_scores = (attention * (grad_attention - row_total)).astype(low_type)
        grad_values = jnp.einsum(
            "hqk,qhd->khd", attention_low, grad_attended, preferred_element_type=f32
        ).astype(low_type)
        grad_queries = (
            jnp.einsum("hqk,khd->qhd", grad_scores, key_heads, preferred_element_type=f32)
            * score_scale
        ).astype(low_type)
        grad_keys = (
            jnp.einsum("hqk,qhd->khd", grad_scores, query_heads, preferred_element_type=f32)
            * score_scale
        ).astype(low_type)
        grad_qkv.append(
            jnp.concatenate(
                [
                    grad_queries.reshape(rows_here, local_cols),
                    grad_keys.reshape(rows_here, local_cols),
                    grad_values.reshape(rows_here, local_cols),
                ],
                axis=1,
            )
        )
        grad_normed_one = scatter_rows(dot_nt(grad_qkv[i], w_qkv))
        rows_part, gain_one_rows = norm_back(rows_own[i], norms[0], grad_normed_one)
        grad_input = (grad_hidden + rows_part).astype(low_type)
        norm_grads_own = norm_grads_own + jnp.stack(
            [
                jnp.sum(gain_one_rows, axis=0),
                jnp.sum(grad_normed_one, axis=0),
                jnp.sum(grad_hidden, axis=0),
                jnp.sum(gain_two_rows, axis=0),
                jnp.sum(grad_normed_two[i], axis=0),
                jnp.sum(grad_out_own[i], axis=0),
            ]
        )
        inputs_given.append(return_rows(grad_input, i))

    qkv_grad = dot_tn(normed_one[0], grad_qkv[0])
    out_grad = dot_tn(grad_hidden_low[0], saved[0][5])
    for i in micros[1:]:
        qkv_grad = qkv_grad + dot_tn(normed_one[i], grad_qkv[i])
        out_grad = out_grad + dot_tn(grad_hidden_low[i], saved[i][5])
    summed_one = lax.psum_scatter(
        jnp.concatenate([qkv_grad, out_grad], axis=1).astype(low_type),
        "dp",
        scatter_dimension=0,
        tiled=True,
    )

    head_own = 0.0
    for i in micros:
        head_own = head_own + jnp.concatenate(
            [
                jnp.sum(grad_qkv[i][:, :local_cols].astype(f32), axis=0)[None],
                jnp.sum(grad_qkv[i][:, 2 * local_cols :].astype(f32), axis=0)[None],
                jnp.sum(grad_up[i].astype(f32), axis=0).reshape(ffn_count, local_cols),
            ],
            axis=0,
        )
    head_total = sum_over(head_own, "dp")
    norm_all = sum_over(sum_over(norm_grads_own, "mp"), "dp")
    norm_cols = norm_vectors.shape[1]
    norm_total = lax.dynamic_slice_in_dim(norm_all, data_index * norm_cols, norm_cols, 1)

    slot_count = left_stats.shape[0]
    all_slots = slot_count * data_count
    slot_match = block_slot_index[None, :] == jnp.arange(all_slots)[:, None]
    filled = jnp.any(slot_match, axis=1)
    block_of = jnp.sum(jnp.where(slot_match, jnp.arange(blocks)[None, :], 0), axis=1)
    summed = jnp.concatenate([summed_one, summed_two], axis=1)
    summed = jnp.swapaxes(summed.reshape(shard_rows, blocks, local_cols), 0, 1)
    slotted = jnp.where(filled[:, None, None], summed[block_of], 0.0).astype(low_type)
    owned = exchange(slotted.reshape(data_count, slot_count * shard_rows, local_cols))
    owned = owned.reshape(data_count, slot_count, shard_rows, local_cols)
    owned = jnp.swapaxes(owned, 0, 1).reshape(slot_count, model_width, local_cols)
    whole = gather_columns(owned, "mp")
    slot_match_own = lax.dynamic_slice_in_dim(slot_match, data_index * slot_count, slot_count, 0)
    weights_all = jnp.concatenate([weights_one, weights_two], axis=1)

    row_total_count = left_stats.shape[1]
    lefts, rights, directions, squares, owned_weights = [], [], [], [], []
    for s in range(slot_count):
        grads = whole[s]
        my_rows = lax.dynamic_slice_in_dim(
            grads, model_index * row_total_count, row_total_count, 0
        )
        lefts.append(stat_decay * left_stats[s] + dot_nt(my_rows, grads))
        rights.append(stat_decay * right_stats[s] + dot_tn(owned[s], grads))
        halfway = dot_nt(grads, right_roots[s].astype(low_type))
        direction = dot(left_roots[s].astype(low_type), halfway.astype(low_type))
        directions.append(direction)
        squares.append(jnp.sum(direction * direction))
        chosen = 0.0
        for b in range(blocks):
            chosen = chosen + jnp.where(
                slot_match_own[s, b],
                weights_all[:, b * local_cols : (b + 1) * local_cols].astype(f32),
                0.0,
            )
        owned_weights.append(chosen)
    square_total = sum_over(jnp.stack(squares).reshape(1, slot_count), "mp")[0]
    factor = lax.rsqrt(square_total / (model_width * model_width) + mean_eps)
    updated_blocks = jnp.stack(
        [
            owned_weights[s] - matrix_rate * factor[s] * directions[s]
            for s in range(slot_count)
        ],
        axis=1,
    )
    owned_grads = jnp.swapaxes(owned, 0, 1).astype(f32)
    new_norm_state = stat_decay * norm_state + norm_total * norm_total
    new_norm_vectors = norm_vectors - vector_rate * norm_total / (
        jnp.sqrt(new_norm_state) + diag_eps
    )
    new_head_state = stat_decay * head_state + head_total * head_total
    new_head_vectors = head_vectors - vector_rate * head_total / (
        jnp.sqrt(new_head_state) + diag_eps
    )
    return (
        jnp.stack(outputs_given),
        jnp.stack(inputs_given),
        owned_grads,
        jnp.stack(lefts),
        jnp.stack(rights),
        updated_blocks,
        norm_total,
        new_norm_state,
        new_norm_vectors,
        head_total,
        new_head_state,
        new_head_vectors,
    )


def solution(mesh):
    placed = (
        P(None, "dp", None),
        P(None, "dp", None),
        P(None, "dp", None),
        P(),
        P(),
        P("dp", None, "mp"),
        P(None, "dp"),
        P(None, "mp"),
        P("dp", "mp", None),
        P("dp", "mp", None),
        P("dp", None, None),
        P("dp", "mp", None),
        P(None, "dp"),
        P(None, "mp"),
    )
    return jax.shard_map(
        on_device,
        mesh=mesh,
        in_specs=placed,
        out_specs=(
            P(None, "dp", None),
            P(None, "dp", None),
            P(None, "dp", "mp"),
            P("dp", "mp", None),
            P("dp", "mp", None),
            P(None, "dp", "mp"),
            P(None, "dp"),
            P(None, "dp"),
            P(None, "dp"),
            P(None, "mp"),
            P(None, "mp"),
            P(None, "mp"),
        ),
        check_vma=False,
    )
```

time: 1650 us -> 795 us (0.48)
  waiting for transfers between devices: 871 us -> 307 us
  local copies, waits for them, and re-layouts: 216 us -> 48.4 us
  blocking collectives: 93.3 us -> 0 us
  starting transfers between devices: 50.7 us -> 100 us
  other arithmetic: 160 us -> 115 us
  matrix products: 231 us -> 200 us
    psum x3 -> x0, waiting for transfers between devices: 428 us -> none  [model_rows(): lax.psum(jnp.einsum('qk,mk->qm', left, right, preferred_element_type=jnp....]
    all_to_all x10 -> x9, waiting for transfers between devices: 343 us -> 48.5 us  [exchange(): return lax.all_to_all(rows, 'dp', split_axis=0, concat_axis=0, tiled=True)]
    ppermute x0 -> x79, waiting for transfers between devices: none -> 170 us  [swap(): return lax.ppermute(values, axis, [(i, i ^ bit) for i in range(count)])]
    reduce_scatter x2 -> x0, waiting for transfers between devices: 100 us -> none  [the longest x1 100 us: on_device(): lax.psum_scatter(weight_grads, 'dp', scatter_dimension=0, tiled=True)]
    gather x14 -> x4, local copies, waits for them, and re-layouts: 102 us -> 4.52 us  [the longest x1 2.84 us: on_device(): summed[block_of]]
    unnamed x7 -> x6, waiting for transfers between devices: 0.11 us -> 89.3 us
    ppermute x0 -> x79, starting transfers between devices: none -> 59.2 us  [swap(): return lax.ppermute(values, axis, [(i, i ^ bit) for i in range(count)])]
    psum x2 -> x0, blocking collectives: 54.9 us -> none  [the longest x1 48.9 us: on_device(): head_total = lax.psum(head_grads_local, 'dp')]
  transfers between devices with their start and end apart: 17 -> 92, of which waited for: 10 -> 31; matrix products, arithmetic and copies ran while one was open for 27% -> 34% of each run, Pallas kernels for 0% -> 0%
where the time goes in v1:
time: 795 us; the launch traced here: 788 us
  waiting for transfers between devices  307 us (39%)
  matrix products  200 us (25%)
  other arithmetic  115 us (14%)
  starting transfers between devices  100 us (13%)
  local copies, waits for them, and re-layouts  48.4 us (6%)
  between operations  17.5 us (2%)
    ppermute x79, waiting for transfers between devices, swap(): return lax.ppermute(values, axis, [(i, i ^ bit) for i in range(count)])  170 us
    unnamed x6, waiting for transfers between devices  89.3 us
    dot_general x20, matrix products, dot(): lax.dot_general(left, right, (((1,), (0,)), ((), ())), preferred_element_...  77.2 us
    ppermute x79, starting transfers between devices, swap(): return lax.ppermute(values, axis, [(i, i ^ bit) for i in range(count)])  59.2 us
    all_to_all x9, waiting for transfers between devices, exchange(): return lax.all_to_all(rows, 'dp', split_axis=0, concat_axis=0, tiled=True)  48.5 us
    all_to_all x9, starting transfers between devices, exchange(): return lax.all_to_all(rows, 'dp', split_axis=0, concat_axis=0, tiled=True)  40.6 us
    dot_general x10, matrix products, dot_tn(): lax.dot_general(left, right, (((0,), (0,)), ((), ())), preferred_element_...  28.6 us
    unnamed x256, local copies, waits for them, and re-layouts  24 us
  transfers between devices with their start and end apart: 92, of which 31 were waited for; matrix products, arithmetic and copies ran while one was open for 34% of the time, Pallas kernels for 0%

profile of v1, /device:TPU:0, one launch (start us, length us, event | category | flops | bytes accessed | tf_op | source)
XLA Modules:
  0.0 788.4 jit_solution(4896526333637559768)
XLA Ops:
  50.9 24.5 %all-to-all-done = bf16[8,32,1024]{2,1,0:T(8,128)(2,1)S(1)} async-done(((bf16[8,32,1024]{2,1,0:T(8,128)(2,1)}), bf16[8,32,1024]{2,1,0:T(8,128)(2,1)S(1)}, u32[]{:S(2)}, u32[]{:S(2)}) %all-to-all-start) | async-done | bytes 524320 | tf_op jit(solution)/shard_map/all_to_all | solution.py:114
  82.8 9.2 %collective-permute-done.23 = bf16[256,1024]{1,0:T(8,128)(2,1)S(1)} collective-permute-done((bf16[256,1024]{1,0:T(8,128)(2,1)S(1)}, bf16[256,1024]{1,0:T(8,128)(2,1)S(1)}, u32[]{:S(2)}, u32[]{:S(2)}) %collective-permute-start.23) | collective-permute-done | bytes 524320 | tf_op jit(solution)/shard_map/ppermute | solution.py:60
  94.4 7.6 collective-permute-done.8
  113.6 11.4 %fusion.406 = (f32[4,1024]{1,0:T(4,128)S(1)}, f32[4,1024,1024]{1,2,0:T(8,128)}) fusion(pred[1024,1024]{0,1:T(8,128)(4,1)} %compare_and_fusion, bf16[1024,4,64]{0,2,1:T(8,128)(2,1)} %bitcast.408, bf16[1024,4,64]{0,2,1:T(8,128)(2,1)} %bitcast.412), kind=kOutput, calls=%fused_computation.597 | convolution fusion | flops 553649152 | bytes 18890752 | tf_op jit(solution)/shard_map/sub | solution.py:244
  125.1 7.6 fusion.158
  137.1 11.3 %fusion.404 = (f32[4,1024]{1,0:T(4,128)S(1)}, f32[4,1024,1024]{1,2,0:T(8,128)}) fusion(pred[1024,1024]{0,1:T(8,128)(4,1)} %compare_and_fusion.1, bf16[1024,4,64]{0,2,1:T(8,128)(2,1)} %bitcast.406, bf16[1024,4,64]{0,2,1:T(8,128)(2,1)} %bitcast.410), kind=kOutput, calls=%fused_computation.595 | convolution fusion | flops 553649152 | bytes 18890752 | tf_op jit(solution)/shard_map/sub | solution.py:244
  148.4 7.5 fusion.152
  175.7 10.3 %collective-permute-done.12 = bf16[256,1024]{1,0:T(8,128)(2,1)S(1)} collective-permute-done((bf16[256,1024]{1,0:T(8,128)(2,1)S(1)}, bf16[256,1024]{1,0:T(8,128)(2,1)S(1)}, u32[]{:S(2)}, u32[]{:S(2)}) %collective-permute-start.12) | collective-permute-done | bytes 524320 | tf_op jit(solution)/shard_map/ppermute | solution.py:60
  200.2 8.8 %all-to-all-done.6 = bf16[8,32,1024]{2,1,0:T(8,128)(2,1)S(1)} async-done(((bf16[8,32,1024]{2,1,0:T(8,128)(2,1)}), bf16[8,32,1024]{2,1,0:T(8,128)(2,1)S(1)}, u32[]{:S(2)}, u32[]{:S(2)}) %all-to-all-start.6) | async-done | bytes 524320 | tf_op jit(solution)/shard_map/all_to_all | solution.py:114
  212.6 10.7 %collective-permute-done.38 = bf16[256,1024]{1,0:T(8,128)(2,1)} collective-permute-done((bf16[256,1024]{1,0:T(8,128)(2,1)S(1)}, bf16[256,1024]{1,0:T(8,128)(2,1)}, u32[]{:S(2)}, u32[]{:S(2)}) %collective-permute-start.38) | collective-permute-done | bytes 524320 | tf_op jit(solution)/shard_map/ppermute | solution.py:60
  223.3 9.2 %collective-permute-done.53 = bf16[256,1024]{1,0:T(8,128)(2,1)} collective-permute-done((bf16[256,1024]{1,0:T(8,128)(2,1)}, bf16[256,1024]{1,0:T(8,128)(2,1)}, u32[]{:S(2)}, u32[]{:S(2)}) %collective-permute-start.53) | collective-permute-done | bytes 524320 | tf_op jit(solution)/shard_map/ppermute | solution.py:60
  247.8 7.8 convert_reduce_fusion
  261.9 8.1 %convert_reduce_fusion.1 = (f32[1024]{0:T(1024)}, bf16[1024,1024]{1,0:T(8,128)(2,1)S(1)}) fusion(f32[1024,1024]{1,0:T(8,128)S(1)} %fusion.150, f32[1024]{0:T(1024)S(1)} %bitcast.486, bf16[1024,2048]{0,1:T(8,128)(2,1)S(1)} %copy-done.5, bf16[256,1024]{1,0:T(8,128)(2,1)} %collective-permute-done.39, bf16[256,1024]{1,0:T(8,128)(2,1)} %collective-permute-done.38, ...), kind=kOutput, calls=%fused_computation.47 | convolution fusion | flops 2179988480 | bytes 10493952 | tf_op jit(solution)/shard_map/dot_general | solution.py:47
  281.9 10.0 %collective-permute-done.57 = bf16[256,1024]{1,0:T(8,128)(2,1)S(1)} collective-permute-done((bf16[256,1024]{1,0:T(8,128)(2,1)S(1)}, bf16[256,1024]{1,0:T(8,128)(2,1)S(1)}, u32[]{:S(2)}, u32[]{:S(2)}) %collective-permute-start.57) | collective-permute-done | bytes 524320 | tf_op jit(solution)/shard_map/ppermute | solution.py:60
  293.4 9.8 %collective-permute-done.42 = bf16[256,1024]{1,0:T(8,128)(2,1)S(1)} collective-permute-done((bf16[256,1024]{1,0:T(8,128)(2,1)S(1)}, bf16[256,1024]{1,0:T(8,128)(2,1)S(1)}, u32[]{:S(2)}, u32[]{:S(2)}) %collective-permute-start.42) | collective-permute-done | bytes 524320 | tf_op jit(solution)/shard_map/ppermute | solution.py:60
  305.0 9.4 %collective-permute-done.33 = bf16[256,1024]{1,0:T(8,128)(2,1)S(1)} collective-permute-done((bf16[256,1024]{1,0:T(8,128)(2,1)S(1)}, bf16[256,1024]{1,0:T(8,128)(2,1)S(1)}, u32[]{:S(2)}, u32[]{:S(2)}) %collective-permute-start.33) | collective-permute-done | bytes 524320 | tf_op jit(solution)/shard_map/ppermute | solution.py:60
  319.1 6.6 collective-permute-done.18
  337.4 10.0 %collective-permute-done.44 = bf16[256,1024]{1,0:T(8,128)(2,1)} collective-permute-done((bf16[256,1024]{1,0:T(8,128)(2,1)}, bf16[256,1024]{1,0:T(8,128)(2,1)}, u32[]{:S(2)}, u32[]{:S(2)}) %collective-permute-start.44) | collective-permute-done | bytes 524320 | tf_op jit(solution)/shard_map/ppermute | solution.py:60
  353.9 7.1 multiply_reduce_fusion
  361.1 12.5 %multiply_convert_fusion = bf16[4,1024,1024]{1,2,0:T(8,128)(2,1)S(1)} fusion(f32[4,1024,1024]{1,2,0:T(8,128)} %get-tuple-element.221, f32[4,1024]{1,0:T(4,128)S(1)} %get-tuple-element.220, f32[4,1024,1024]{1,2,0:T(8,128)} %get-tuple-element.209, f32[4,1024]{1,0:T(4,128)S(1)} %get-tuple-element.208), kind=kLoop, calls=%fused_computation.6 | loop fusion | flops 16777216 | bytes 41975808 | tf_op jit(solution)/shard_map/convert_element_type | solution.py:299
  387.4 9.5 %multiply_reduce_fusion.1 = (f32[4,1024]{1,0:T(4,128)S(1)}, f32[4,1024,1024]{1,2,0:T(8,128)}) fusion(f32[4,1024,1024]{1,2,0:T(8,128)S(1)} %bitcast.398, f32[4,1024]{1,0:T(4,128)S(1)} %copy-done.58, bf16[1024,4,64]{0,2,1:T(8,128)(2,1)} %bitcast.499, bf16[1024,4,64]{0,2,1:T(8,128)(2,1)} %bitcast.425), kind=kOutput, calls=%fused_computation.9 | convolution fusion | flops 549449728 | bytes 34635776 | tf_op jit(solution)/shard_map/qhd,khd->hqk/dot_general | solution.py:295
  396.9 7.9 %multiply_convert_fusion.1 = bf16[4,1024,1024]{1,2,0:T(8,128)(2,1)S(1)} fusion(f32[4,1024,1024]{1,2,0:T(8,128)} %get-tuple-element.223, f32[4,1024]{1,0:T(4,128)S(1)} %get-tuple-element.222, f32[4,1024,1024]{1,2,0:T(8,128)S(1)} %bitcast.398, f32[4,1024]{1,0:T(4,128)S(1)} %copy-done.58), kind=kLoop, calls=%fused_computation.8 | loop fusion | flops 16777216 | bytes 41975808 | tf_op jit(solution)/shard_map/convert_element_type | solution.py:299
  444.9 6.5 copy.129
  451.4 6.1 all-to-all-start.3
  483.6 8.4 %collective-permute-done.63 = bf16[256,1024]{1,0:T(8,128)(2,1)} collective-permute-done((bf16[256,1024]{1,0:T(8,128)(2,1)}, bf16[256,1024]{1,0:T(8,128)(2,1)}, u32[]{:S(2)}, u32[]{:S(2)}) %collective-permute-start.63) | collective-permute-done | bytes 524320 | tf_op jit(solution)/shard_map/ppermute | solution.py:60
  504.5 89.2 %reduce-scatter.9.cloned.1.call-done = bf16[128,2048]{1,0:T(8,128)(2,1)} async-done(((bf16[1024,2048]{1,0:T(8,128)(2,1)}), bf16[128,2048]{1,0:T(8,128)(2,1)}) %reduce-scatter.9.cloned.1.call-update) | async-done | bytes 524304
  626.7 7.4 all-to-all-done.8
  698.1 29.5 %collective-permute-done.68 = bf16[2,1024,512]{2,1,0:T(8,128)(2,1)S(1)} collective-permute-done((bf16[2,1024,512]{2,1,0:T(8,128)(2,1)S(1)}, bf16[2,1024,512]{2,1,0:T(8,128)(2,1)S(1)}, u32[]{:S(2)}, u32[]{:S(2)}) %collective-permute-start.68) | collective-permute-done | bytes 2097184 | tf_op jit(solution)/shard_map/ppermute | solution.py:60
  730.2 6.3 multiply_reduce_fusion.7
  736.5 6.3 multiply_reduce_fusion.6
  761.0 9.1 %fusion.205 = f32[1024,1,256]{0,2,1:T(8,128)S(1)} fusion(f32[256,1024]{1,0:T(8,128)S(1)} %copy-done.23, f32[]{:T(128)} %bitcast.127, pred[]{:T(512)} %bitcast.119, pred[]{:T(512)} %bitcast.118, pred[]{:T(512)} %bitcast.117, pred[]{:T(512)} %bitcast.116, pred[]{:T(512)} %bitcast.115, pred[]{:T(512)} %bitcast.114, pred[]{:T(512)} %bitcast.113, pred[]{:T(512)} %bitcast.112, ...), kind=kLoop, calls=%fused_computation.242 | loop fusion | flops 9699328 | bytes 8388624 | tf_op jit(solution)/shard_map/stack | solution.py:401
  770.1 8.9 %fusion.218 = f32[1024,1,256]{0,2,1:T(8,128)S(1)} fusion(f32[256,1024]{1,0:T(8,128)S(1)} %copy-done.22, f32[]{:T(128)} %bitcast.142, pred[]{:T(512)} %bitcast.141, pred[]{:T(512)} %bitcast.140, pred[]{:T(512)} %bitcast.139, pred[]{:T(512)} %bitcast.138, pred[]{:T(512)} %bitcast.137, pred[]{:T(512)} %bitcast.136, pred[]{:T(512)} %bitcast.135, pred[]{:T(512)} %bitcast.134, ...), kind=kLoop, calls=%fused_computation.255 | loop fusion | flops 9699328 | bytes 8388624 | tf_op jit(solution)/shard_map/stack | solution.py:401
  (630 shorter events, 376.3 us)
Async XLA Ops:
  7.2 95.7 %all-gather.3.cloned.1.call-start = ((), (), s32[]{:S(2)}) async-start(), calls=%async_computation.11 | async-start | bytes 2359296 | tf_op jit(solution)/shard_map/all_gather | solution.py:155
  10.3 26.0 %collective-permute-start.1 = (bf16[6,128]{1,0:T(8,128)(2,1)S(1)}, bf16[6,128]{1,0:T(8,128)(2,1)S(1)}, u32[]{:S(2)}, u32[]{:S(2)}) collective-permute-start(bf16[6,128]{1,0:T(8,128)(2,1)S(1)} %get-tuple-element.121), channel_id=1, source_target_pairs={{0,8},{4,12},{8,0},{12,4},{16,24},{20,28},{24,16},{28,20},{1,9},{5... | collective-permute-start | bytes 4616 | tf_op jit(solution)/shard_map/ppermute | solution.py:60
  13.3 23.5 %collective-permute-start = (bf16[6,128]{1,0:T(8,128)(2,1)S(1)}, bf16[6,128]{1,0:T(8,128)(2,1)S(1)}, u32[]{:S(2)}, u32[]{:S(2)}) collective-permute-start(bf16[6,128]{1,0:T(8,128)(2,1)S(1)} %get-tuple-element.121), channel_id=1, source_target_pairs={{0,4},{4,0},{8,12},{12,8},{16,20},{20,16},{24,28},{28,24},{1,5},{5... | collective-permute-start | bytes 4616 | tf_op jit(solution)/shard_map/ppermute | solution.py:60
  22.3 22.9 %all-to-all-start.2 = ((bf16[8,32,1024]{2,1,0:T(8,128)(2,1)}), bf16[8,32,1024]{2,1,0:T(8,128)(2,1)S(1)}, u32[]{:S(2)}, u32[]{:S(2)}) async-start(bf16[8,32,1024]{2,1,0:T(8,128)(2,1)} %bitcast.42), calls=%async_computation.2 | async-start | bytes 1048576 | tf_op jit(solution)/shard_map/all_to_all | solution.py:114
  25.8 208.7 %all-gather.5.cloned.1.call-start = ((), (), s32[]{:S(2)}) async-start(), calls=%async_computation.12 | async-start | bytes 4718592 | tf_op jit(solution)/shard_map/all_gather | solution.py:156
  45.3 30.1 %all-to-all-start = ((bf16[8,32,1024]{2,1,0:T(8,128)(2,1)}), bf16[8,32,1024]{2,1,0:T(8,128)(2,1)S(1)}, u32[]{:S(2)}, u32[]{:S(2)}) async-start(bf16[8,32,1024]{2,1,0:T(8,128)(2,1)} %bitcast.4), calls=%async_computation | async-start | bytes 1048576 | tf_op jit(solution)/shard_map/all_to_all | solution.py:114
  162.5 23.5 %collective-permute-start.12 = (bf16[256,1024]{1,0:T(8,128)(2,1)S(1)}, bf16[256,1024]{1,0:T(8,128)(2,1)S(1)}, u32[]{:S(2)}, u32[]{:S(2)}) collective-permute-start(bf16[256,1024]{1,0:T(8,128)(2,1)S(1)} %fusion.243), channel_id=1, source_target_pairs={{0,2},{1,3},{2,0},{3,1},{4,6},{5,7},{6,4},{7,5},{8,10},{9,11},{10,... | collective-permute-start | bytes 1572872 | tf_op jit(solution)/shard_map/ppermute | solution.py:60
  164.7 25.5 %all-to-all-start.4 = ((bf16[8,32,1024]{2,1,0:T(8,128)(2,1)}), bf16[8,32,1024]{2,1,0:T(8,128)(2,1)}, u32[]{:S(2)}, u32[]{:S(2)}) async-start(bf16[8,32,1024]{2,1,0:T(8,128)(2,1)} %bitcast.56), calls=%async_computation.4 | async-start | bytes 1048576 | tf_op jit(solution)/shard_map/all_to_all | solution.py:114
  195.0 308.3 %reduce-scatter.7.cloned.1.call-start = ((), (), s32[]{:S(2)}) async-start(), calls=%async_computation.13 | async-start | bytes 2359296
  199.6 23.7 %collective-permute-start.38 = (bf16[256,1024]{1,0:T(8,128)(2,1)S(1)}, bf16[256,1024]{1,0:T(8,128)(2,1)}, u32[]{:S(2)}, u32[]{:S(2)}) collective-permute-start(bf16[256,1024]{1,0:T(8,128)(2,1)S(1)} %fusion.287), channel_id=1, source_target_pairs={{0,2},{1,3},{2,0},{3,1},{4,6},{5,7},{6,4},{7,5},{8,10},{9,11},{10,... | collective-permute-start | bytes 1572872 | tf_op jit(solution)/shard_map/ppermute | solution.py:60
  210.0 22.6 %collective-permute-start.53 = (bf16[256,1024]{1,0:T(8,128)(2,1)}, bf16[256,1024]{1,0:T(8,128)(2,1)}, u32[]{:S(2)}, u32[]{:S(2)}) collective-permute-start(bf16[256,1024]{1,0:T(8,128)(2,1)} %fusion.288), channel_id=1, source_target_pairs={{0,2},{1,3},{2,0},{3,1},{4,6},{5,7},{6,4},{7,5},{8,10},{9,11},{10,... | collective-permute-start | bytes 1572872 | tf_op jit(solution)/shard_map/ppermute | solution.py:60
  212.1 49.8 %collective-permute-start.37 = (bf16[256,1024]{1,0:T(8,128)(2,1)S(1)}, bf16[256,1024]{1,0:T(8,128)(2,1)}, u32[]{:S(2)}, u32[]{:S(2)}) collective-permute-start(bf16[256,1024]{1,0:T(8,128)(2,1)S(1)} %fusion.287), channel_id=1, source_target_pairs={{0,1},{1,0},{2,3},{3,2},{4,5},{5,4},{6,7},{7,6},{8,9},{9,8},{10,11... | collective-permute-start | bytes 1572872 | tf_op jit(solution)/shard_map/ppermute | solution.py:60
  232.5 29.4 %collective-permute-start.39 = (bf16[256,1024]{1,0:T(8,128)(2,1)}, bf16[256,1024]{1,0:T(8,128)(2,1)}, u32[]{:S(2)}, u32[]{:S(2)}) collective-permute-start(bf16[256,1024]{1,0:T(8,128)(2,1)} %collective-permute-done.38), channel_id=1, source_target_pairs={{0,1},{1,0},{2,3},{3,2},{4,5},{5,4},{6,7},{7,6},{8,9},{9,8},{10,11... | collective-permute-start | bytes 1572872 | tf_op jit(solution)/shard_map/ppermute | solution.py:60
  247.3 31.5 %collective-permute-start.32 = (bf16[256,1024]{1,0:T(8,128)(2,1)S(1)}, bf16[256,1024]{1,0:T(8,128)(2,1)S(1)}, u32[]{:S(2)}, u32[]{:S(2)}) collective-permute-start(bf16[256,1024]{1,0:T(8,128)(2,1)S(1)} %get-tuple-element.141), channel_id=1, source_target_pairs={{0,1},{1,0},{2,3},{3,2},{4,5},{5,4},{6,7},{7,6},{8,9},{9,8},{10,11... | collective-permute-start | bytes 1572872 | tf_op jit(solution)/shard_map/ppermute | solution.py:60
  278.8 24.4 %collective-permute-start.42 = (bf16[256,1024]{1,0:T(8,128)(2,1)S(1)}, bf16[256,1024]{1,0:T(8,128)(2,1)S(1)}, u32[]{:S(2)}, u32[]{:S(2)}) collective-permute-start(bf16[256,1024]{1,0:T(8,128)(2,1)S(1)} %fusion.225), channel_id=1, source_target_pairs={{0,2},{1,3},{2,0},{3,1},{4,6},{5,7},{6,4},{7,5},{8,10},{9,11},{10,... | collective-permute-start | bytes 1572872 | tf_op jit(solution)/shard_map/ppermute | solution.py:60
  279.6 25.4 %collective-permute-start.31 = (bf16[256,1024]{1,0:T(8,128)(2,1)S(1)}, bf16[256,1024]{1,0:T(8,128)(2,1)S(1)}, u32[]{:S(2)}, u32[]{:S(2)}) collective-permute-start(bf16[256,1024]{1,0:T(8,128)(2,1)S(1)} %get-tuple-element.140), channel_id=1, source_target_pairs={{0,1},{1,0},{2,3},{3,2},{4,5},{5,4},{6,7},{7,6},{8,9},{9,8},{10,11... | collective-permute-start | bytes 1572872 | tf_op jit(solution)/shard_map/ppermute | solution.py:60
  279.9 39.2 %collective-permute-start.16 = (bf16[256,1024]{1,0:T(8,128)(2,1)S(1)}, bf16[256,1024]{1,0:T(8,128)(2,1)S(1)}, u32[]{:S(2)}, u32[]{:S(2)}) collective-permute-start(bf16[256,1024]{1,0:T(8,128)(2,1)S(1)} %get-tuple-element.136), channel_id=1, source_target_pairs={{0,1},{1,0},{2,3},{3,2},{4,5},{5,4},{6,7},{7,6},{8,9},{9,8},{10,11... | collective-permute-start | bytes 1572872 | tf_op jit(solution)/shard_map/ppermute | solution.py:60
  280.4 34.0 %collective-permute-start.33 = (bf16[256,1024]{1,0:T(8,128)(2,1)S(1)}, bf16[256,1024]{1,0:T(8,128)(2,1)S(1)}, u32[]{:S(2)}, u32[]{:S(2)}) collective-permute-start(bf16[256,1024]{1,0:T(8,128)(2,1)S(1)} %fusion.227), channel_id=1, source_target_pairs={{0,2},{1,3},{2,0},{3,1},{4,6},{5,7},{6,4},{7,5},{8,10},{9,11},{10,... | collective-permute-start | bytes 1572872 | tf_op jit(solution)/shard_map/ppermute | solution.py:60
  291.9 33.7 %collective-permute-start.18 = (bf16[256,1024]{1,0:T(8,128)(2,1)S(1)}, bf16[256,1024]{1,0:T(8,128)(2,1)S(1)}, u32[]{:S(2)}, u32[]{:S(2)}) collective-permute-start(bf16[256,1024]{1,0:T(8,128)(2,1)S(1)} %fusion.238), channel_id=1, source_target_pairs={{0,2},{1,3},{2,0},{3,1},{4,6},{5,7},{6,4},{7,5},{8,10},{9,11},{10,... | collective-permute-start | bytes 1572872 | tf_op jit(solution)/shard_map/ppermute | solution.py:60
  336.9 42.6 %collective-permute-start.43 = (bf16[256,1024]{1,0:T(8,128)(2,1)}, bf16[256,1024]{1,0:T(8,128)(2,1)}, u32[]{:S(2)}, u32[]{:S(2)}) collective-permute-start(bf16[256,1024]{1,0:T(8,128)(2,1)} %convert_element_type.528), channel_id=1, source_target_pairs={{0,1},{1,0},{2,3},{3,2},{4,5},{5,4},{6,7},{7,6},{8,9},{9,8},{10,11... | collective-permute-start | bytes 1572872 | tf_op jit(solution)/shard_map/ppermute | solution.py:60
  347.4 32.1 %collective-permute-start.45 = (bf16[256,1024]{1,0:T(8,128)(2,1)}, bf16[256,1024]{1,0:T(8,128)(2,1)}, u32[]{:S(2)}, u32[]{:S(2)}) collective-permute-start(bf16[256,1024]{1,0:T(8,128)(2,1)} %collective-permute-done.44), channel_id=1, source_target_pairs={{0,1},{1,0},{2,3},{3,2},{4,5},{5,4},{6,7},{7,6},{8,9},{9,8},{10,11... | collective-permute-start | bytes 1572872 | tf_op jit(solution)/shard_map/ppermute | solution.py:60
  424.8 168.9 %reduce-scatter.9.cloned.1.call-start = ((), (), s32[]{:S(2)}) async-start(), calls=%async_computation.14 | async-start | bytes 4718592
  468.8 23.2 %collective-permute-start.63 = (bf16[256,1024]{1,0:T(8,128)(2,1)}, bf16[256,1024]{1,0:T(8,128)(2,1)}, u32[]{:S(2)}, u32[]{:S(2)}) collective-permute-start(bf16[256,1024]{1,0:T(8,128)(2,1)} %fusion.219), channel_id=1, source_target_pairs={{0,2},{1,3},{2,0},{3,1},{4,6},{5,7},{6,4},{7,5},{8,10},{9,11},{10,... | collective-permute-start | bytes 1572872 | tf_op jit(solution)/shard_map/ppermute | solution.py:60
  472.8 26.0 %all-to-all-start.1 = ((bf16[8,32,1024]{2,1,0:T(8,128)(2,1)}), bf16[8,32,1024]{2,1,0:T(8,128)(2,1)}, u32[]{:S(2)}, u32[]{:S(2)}) async-start(bf16[8,32,1024]{2,1,0:T(8,128)(2,1)} %bitcast.418), calls=%async_computation.1 | async-start | bytes 1048576 | tf_op jit(solution)/shard_map/all_to_all | solution.py:114
  498.8 104.9 %all-to-all-start.5 = ((bf16[8,32,1024]{2,1,0:T(8,128)(2,1)}), bf16[8,32,1024]{2,1,0:T(8,128)(2,1)}, u32[]{:S(2)}, u32[]{:S(2)}) async-start(bf16[8,32,1024]{2,1,0:T(8,128)(2,1)} %bitcast.414), calls=%async_computation.5 | async-start | bytes 1048576 | tf_op jit(solution)/shard_map/all_to_all | solution.py:114
  603.6 30.5 %all-to-all-start.8 = ((bf16[8,256,256]{2,1,0:T(8,128)(2,1)}), bf16[8,256,256]{2,1,0:T(8,128)(2,1)}, u32[]{:S(2)}, u32[]{:S(2)}) async-start(bf16[8,256,256]{2,1,0:T(8,128)(2,1)} %bitcast_select_fusion), calls=%async_computation.8 | async-start | bytes 2097152 | tf_op jit(solution)/shard_map/all_to_all | solution.py:114
  613.6 42.0 %collective-permute-start.19 = (bf16[256,1024]{1,0:T(8,128)(2,1)}, bf16[256,1024]{1,0:T(8,128)(2,1)}, u32[]{:S(2)}, u32[]{:S(2)}) collective-permute-start(bf16[256,1024]{1,0:T(8,128)(2,1)} %bitcast.36), channel_id=1, source_target_pairs={{0,1},{1,0},{2,3},{3,2},{4,5},{5,4},{6,7},{7,6},{8,9},{9,8},{10,11... | collective-permute-start | bytes 1572872 | tf_op jit(solution)/shard_map/ppermute | solution.py:60
  613.7 40.7 %collective-permute-start.35 = (bf16[256,1024]{1,0:T(8,128)(2,1)}, bf16[256,1024]{1,0:T(8,128)(2,1)}, u32[]{:S(2)}, u32[]{:S(2)}) collective-permute-start(bf16[256,1024]{1,0:T(8,128)(2,1)} %bitcast.53), channel_id=1, source_target_pairs={{0,2},{1,3},{2,0},{3,1},{4,6},{5,7},{6,4},{7,5},{8,10},{9,11},{10,... | collective-permute-start | bytes 1572872 | tf_op jit(solution)/shard_map/ppermute | solution.py:60
  615.1 24.0 %collective-permute-start.77 = (f32[6,256]{1,0:T(8,128)S(1)}, f32[6,256]{1,0:T(8,128)S(1)}, u32[]{:S(2)}, u32[]{:S(2)}) collective-permute-start(f32[6,256]{1,0:T(8,128)S(1)} %add.703), channel_id=1, source_target_pairs={{0,8},{4,12},{8,0},{12,4},{16,24},{20,28},{24,16},{28,20},{1,9},{5... | collective-permute-start | bytes 18440 | tf_op jit(solution)/shard_map/ppermute | solution.py:60
  623.2 33.9 %collective-permute-start.21 = (bf16[256,1024]{1,0:T(8,128)(2,1)}, bf16[256,1024]{1,0:T(8,128)(2,1)}, u32[]{:S(2)}, u32[]{:S(2)}) collective-permute-start(bf16[256,1024]{1,0:T(8,128)(2,1)} %collective-permute-done.20), channel_id=1, source_target_pairs={{0,1},{1,0},{2,3},{3,2},{4,5},{5,4},{6,7},{7,6},{8,9},{9,8},{10,11... | collective-permute-start | bytes 1572872 | tf_op jit(solution)/shard_map/ppermute | solution.py:60
  634.1 30.4 %all-to-all-start.7 = ((bf16[8,32,1024]{2,1,0:T(8,128)(2,1)}), bf16[8,32,1024]{2,1,0:T(8,128)(2,1)}, u32[]{:S(2)}, u32[]{:S(2)}) async-start(bf16[8,32,1024]{2,1,0:T(8,128)(2,1)} %bitcast.78), calls=%async_computation.7 | async-start | bytes 1048576 | tf_op jit(solution)/shard_map/all_to_all | solution.py:114
  674.4 53.1 %collective-permute-start.68 = (bf16[2,1024,512]{2,1,0:T(8,128)(2,1)S(1)}, bf16[2,1024,512]{2,1,0:T(8,128)(2,1)S(1)}, u32[]{:S(2)}, u32[]{:S(2)}) collective-permute-start(bf16[2,1024,512]{2,1,0:T(8,128)(2,1)S(1)} %maximum_select_fusion.1), channel_id=1, source_target_pairs={{0,2},{1,3},{2,0},{3,1},{4,6},{5,7},{6,4},{7,5},{8,10},{9,11},{10,... | collective-permute-start | bytes 6291464 | tf_op jit(solution)/shard_map/ppermute | solution.py:60
  (180 other events, 2809.4 us)
Sparse Core Ops, SparseCore 0:
  10.6 69.1 all-gather.2
  81.9 76.1 all-gather.4
  424.9 76.4 reduce-scatter.6
  504.9 88.7 reduce-scatter.8

commit v2 on v1

v2 whole, which is shorter than its diff:
```python
import functools
import math

import jax
import jax.numpy as jnp
from jax import lax
from jax.experimental import pallas as pl
from jax.experimental.pallas import tpu as pltpu
from jax.sharding import PartitionSpec as P

HEAD_DIM = 64


stat_decay = 0.5
matrix_rate = 0.02
vector_rate = 0.3
norm_eps = 1e-05
mean_eps = 1e-06
diag_eps = 1e-08
masked_score = -1000000000.0

f32 = jnp.float32
low_type = jnp.bfloat16


def unit_rows_of(values):
    center = values - jnp.mean(values, axis=-1, keepdims=True)
    spread = jnp.mean(center * center, axis=-1, keepdims=True)
    scale_rows = lax.rsqrt(spread + norm_eps)
    return center * scale_rows, scale_rows


def layer_norm(values, gain, shift):
    unit_rows, _ = unit_rows_of(values)
    return unit_rows * gain + shift


def norm_back(values, gain, grad_normed):
    unit_rows, scale_rows = unit_rows_of(values)
    grad_unit = grad_normed * gain
    grad_values = scale_rows * (
        grad_unit
        - jnp.mean(grad_unit, axis=-1, keepdims=True)
        - unit_rows * jnp.mean(grad_unit * unit_rows, axis=-1, keepdims=True)
    )
    return (grad_values, grad_normed * unit_rows)


def dot(left, right):
    return lax.dot_general(left, right, (((1,), (0,)), ((), ())), preferred_element_type=f32)


def dot_nt(left, right):
    return lax.dot_general(left, right, (((1,), (1,)), ((), ())), preferred_element_type=f32)


def dot_tn(left, right):
    return lax.dot_general(left, right, (((0,), (0,)), ((), ())), preferred_element_type=f32)


TILE = 256
STRIP = 64
VMEM_BYTES = 56 * 1024 * 1024
SMALL = pl.CostEstimate(flops=10**9, bytes_accessed=10**6, transcendentals=0)
LARGE = pl.CostEstimate(flops=20 * 10**9, bytes_accessed=10**6, transcendentals=0)
MEDIUM = pl.CostEstimate(flops=11 * 10**9, bytes_accessed=10**6, transcendentals=0)

def whole_spec():
    return pl.BlockSpec(memory_space=pltpu.VMEM)

def attention_forward_kernel(
    near_ref, far_ref, norm_ref, weights_ref, bias_ref,
    place_row_ref, place_col_ref, seg_row_ref, seg_col_ref,
    keep_ref, send_ref, normed_ref, attended_ref, qkv_ref, out_ref, lse_ref,
    arrived,
):
    rows = arrived.shape[0]
    half = rows // 2
    cols = attended_ref.shape[1]
    heads = cols // HEAD_DIM
    scale = 1.0 / math.sqrt(HEAD_DIM)
    tiles = rows // TILE
    for start, source in ((0, near_ref), (half, far_ref)):

        def norm_some(i, carry):
            values = source[pl.ds(pl.multiple_of(i * STRIP, STRIP), STRIP), :].astype(f32)
            normed = layer_norm(values, norm_ref[0:1, :], norm_ref[1:2, :])
            normed_ref[pl.ds(pl.multiple_of(start + i * STRIP, STRIP), STRIP), :] = (
                normed.astype(low_type)
            )
            return carry

        lax.fori_loop(0, half // STRIP, norm_some, 0)
    for t in range(tiles):
        part = normed_ref[pl.ds(t * TILE, TILE), :]
        arrived[pl.ds(t * TILE, TILE), :] = (
            dot(part, weights_ref[:, : 3 * cols]) + bias_ref[...]
        ).astype(low_type)
    for t in range(tiles):
        wanted = lax.broadcasted_iota(jnp.int32, (TILE, rows), 0) + t * TILE
        pick = jnp.where(wanted == place_row_ref[...], 1.0, 0.0).astype(low_type)
        qkv_ref[pl.ds(t * TILE, TILE), :] = dot(pick, arrived[...]).astype(low_type)
    for h in range(heads):
        lanes = slice(h * HEAD_DIM, (h + 1) * HEAD_DIM)
        key_lanes = slice(cols + h * HEAD_DIM, cols + (h + 1) * HEAD_DIM)
        value_lanes = slice(2 * cols + h * HEAD_DIM, 2 * cols + (h + 1) * HEAD_DIM)
        for t in range(tiles):
            here = slice(t * TILE, (t + 1) * TILE)
            query = qkv_ref[here, lanes]
            seg_q = seg_col_ref[here, :]
            scores = []
            top = None
            for c in range(t + 1):
                there = slice(c * TILE, (c + 1) * TILE)
                s = dot_nt(query, qkv_ref[there, key_lanes]) * scale
                allowed = seg_q == seg_row_ref[:, there]
                if c == t:
                    allowed = allowed & (
                        lax.broadcasted_iota(jnp.int32, (TILE, TILE), 0)
                        >= lax.broadcasted_iota(jnp.int32, (TILE, TILE), 1)
                    )
                s = jnp.where(allowed, s, masked_score)
                scores.append(s)
                m = jnp.max(s, axis=1, keepdims=True)
                top = m if top is None else jnp.maximum(top, m)
            total = 0.0
            out = 0.0
            for c in range(t + 1):
                there = slice(c * TILE, (c + 1) * TILE)
                e = jnp.exp(scores[c] - top)
                total = total + jnp.sum(e, axis=1, keepdims=True)
                out = out + dot(e.astype(low_type), qkv_ref[there, value_lanes])
            out_ref[here, lanes] = (out / total).astype(low_type)
            lse_ref[here, h : h + 1] = top + jnp.log(total)
    for t in range(tiles):
        wanted = lax.broadcasted_iota(jnp.int32, (TILE, rows), 1)
        pick = jnp.where(wanted == place_col_ref[pl.ds(t * TILE, TILE), :], 1.0, 0.0).astype(low_type)
        part = dot(pick, out_ref[...]).astype(low_type)
        attended_ref[pl.ds(t * TILE, TILE), :] = part
        branch = dot_nt(part, weights_ref[:, 3 * cols :])
        if t * TILE < half:
            keep_ref[pl.ds(t * TILE, TILE), :] = branch
        else:
            send_ref[pl.ds(t * TILE - half, TILE), :] = branch.astype(low_type)

def attention_forward(near, far, norms, weights, bias, place, segment):
    rows = 2 * near.shape[0]
    width = near.shape[1]
    cols = weights.shape[1] // 4
    heads = cols // HEAD_DIM
    shape = jax.ShapeDtypeStruct
    return pl.pallas_call(
        attention_forward_kernel,
        out_shape=(
            shape((rows // 2, width), f32),
            shape((rows // 2, width), low_type),
            shape((rows, width), low_type),
            shape((rows, cols), low_type),
            shape((rows, 3 * cols), low_type),
            shape((rows, cols), low_type),
            shape((rows, heads), f32),
        ),
        in_specs=[whole_spec()] * 9,
        out_specs=tuple([whole_spec()] * 7),
        scratch_shapes=[pltpu.VMEM((rows, 3 * cols), low_type)],
        compiler_params=pltpu.CompilerParams(vmem_limit_bytes=VMEM_BYTES),
        cost_estimate=LARGE,
    )(near, far, norms, weights, bias, place[None, :], place[:, None], segment[None, :], segment[:, None])

def attention_backward_kernel(
    near_ref, far_ref, weights_ref, place_row_ref, place_col_ref, seg_row_ref, seg_col_ref,
    qkv_ref, out_ref, lse_ref,
    keep_ref, send_ref, grads_ref, sums_ref,
    arrived, placed, grad_key, grad_value, moved,
):
    rows = arrived.shape[0]
    half = rows // 2
    cols = out_ref.shape[1]
    heads = cols // HEAD_DIM
    scale = 1.0 / math.sqrt(HEAD_DIM)
    tiles = rows // TILE
    for t in range(tiles):
        source = near_ref if t * TILE < half else far_ref
        part = source[pl.ds(t * TILE % half, TILE), :]
        arrived[pl.ds(t * TILE, TILE), :] = dot(part, weights_ref[:, 3 * cols :]).astype(low_type)
    for t in range(tiles):
        wanted = lax.broadcasted_iota(jnp.int32, (TILE, rows), 0) + t * TILE
        pick = jnp.where(wanted == place_row_ref[...], 1.0, 0.0).astype(low_type)
        placed[pl.ds(t * TILE, TILE), :] = dot(pick, arrived[...]).astype(low_type)
    for h in range(heads):
        lanes = slice(h * HEAD_DIM, (h + 1) * HEAD_DIM)
        key_lanes = slice(cols + h * HEAD_DIM, cols + (h + 1) * HEAD_DIM)
        value_lanes = slice(2 * cols + h * HEAD_DIM, 2 * cols + (h + 1) * HEAD_DIM)
        grad_key[...] = jnp.zeros_like(grad_key)
        grad_value[...] = jnp.zeros_like(grad_value)
        for t in range(tiles):
            here = slice(t * TILE, (t + 1) * TILE)
            query = qkv_ref[here, lanes]
            grad = placed[here, lanes]
            row_total = jnp.sum(grad.astype(f32) * out_ref[here, lanes].astype(f32), axis=1, keepdims=True)
            seg_q = seg_col_ref[here, :]
            lse = lse_ref[here, h : h + 1]
            grad_query = 0.0
            for c in range(t + 1):
                there = slice(c * TILE, (c + 1) * TILE)
                key = qkv_ref[there, key_lanes]
                s = dot_nt(query, key) * scale
                allowed = seg_q == seg_row_ref[:, there]
                if c == t:
                    allowed = allowed & (
                        lax.broadcasted_iota(jnp.int32, (TILE, TILE), 0)
                        >= lax.broadcasted_iota(jnp.int32, (TILE, TILE), 1)
                    )
                p = jnp.where(allowed, jnp.exp(s - lse), 0.0)
                dp = dot_nt(grad, qkv_ref[there, value_lanes])
                ds = (p * (dp - row_total)).astype(low_type)
                grad_query = grad_query + dot(ds, key)
                grad_key[there, :] += dot_tn(ds, query)
                grad_value[there, :] += dot_tn(p.astype(low_type), grad)
            moved[here, lanes] = (grad_query * scale).astype(low_type)
        moved[:, key_lanes] = (grad_key[...] * scale).astype(low_type)
        moved[:, value_lanes] = grad_value[...].astype(low_type)
    sums_ref[...] = jnp.sum(moved[...].astype(f32), axis=0, keepdims=True)
    for t in range(tiles):
        wanted = lax.broadcasted_iota(jnp.int32, (TILE, rows), 1)
        pick = jnp.where(wanted == place_col_ref[pl.ds(t * TILE, TILE), :], 1.0, 0.0).astype(low_type)
        part = dot(pick, moved[...]).astype(low_type)
        grads_ref[pl.ds(t * TILE, TILE), :] = part
        normed = dot_nt(part, weights_ref[:, : 3 * cols])
        if t * TILE < half:
            keep_ref[pl.ds(t * TILE, TILE), :] = normed
        else:
            send_ref[pl.ds(t * TILE - half, TILE), :] = normed.astype(low_type)

def attention_backward(near, far, weights, place, segment, qkv, out, lse):
    rows = 2 * near.shape[0]
    width = near.shape[1]
    cols = weights.shape[1] // 4
    heads = cols // HEAD_DIM
    shape = jax.ShapeDtypeStruct
    return pl.pallas_call(
        attention_backward_kernel,
        out_shape=(
            shape((rows // 2, width), f32),
            shape((rows // 2, width), low_type),
            shape((rows, 3 * cols), low_type),
            shape((1, 3 * cols), f32),
        ),
        in_specs=[whole_spec()] * 10,
        out_specs=tuple([whole_spec()] * 4),
        scratch_shapes=[
            pltpu.VMEM((rows, cols), low_type),
            pltpu.VMEM((rows, cols), low_type),
            pltpu.VMEM((rows, HEAD_DIM), f32),
            pltpu.VMEM((rows, HEAD_DIM), f32),
            pltpu.VMEM((rows, 3 * cols), low_type),
        ],
        compiler_params=pltpu.CompilerParams(vmem_limit_bytes=VMEM_BYTES),
        cost_estimate=LARGE,
    )(near, far, weights, place[None, :], place[:, None], segment[None, :], segment[:, None], qkv, out, lse)

def mlp_kernel(normed_ref, grad_ref, weights_ref, bias_ref, active_ref, grad_up_ref, feed_ref, back_ref, sums_ref):
    rows, width = normed_ref.shape
    cols = bias_ref.shape[1]
    step = TILE
    total = 0.0
    c0 = math.sqrt(2.0 / math.pi)
    for t in range(rows // step):
        here = slice(t * step, (t + 1) * step)
        pre = dot(normed_ref[here, :], weights_ref[:, :cols]) + bias_ref[...]
        square = pre * pre
        bent = jnp.tanh(c0 * (pre + 0.044715 * (square * pre)))
        active_ref[here, :] = (0.5 * pre * (1.0 + bent)).astype(low_type)
        slope = 0.5 * (1.0 + bent) + 0.5 * pre * (1.0 - bent * bent) * (c0 * (1.0 + 0.134145 * square))
        grad = dot(grad_ref[here, :], weights_ref[:, cols:]) * slope
        grad_low = grad.astype(low_type)
        grad_up_ref[here, :] = grad_low
        total = total + jnp.sum(grad_low.astype(f32), axis=0, keepdims=True)
    sums_ref[...] = total
    for t in range(rows // step):
        here = slice(t * step, (t + 1) * step)
        back_ref[here, :] = dot_nt(grad_up_ref[here, :], weights_ref[:, :cols]).astype(back_ref.dtype)
        feed_ref[here, :] = dot_nt(active_ref[here, :], weights_ref[:, cols:]).astype(feed_ref.dtype)

def mlp(normed, grad, weights, bias, kind):
    rows, width = normed.shape
    cols = bias.shape[1]
    shape = jax.ShapeDtypeStruct
    return pl.pallas_call(
        mlp_kernel,
        out_shape=(
            shape((rows, cols), low_type),
            shape((rows, cols), low_type),
            shape((rows, width), kind),
            shape((rows, width), kind),
            shape((1, cols), f32),
        ),
        in_specs=[whole_spec()] * 4,
        out_specs=tuple([whole_spec()] * 5),
        compiler_params=pltpu.CompilerParams(vmem_limit_bytes=VMEM_BYTES),
        cost_estimate=MEDIUM,
    )(normed, grad, weights, bias)


def grads_kernel(counts, *refs):
    out_ref = refs[-1]
    for t in range(out_ref.shape[0] // TILE):
        rows = slice(t * TILE, (t + 1) * TILE)
        start = 0
        place = 0
        for count in counts:
            total = 0.0
            for g in range(count):
                left, right = refs[place + g], refs[place + count + g]
                total = total + dot_tn(left[:, rows], right[...])
            out_ref[rows, start : start + total.shape[1]] = total.astype(out_ref.dtype)
            start = start + total.shape[1]
            place = place + 2 * count


def grads_of(*groups):
    width = groups[0][0][0].shape[1]
    cols = sum(right[0].shape[1] for _, right in groups)
    pieces = [piece for left, right in groups for piece in (*left, *right)]
    return pl.pallas_call(
        functools.partial(grads_kernel, [len(left) for left, _ in groups]),
        out_shape=jax.ShapeDtypeStruct((width, cols), low_type),
        in_specs=[whole_spec()] * len(pieces),
        out_specs=whole_spec(),
        compiler_params=pltpu.CompilerParams(vmem_limit_bytes=VMEM_BYTES),
        cost_estimate=MEDIUM,
    )(*pieces)


def slots_kernel(cols, slot_count, block_ref, *refs):
    outs, held = refs[-1 - slot_count : -1], refs[-1]
    start = 0
    for part in refs[: -1 - slot_count]:
        held[:, start : start + part.shape[1]] = part[...]
        start = start + part.shape[1]
    for s in range(block_ref.shape[0]):
        out = outs[s % slot_count]
        block = block_ref[s]
        lanes = pl.ds(pl.multiple_of(jnp.maximum(block, 0) * cols, cols), cols)
        rows = held[:, lanes]
        out[s // slot_count] = jnp.where(block >= 0, rows, jnp.zeros_like(rows))


def to_slots(block_of, slot_count, cols, *parts):
    count = block_of.shape[0] // slot_count
    rows = parts[0].shape[0]
    width = sum(part.shape[1] for part in parts)
    return pl.pallas_call(
        functools.partial(slots_kernel, cols, slot_count),
        out_shape=tuple(
            [jax.ShapeDtypeStruct((count, rows, cols), low_type) for _ in range(slot_count)]
        ),
        in_specs=[pl.BlockSpec(memory_space=pltpu.SMEM)] + [whole_spec()] * len(parts),
        out_specs=tuple([whole_spec()] * slot_count),
        scratch_shapes=[pltpu.VMEM((rows, width), low_type)],
        compiler_params=pltpu.CompilerParams(vmem_limit_bytes=VMEM_BYTES),
        cost_estimate=SMALL,
    )(block_of, *parts)


def swap(values, axis, bit):
    count = lax.axis_size(axis)
    return lax.ppermute(values, axis, [(i, i ^ bit) for i in range(count)])


def near_order(count):
    found = [0]
    bit = count // 2
    while bit >= 1:
        found = found + [j ^ bit for j in found]
        bit //= 2
    return found


def gather_chips(share):
    bit = lax.axis_size("mp") // 2
    while bit > 1:
        share = jnp.concatenate([share, swap(share, "mp", bit)], axis=0)
        bit //= 2
    return share


def other_core(values):
    return swap(values, "mp", 1)


def scatter_chips(keep, received):
    values = keep + received.astype(f32)
    bit = 2
    while bit < lax.axis_size("mp"):
        half = values.shape[0] // 2
        values = values[:half] + swap(values[half:].astype(low_type), "mp", bit).astype(f32)
        bit *= 2
    return values


def after(values, others):
    return lax.optimization_barrier((values, others))


def together(*values):
    return lax.optimization_barrier(values)


def scatter_grads(values):
    count = lax.axis_size("dp")
    index = lax.axis_index("dp")
    blocks = values.reshape(count, -1, values.shape[-1])
    bit = 1
    width = count
    while bit < count:
        blocks = blocks.reshape(width // 2, 2, -1, values.shape[-1])
        mine = lax.dynamic_index_in_dim(blocks, index // bit % 2, 1, keepdims=False)
        other = lax.dynamic_index_in_dim(blocks, 1 - index // bit % 2, 1, keepdims=False)
        blocks = mine.astype(f32) + swap(other.astype(low_type), "dp", bit).astype(f32)
        bit *= 2
        width //= 2
    return blocks.reshape(-1, values.shape[-1])


def sum_over(values, axis):
    bit = 1
    while bit < lax.axis_size(axis):
        values = values + swap(values, axis, bit)
        bit *= 2
    return values


def gather_columns(share, axis):
    index = lax.axis_index(axis)
    bit = 1
    while bit < lax.axis_size(axis):
        other = swap(share, axis, bit)
        share = jnp.where(
            (index & bit) != 0,
            jnp.concatenate([other, share], axis=-1),
            jnp.concatenate([share, other], axis=-1),
        )
        bit *= 2
    return share


def exchange(rows):
    return lax.all_to_all(rows, "dp", split_axis=0, concat_axis=0, tiled=True)


def on_device(
    tokens,
    cotangent,
    lengths,
    placement_ids,
    block_slot_index,
    matrices,
    norm_vectors,
    head_vectors,
    left_stats,
    right_stats,
    left_roots,
    right_roots,
    norm_state,
    head_state,
):
    data_count = lax.axis_size("dp")
    data_index = lax.axis_index("dp")
    model_count = lax.axis_size("mp")
    model_index = lax.axis_index("mp")
    micro_count, rows_here, model_width = tokens.shape
    piece_rows = rows_here // data_count
    sub_rows = piece_rows // model_count
    own_rows = rows_here // model_count
    blocks = matrices.shape[1]
    local_cols = matrices.shape[2]
    shard_rows = matrices.shape[0]
    ffn_count = (blocks - 4) // 2
    ffn_cols = ffn_count * local_cols

    matrices_low = matrices.astype(low_type)
    shipped_one = matrices_low[:, :4, :].reshape(shard_rows, 4 * local_cols)
    shipped_two = matrices_low[:, 4:, :].reshape(shard_rows, 2 * ffn_cols)
    lanes = 128
    norm_columns = jnp.swapaxes(norm_vectors.astype(low_type), 0, 1)
    shipped_one = jnp.concatenate(
        [shipped_one, jnp.pad(norm_columns, ((0, 0), (0, lanes - norm_columns.shape[1])))], axis=1
    )
    gathered = lax.all_gather(shipped_one, "dp", axis=0, tiled=True)
    order = jnp.arange(rows_here)
    earlier = (order[:, None] < order[None, :]).astype(low_type)
    device_ids = jnp.arange(data_count)[:, None]
    near = near_order(model_count)
    slots_mine = []
    positions = []
    for micro in range(micro_count):
        dest_all = placement_ids[micro].reshape(data_count, rows_here)
        dest_mine = lax.dynamic_slice_in_dim(dest_all, data_index, 1, 0)
        target = dest_mine // rows_here
        to_each = target == device_ids
        to_me = (dest_all // rows_here) == data_index
        rank_both = dot(jnp.concatenate([to_each, to_me]).astype(low_type), earlier).astype(
            jnp.int32
        )
        rank_out = jnp.sum(jnp.where(to_each, rank_both[:data_count], 0), axis=0)
        slots_mine.append((rank_out, target[0]))
        rank_in = jnp.where(to_me, rank_both[data_count:], -1)
        place = jnp.sum(
            jnp.where(
                rank_in[:, None, :] == jnp.arange(piece_rows)[None, :, None],
                (dest_all - data_index * rows_here)[:, None, :],
                0,
            ),
            axis=2,
        )
        place = place.reshape(data_count, model_count, sub_rows).transpose(1, 0, 2)
        place = place.reshape(model_count, own_rows)[model_index ^ jnp.array(near)]
        positions.append(place.reshape(rows_here))

    def send_rows(micro, *given):
        rank, target = slots_mine[micro]
        here = (rank // sub_rows) == model_index
        slot = jnp.where(here, target * sub_rows + rank % sub_rows, -1)
        pick = (slot[None, :] == jnp.arange(own_rows)[:, None]).astype(low_type)
        picked = [dot(pick, rows[micro]).astype(low_type) for rows in given]
        picked = [rows.reshape(data_count, sub_rows, model_width) for rows in picked]
        got = exchange(jnp.concatenate(picked, axis=1))
        got = got.reshape(data_count, len(given), sub_rows, model_width)
        return [got[:, i].reshape(own_rows, model_width).astype(f32) for i in range(len(given))]

    def exchange_back(own):
        sent = [rows.reshape(data_count, sub_rows, model_width) for rows in own]
        return exchange(jnp.concatenate(sent, axis=1))

    def return_rows(back, which):
        back = back.reshape(data_count, len(which), sub_rows, model_width)
        back = jnp.swapaxes(back, 0, 1).reshape(1, len(which) * own_rows, model_width)
        bit = model_count // 2
        while bit >= 1:
            back = jnp.concatenate([back, swap(back, "mp", bit)], axis=0)
            bit //= 2
        returned = []
        for i, micro in enumerate(which):
            rank, target = slots_mine[micro]
            block = jnp.sum(
                jnp.where(
                    ((rank // sub_rows) ^ model_index) == jnp.array(near)[:, None],
                    jnp.arange(model_count)[:, None],
                    0,
                ),
                axis=0,
            )
            slot = block * own_rows + target * sub_rows + rank % sub_rows
            pick = (slot[:, None] == order[None, :]).astype(low_type)
            rows = back[:, i * own_rows : (i + 1) * own_rows]
            returned.append(dot(pick, rows.reshape(rows_here, model_width)).astype(low_type))
        return jnp.stack(returned)

    micros = range(micro_count)
    bounds = [jnp.cumsum(lengths[i, 0]) for i in micros]
    segments = [
        jnp.sum((order[:, None] >= bounds[i][None, :]).astype(jnp.int32), axis=1) for i in micros
    ]
    bias_qkv = jnp.concatenate(
        [head_vectors[0], jnp.zeros((local_cols,), f32), head_vectors[1]]
    )[None]
    bias_up = head_vectors[2:].reshape(1, -1)
    half = rows_here // 2

    def arrived(i):
        rows, grads = send_rows(i, tokens, cotangent)
        keep = (positions[i][:own_rows] < bounds[i][-2]).astype(f32)[:, None]
        return rows, grads * keep

    def attend(i, near, far):
        return attention_forward(
            near, far, norms[:2], weights_one, bias_qkv, positions[i], segments[i]
        )

    def second_share(hidden):
        return layer_norm(hidden, norms[3], norms[4]).astype(low_type)

    def feed_forward(near, far, grad_near, grad_far):
        far_parts = mlp(far, grad_far, weights_two, bias_up, low_type)
        near_parts = mlp(near, grad_near, weights_two, bias_up, f32)
        active, grad_up, (feed_keep, feed_send), (back_keep, back_send), sums = zip(
            near_parts, far_parts
        )
        return active, grad_up, feed_keep, feed_send, back_keep, back_send, sum(sums)

    def second_back(i, hidden, grad_normed):
        hidden_part, gain_rows = norm_back(hidden, norms[3], grad_normed)
        grad_hidden = grad_out[i] + hidden_part
        sums = [
            jnp.sum(grad_hidden, axis=0),
            jnp.sum(gain_rows, axis=0),
            jnp.sum(grad_normed, axis=0),
            jnp.sum(grad_out[i], axis=0),
        ]
        return grad_hidden, grad_hidden.astype(low_type), jnp.stack(sums)

    def attend_back(i, near, far, kept):
        _, qkv, out, lse = kept
        return attention_backward(
            near, far, weights_one, positions[i], segments[i], qkv, out, lse
        )

    def first_back(i, grad_hidden, grad_normed):
        rows_part, gain_rows = norm_back(rows_own[i], norms[0], grad_normed)
        sums = [jnp.sum(gain_rows, axis=0), jnp.sum(grad_normed, axis=0)]
        return (grad_hidden + rows_part).astype(low_type), jnp.stack(sums)

    rows_0, grad_0 = arrived(0)
    rows_1, grad_1 = arrived(1)
    x_0 = gather_chips(rows_0.astype(low_type))
    g_0 = gather_chips(grad_0.astype(low_type))
    x_0, g_0, rows_1, grad_1 = together(x_0, g_0, rows_1, grad_1)
    rows_own = (rows_0, rows_1)
    grad_out = (grad_0, grad_1)
    xf_0, gf_0, gathered, shipped_two = together(
        other_core(x_0), other_core(g_0), gathered, shipped_two
    )
    weights_one = gathered[:, : 4 * local_cols]
    norms = jnp.swapaxes(gathered[:, 4 * local_cols :], 0, 1)[:6].astype(f32)
    weights_two = lax.all_gather(shipped_two, "dp", axis=0, tiled=True)

    keep_0, send_0, normed_0, *kept_0 = attend(0, x_0, xf_0)
    x_1 = gather_chips(rows_1.astype(low_type))
    g_1 = gather_chips(grad_1.astype(low_type))
    keep_0, send_0, x_1, g_1 = together(keep_0, send_0, x_1, g_1)
    core_0, xf_1 = together(other_core(send_0), other_core(x_1))
    keep_1, send_1, normed_1, *kept_1 = attend(1, x_1, xf_1)
    branch_0 = scatter_chips(keep_0, core_0)
    keep_1, send_1, branch_0, g_1 = together(keep_1, send_1, branch_0, g_1)
    core_1 = other_core(send_1)
    gf_1 = other_core(g_1)
    hidden_0 = rows_0 + branch_0 + norms[2]
    z_0 = second_share(hidden_0)
    z_0, core_1, gf_1 = together(z_0, core_1, gf_1)
    branch_1 = scatter_chips(keep_1, core_1)
    z_0 = gather_chips(z_0)
    z_0, branch_1 = together(z_0, branch_1)
    hidden_1 = rows_1 + branch_1 + norms[2]
    z_1, zf_0, weights_two = together(second_share(hidden_1), other_core(z_0), weights_two)

    active_0, grad_up_0, feed_keep_0, feed_0, keep_0, send_0, up_sums_0 = feed_forward(
        z_0, zf_0, g_0, gf_0
    )
    feed_0 = other_core(feed_0)
    core_0 = other_core(send_0)
    z_1 = gather_chips(z_1)
    grad_up_0, feed_0, core_0, z_1 = together(grad_up_0, feed_0, core_0, z_1)
    zf_1, core_0, feed_0 = together(other_core(z_1), core_0, feed_0)
    active_1, grad_up_1, feed_keep_1, feed_1, keep_1, send_1, up_sums_1 = feed_forward(
        z_1, zf_1, g_1, gf_1
    )
    core_1 = other_core(send_1)
    back_0 = scatter_chips(keep_0, core_0)
    feed_0 = scatter_chips(feed_keep_0, feed_0)
    grad_up_1, core_1, back_0, feed_0, feed_1 = together(
        grad_up_1, core_1, back_0, feed_0, feed_1
    )
    hidden_grad_0, h_0, second_sums_0 = second_back(0, hidden_0, back_0)
    h_0, core_1, grad_up_1, feed_1 = together(h_0, core_1, grad_up_1, feed_1)
    grads_two = grads_of(
        ([z_0, zf_0, z_1, zf_1], [*grad_up_0, *grad_up_1]),
        ([g_0, gf_0, g_1, gf_1], [*active_0, *active_1]),
    )
    back_1 = scatter_chips(keep_1, core_1)
    h_0 = gather_chips(h_0)
    feed_1 = other_core(feed_1)
    grads_two, back_1, h_0, feed_1 = together(grads_two, back_1, h_0, feed_1)
    summed_two = lax.psum_scatter(grads_two, "dp", scatter_dimension=0, tiled=True)
    hidden_grad_1, h_1, second_sums_1 = second_back(1, hidden_1, back_1)
    hf_0, h_1, feed_1 = together(other_core(h_0), h_1, feed_1)

    keep_0, send_0, grad_qkv_0, sums_0 = attend_back(0, h_0, hf_0, kept_0)
    h_1 = gather_chips(h_1)
    feed_1 = scatter_chips(feed_keep_1, feed_1)
    keep_0, send_0, h_1, feed_1, feed_0 = together(keep_0, send_0, h_1, feed_1, feed_0)
    outputs_back = exchange_back(
        [
            (hidden_0 + feed_0 + norms[5]).astype(low_type),
            (hidden_1 + feed_1 + norms[5]).astype(low_type),
        ]
    )
    core_0, hf_1 = together(other_core(send_0), other_core(h_1))
    keep_1, send_1, grad_qkv_1, sums_1 = attend_back(1, h_1, hf_1, kept_1)
    normed_back_0 = scatter_chips(keep_0, core_0)
    keep_1, send_1, normed_back_0, outputs_back = together(
        keep_1, send_1, normed_back_0, outputs_back
    )
    input_0, first_sums_0 = first_back(0, hidden_grad_0, normed_back_0)
    input_0, core_1 = together(input_0, other_core(send_1))
    inputs_back_0 = exchange_back([input_0])
    grads_one = grads_of(
        ([normed_0, normed_1], [grad_qkv_0, grad_qkv_1]),
        (
            [h_0, hf_0, h_1, hf_1],
            [kept[0][rows] for kept in (kept_0, kept_1) for rows in (slice(0, half), slice(half, rows_here))],
        ),
    )
    normed_back_1 = scatter_chips(keep_1, core_1)
    grads_one, normed_back_1, inputs_back_0 = together(grads_one, normed_back_1, inputs_back_0)
    input_1, first_sums_1 = first_back(1, hidden_grad_1, normed_back_1)
    summed_one = [
        scatter_grads(grads_one[:, h * 2 * local_cols : (h + 1) * 2 * local_cols])
        for h in range(2)
    ]
    norm_grads_own = jnp.concatenate(
        [first_sums_0 + first_sums_1, second_sums_0 + second_sums_1], axis=0
    )
    qkv_sums = sums_0 + sums_1
    up_sums = [up_sums_0, up_sums_1]

    head_own = jnp.concatenate(
        [
            qkv_sums[:, :local_cols],
            qkv_sums[:, 2 * local_cols :],
            sum(up_sums).reshape(ffn_count, local_cols),
        ],
        axis=0,
    )
    vectors = jnp.concatenate([sum_over(norm_grads_own, "mp"), head_own], axis=1)
    vectors = sum_over(vectors, "dp")
    norm_all = vectors[:, :model_width]
    head_total = vectors[:, model_width:]
    norm_cols = norm_vectors.shape[1]
    norm_total = lax.dynamic_slice_in_dim(norm_all, data_index * norm_cols, norm_cols, 1)

    slot_count = left_stats.shape[0]
    all_slots = slot_count * data_count
    slot_match = block_slot_index[None, :] == jnp.arange(all_slots)[:, None]
    filled = jnp.any(slot_match, axis=1)
    block_of = jnp.sum(jnp.where(slot_match, jnp.arange(blocks)[None, :], 0), axis=1)
    summed = [part.astype(low_type) for part in (*summed_one, summed_two)]
    owned = [
        exchange(rows).reshape(model_width, local_cols)
        for rows in to_slots(jnp.where(filled, block_of, -1), slot_count, local_cols, *summed)
    ]
    owned, input_1 = after(owned, input_1)
    inputs_back_1 = exchange_back([input_1])
    outputs_given = return_rows(outputs_back, micros)
    inputs_given = jnp.concatenate(
        [return_rows(inputs_back_0, [0]), return_rows(inputs_back_1, [1])], axis=0
    )
    whole = [gather_columns(owned[s], "mp") for s in range(slot_count)]
    slot_match_own = lax.dynamic_slice_in_dim(slot_match, data_index * slot_count, slot_count, 0)
    weights_all = jnp.concatenate([weights_one, weights_two], axis=1)

    row_total_count = left_stats.shape[1]
    lefts, rights, directions, squares, owned_weights = [], [], [], [], []
    for s in range(slot_count):
        grads = whole[s]
        my_rows = lax.dynamic_slice_in_dim(
            grads, model_index * row_total_count, row_total_count, 0
        )
        lefts.append(stat_decay * left_stats[s] + dot_nt(my_rows, grads))
        rights.append(stat_decay * right_stats[s] + dot_tn(owned[s], grads))
        halfway = dot_nt(grads.astype(f32), right_roots[s])
        direction = dot(left_roots[s], halfway)
        directions.append(direction)
        squares.append(jnp.sum(direction * direction))
        chosen = 0.0
        for b in range(blocks):
            chosen = chosen + jnp.where(
                slot_match_own[s, b],
                weights_all[:, b * local_cols : (b + 1) * local_cols].astype(f32),
                0.0,
            )
        owned_weights.append(chosen)
    square_total = sum_over(jnp.stack(squares).reshape(1, slot_count), "mp")[0]
    factor = lax.rsqrt(square_total / (model_width * model_width) + mean_eps)
    updated_blocks = jnp.stack(
        [
            owned_weights[s] - matrix_rate * factor[s] * directions[s]
            for s in range(slot_count)
        ],
        axis=1,
    )
    owned_grads = jnp.stack(owned, axis=1).astype(f32)
    new_norm_state = stat_decay * norm_state + norm_total * norm_total
    new_norm_vectors = norm_vectors - vector_rate * norm_total / (
        jnp.sqrt(new_norm_state) + diag_eps
    )
    new_head_state = stat_decay * head_state + head_total * head_total
    new_head_vectors = head_vectors - vector_rate * head_total / (
        jnp.sqrt(new_head_state) + diag_eps
    )
    return (
        outputs_given,
        inputs_given,
        owned_grads,
        jnp.stack(lefts),
        jnp.stack(rights),
        updated_blocks,
        norm_total,
        new_norm_state,
        new_norm_vectors,
        head_total,
        new_head_state,
        new_head_vectors,
    )


def solution(mesh):
    placed = (
        P(None, "dp", None),
        P(None, "dp", None),
        P(None, "dp", None),
        P(),
        P(),
        P("dp", None, "mp"),
        P(None, "dp"),
        P(None, "mp"),
        P("dp", "mp", None),
        P("dp", "mp", None),
        P("dp", None, None),
        P("dp", "mp", None),
        P(None, "dp"),
        P(None, "mp"),
    )
    return jax.shard_map(
        on_device,
        mesh=mesh,
        in_specs=placed,
        out_specs=(
            P(None, "dp", None),
            P(None, "dp", None),
            P(None, "dp", "mp"),
            P("dp", "mp", None),
            P("dp", "mp", None),
            P(None, "dp", "mp"),
            P(None, "dp"),
            P(None, "dp"),
            P(None, "dp"),
            P(None, "mp"),
            P(None, "mp"),
            P(None, "mp"),
        ),
        check_vma=False,
    )
```

time: 795 us -> 689 us (0.87)
  Pallas kernels: 0 us -> 161 us
  matrix products: 200 us -> 43.3 us
  waiting for transfers between devices: 307 us -> 239 us
  starting transfers between devices: 100 us -> 67.1 us
    pallas_call x0 -> x11, Pallas kernels: none -> 161 us  [the longest x2 50.9 us: attention_backward(): pl.pallas_call(attention_backward_kernel, out_shape=(shape((rows // 2, wi...]
    unnamed x6 -> x3, waiting for transfers between devices: 89.3 us -> 0.05 us
    dot_general x10 -> x0, matrix products: 50.9 us -> none  [the longest x2 16.7 us: on_device(): jnp.einsum('qhd,khd->hqk', grad_attended, value_heads, preferred_element_...]
    all_to_all x9 -> x7, waiting for transfers between devices: 48.5 us -> 94.3 us  [exchange(): return lax.all_to_all(rows, 'dp', split_axis=0, concat_axis=0, tiled=True)]
    dot_general x20 -> x12, matrix products: 77.2 us -> 35.4 us  [dot(): lax.dot_general(left, right, (((1,), (0,)), ((), ())), preferred_element_...]
    concatenate x3 -> x22, other arithmetic: 4.88 us -> 30.6 us  [the longest x8 12.4 us: gather_chips(): share = jnp.concatenate([share, swap(share, 'mp', bit)], axis=0)]
    ppermute x79 -> x55, waiting for transfers between devices: 170 us -> 144 us  [swap(): return lax.ppermute(values, axis, [(i, i ^ bit) for i in range(count)])]
    convert_element_type x22 -> x17, other arithmetic: 36.7 us -> 12.4 us  [the longest x2 2.4 us: first_back(): return ((grad_hidden + rows_part).astype(low_type), jnp.stack(sums))]
  transfers between devices with their start and end apart: 92 -> 65, of which waited for: 31 -> 26; matrix products, arithmetic and copies ran while one was open for 34% -> 23% of each run, Pallas kernels for 0% -> 24%
where the time goes in v2:
time: 689 us; the launch traced here: 680 us
  waiting for transfers between devices  239 us (35%)
  Pallas kernels  161 us (23%)
  other arithmetic  110 us (16%)
  starting transfers between devices  67.1 us (10%)
  matrix products  43.3 us (6%)
  local copies, waits for them, and re-layouts  43.2 us (6%)
  between operations  17.2 us (2%)
    ppermute x55, waiting for transfers between devices, swap(): return lax.ppermute(values, axis, [(i, i ^ bit) for i in range(count)])  144 us
    all_to_all x7, waiting for transfers between devices, exchange(): return lax.all_to_all(rows, 'dp', split_axis=0, concat_axis=0, tiled=True)  94.3 us
    pallas_call x2, Pallas kernels, attention_backward(): pl.pallas_call(attention_backward_kernel, out_shape=(shape((rows // 2, wi...  50.9 us
    pallas_call x2, Pallas kernels, attention_forward(): pl.pallas_call(attention_forward_kernel, out_shape=(shape((rows // 2, wid...  43.4 us
    pallas_call x4, Pallas kernels, mlp(): pl.pallas_call(mlp_kernel, out_shape=(shape((rows, cols), low_type), shap...  37.1 us
    ppermute x55, starting transfers between devices, swap(): return lax.ppermute(values, axis, [(i, i ^ bit) for i in range(count)])  36.6 us
    dot_general x12, matrix products, dot(): lax.dot_general(left, right, (((1,), (0,)), ((), ())), preferred_element_...  35.4 us
    all_to_all x7, starting transfers between devices, exchange(): return lax.all_to_all(rows, 'dp', split_axis=0, concat_axis=0, tiled=True)  30.4 us
  transfers between devices with their start and end apart: 65, of which 26 were waited for; matrix products, arithmetic and copies ran while one was open for 23% of the time, Pallas kernels for 24%

profile of v2, /device:TPU:0, one launch (start us, length us, event | category | flops | bytes accessed | tf_op | source)
XLA Modules:
  0.0 680.2 jit_solution(16661660887790640272)
XLA Ops:
  13.8 7.3 %all-to-all-start = ((bf16[8,64,1024]{2,1,0:T(8,128)(2,1)}), bf16[8,64,1024]{2,1,0:T(8,128)(2,1)S(1)}, u32[]{:S(2)}, u32[]{:S(2)}) async-start(bf16[8,64,1024]{2,1,0:T(8,128)(2,1)} %pad_maximum_fusion.9), calls=%async_computation | async-start | bytes 2097152 | tf_op jit(solution)/shard_map/all_to_all | solution.py:449
  28.7 27.7 %all-to-all-done = bf16[8,64,1024]{2,1,0:T(8,128)(2,1)S(1)} async-done(((bf16[8,64,1024]{2,1,0:T(8,128)(2,1)}), bf16[8,64,1024]{2,1,0:T(8,128)(2,1)S(1)}, u32[]{:S(2)}, u32[]{:S(2)}) %all-to-all-start) | async-done | bytes 1048608 | tf_op jit(solution)/shard_map/all_to_all | solution.py:449
  69.3 34.6 %all-to-all-done.1 = bf16[8,64,1024]{2,1,0:T(8,128)(2,1)S(1)} async-done(((bf16[8,64,1024]{2,1,0:T(8,128)(2,1)}), bf16[8,64,1024]{2,1,0:T(8,128)(2,1)S(1)}, u32[]{:S(2)}, u32[]{:S(2)}) %all-to-all-start.1) | async-done | bytes 1048608 | tf_op jit(solution)/shard_map/all_to_all | solution.py:449
  117.8 6.9 %collective-permute-done.4 = bf16[256,1024]{1,0:T(8,128)(2,1)} collective-permute-done((bf16[256,1024]{1,0:T(8,128)(2,1)S(1)}, bf16[256,1024]{1,0:T(8,128)(2,1)}, u32[]{:S(2)}, u32[]{:S(2)}) %collective-permute-start.4) | collective-permute-done | bytes 524320 | tf_op jit(solution)/shard_map/ppermute | solution.py:368
  126.7 8.2 %collective-permute-done.5 = bf16[256,1024]{1,0:T(8,128)(2,1)} collective-permute-done((bf16[256,1024]{1,0:T(8,128)(2,1)S(1)}, bf16[256,1024]{1,0:T(8,128)(2,1)}, u32[]{:S(2)}, u32[]{:S(2)}) %collective-permute-start.5) | collective-permute-done | bytes 524320 | tf_op jit(solution)/shard_map/ppermute | solution.py:368
  142.0 21.8 %shard_map.283 = (f32[512,1024]{1,0:T(8,128)}, bf16[512,1024]{1,0:T(8,128)(2,1)}, bf16[1024,1024]{1,0:T(8,128)(2,1)}, bf16[1024,256]{1,0:T(8,128)(2,1)}, bf16[10...) custom-call(bf16[512,1024]{1,0:T(8,128)(2,1)} %pad_maximum_fusion.10.near_ref, ...), custom_call_target="tpu_custom_call" | custom-call | flops 20000000000 | bytes 1000000 | tf_op jit(solution)/shard_map/pallas_call | solution.py:152
  170.3 21.5 %shard_map.284 = (f32[512,1024]{1,0:T(8,128)}, bf16[512,1024]{1,0:T(8,128)(2,1)}, bf16[1024,1024]{1,0:T(8,128)(2,1)}, bf16[1024,256]{1,0:T(8,128)(2,1)}, bf16[10...) custom-call(bf16[512,1024]{1,0:T(8,128)(2,1)} %pad_maximum_fusion.13.near_ref, ...), custom_call_target="tpu_custom_call" | custom-call | flops 20000000000 | bytes 1000000 | tf_op jit(solution)/shard_map/pallas_call | solution.py:152
  202.1 10.8 %collective-permute-done.11 = bf16[256,1024]{1,0:T(8,128)(2,1)S(1)} collective-permute-done((bf16[256,1024]{1,0:T(8,128)(2,1)S(1)}, bf16[256,1024]{1,0:T(8,128)(2,1)S(1)}, u32[]{:S(2)}, u32[]{:S(2)}) %collective-permute-start.11) | collective-permute-done | bytes 524320 | tf_op jit(solution)/shard_map/ppermute | solution.py:368
  213.0 10.4 %collective-permute-done.12 = bf16[256,1024]{1,0:T(8,128)(2,1)S(1)} collective-permute-done((bf16[256,1024]{1,0:T(8,128)(2,1)S(1)}, bf16[256,1024]{1,0:T(8,128)(2,1)S(1)}, u32[]{:S(2)}, u32[]{:S(2)}) %collective-permute-start.12) | collective-permute-done | bytes 524320 | tf_op jit(solution)/shard_map/ppermute | solution.py:368
  226.9 9.0 %shard_map.286 = (bf16[512,1024]{1,0:T(8,128)(2,1)}, bf16[512,1024]{1,0:T(8,128)(2,1)}, bf16[512,1024]{1,0:T(8,128)(2,1)}, bf16[512,1024]{1,0:T(8,128)(2,1)}, f32[1,1024]{1,0:T(1,128)}) custom-call(bf16[512,1024]{1,0:T(8,128)(2,1)} %collective-permute-done.13.normed_ref.refs_1_, bf16[512,1024]{1,0:T(8,128)(2,1)} %collective-permute-done.3.grad_ref.refs_9_, ...), custom_call_target="tpu_custom_call" | custom-call | flops 11000000512 | bytes 1000000 | tf_op jit(solution)/shard_map/pallas_call | solution.py:289
  236.5 9.5 %shard_map.285 = (bf16[512,1024]{1,0:T(8,128)(2,1)}, bf16[512,1024]{1,0:T(8,128)(2,1)}, f32[512,1024]{1,0:T(8,128)}, f32[512,1024]{1,0:T(8,128)}, f32[1,1024]{1,0:T(1,128)}) custom-call(bf16[512,1024]{1,0:T(8,128)(2,1)} %copy-done.42, bf16[512,1024]{1,0:T(8,128)(2,1)} %pad_maximum_fusion.11.grad_ref.refs_8_, ...), custom_call_target="tpu_custom_call" | custom-call | flops 11000000512 | bytes 1000000 | tf_op jit(solution)/shard_map/pallas_call | solution.py:289
  258.8 9.0 %shard_map.288 = (bf16[512,1024]{1,0:T(8,128)(2,1)}, bf16[512,1024]{1,0:T(8,128)(2,1)}, bf16[512,1024]{1,0:T(8,128)(2,1)}, bf16[512,1024]{1,0:T(8,128)(2,1)}, f32[1,1024]{1,0:T(1,128)}) custom-call(bf16[512,1024]{1,0:T(8,128)(2,1)} %collective-permute-done.17.normed_ref.refs_3_, bf16[512,1024]{1,0:T(8,128)(2,1)} %copy-done.70, ...), custom_call_target="tpu_custom_call" | custom-call | flops 11000000512 | bytes 1000000 | tf_op jit(solution)/shard_map/pallas_call | solution.py:289
  267.9 9.5 %shard_map.287 = (bf16[512,1024]{1,0:T(8,128)(2,1)}, bf16[512,1024]{1,0:T(8,128)(2,1)}, f32[512,1024]{1,0:T(8,128)}, f32[512,1024]{1,0:T(8,128)}, f32[1,1024]{1,0:T(1,128)}) custom-call(bf16[512,1024]{1,0:T(8,128)(2,1)} %pad_maximum_fusion.16.normed_ref.refs_2_, bf16[512,1024]{1,0:T(8,128)(2,1)} %pad_maximum_fusion.14.grad_ref.refs_10_, ...), custom_call_target="tpu_custom_call" | custom-call | flops 11000000512 | bytes 1000000 | tf_op jit(solution)/shard_map/pallas_call | solution.py:289
  292.9 16.7 %shard_map.289 = bf16[1024,2048]{1,0:T(8,128)(2,1)} custom-call(bf16[512,1024]{1,0:T(8,128)(2,1)} %copy-done.42, bf16[512,1024]{1,0:T(8,128)(2,1)} %collective-permute-done.13.normed_ref.refs_1_, bf16[512,1024]{1,0:T(8,128)(2,1)} %pad_maximum_fusion.16.normed_ref.refs_2_, bf16[512,1024]{1,0:T(8,128)(2,1)} %collective-permute-done.17.normed_ref.refs_3_, ...), custom_call_target="tpu_custom_call" | custom-call | flops 11000000512 | bytes 1000000 | tf_op jit(solution)/shard_map/pallas_call | solution.py:325
  309.6 6.3 collective-permute-done.22
  326.2 25.5 %shard_map.290 = (f32[512,1024]{1,0:T(8,128)}, bf16[512,1024]{1,0:T(8,128)(2,1)}, bf16[1024,768]{1,0:T(8,128)(2,1)}, f32[1,768]{1,0:T(1,128)}) custom-call(bf16[512,1024]{1,0:T(8,128)(2,1)} %copy-done.43, bf16[512,1024]{1,0:T(8,128)(2,1)} %copy-done.71, bf16[1024,1024]{1,0:T(8,128)(2,1)} %slice.387.weights_ref, s32[1,1024]{1,0:T(1,128)} %bitcast.336, ...), custom_call_target="tpu_custom_call" | custom-call | flops 20000000000 | bytes 1000000 | tf_op jit(solution)/shard_map/pallas_call | solution.py:241
  366.0 25.5 %shard_map.291 = (f32[512,1024]{1,0:T(8,128)}, bf16[512,1024]{1,0:T(8,128)(2,1)}, bf16[1024,768]{1,0:T(8,128)(2,1)}, f32[1,768]{1,0:T(1,128)}) custom-call(bf16[512,1024]{1,0:T(8,128)(2,1)} %pad_maximum_fusion.18.near_ref.refs_6_, bf16[512,1024]{1,0:T(8,128)(2,1)} %collective-permute-done.28.far_ref.refs_7_, bf16[1024,1024]{1,0:T(8,128)(2,1)} %slice.387.weights_ref, ...), custom_call_target="tpu_custom_call" | custom-call | flops 20000000000 | bytes 1000000 | tf_op jit(solution)/shard_map/pallas_call | solution.py:241
  392.6 21.1 %all-to-all-done.2 = bf16[8,64,1024]{2,1,0:T(8,128)(2,1)} async-done(((bf16[8,64,1024]{2,1,0:T(8,128)(2,1)}), bf16[8,64,1024]{2,1,0:T(8,128)(2,1)}, u32[]{:S(2)}, u32[]{:S(2)}) %all-to-all-start.2) | async-done | bytes 1048608 | tf_op jit(solution)/shard_map/all_to_all | solution.py:449
  426.1 10.6 %shard_map.292 = bf16[1024,1024]{1,0:T(8,128)(2,1)} custom-call(bf16[1024,1024]{1,0:T(8,128)(2,1)} %get-tuple-element.216.refs_0_, bf16[1024,1024]{1,0:T(8,128)(2,1)} %get-tuple-element.217.refs_1_, bf16[1024,768]{1,0:T(8,128)(2,1)} %get-tuple-element.218.refs_2_, bf16[1024,768]{1,0:T(8,128)(2,1)} %get-tuple-element.219.refs_3_, ...), custom_call_target="tpu_custom_call" | custom-call | flops 11000000512 | bytes 1000000 | tf_op jit(solution)/shard_map/pallas_call | solution.py:325
  445.4 7.6 %collective-permute-done.33 = bf16[256,1024]{1,0:T(8,128)(2,1)S(1)} collective-permute-done((bf16[256,1024]{1,0:T(8,128)(2,1)S(1)}, bf16[256,1024]{1,0:T(8,128)(2,1)S(1)}, u32[]{:S(2)}, u32[]{:S(2)}) %collective-permute-start.33) | collective-permute-done | bytes 524320 | tf_op jit(solution)/shard_map/ppermute | solution.py:368
  461.4 10.7 %collective-permute-done.52 = f32[6,1280]{1,0:T(8,128)S(1)} collective-permute-done((f32[6,1280]{1,0:T(8,128)S(1)}, f32[6,1280]{1,0:T(8,128)S(1)}, u32[]{:S(2)}, u32[]{:S(2)}) %collective-permute-start.52) | collective-permute-done | bytes 30752 | tf_op jit(solution)/shard_map/ppermute | solution.py:368
  474.5 7.9 %collective-permute-done.36 = bf16[4,128,512]{2,1,0:T(8,128)(2,1)S(1)} collective-permute-done((bf16[4,128,512]{2,1,0:T(8,128)(2,1)S(1)}, bf16[4,128,512]{2,1,0:T(8,128)(2,1)S(1)}, u32[]{:S(2)}, u32[]{:S(2)}) %collective-permute-start.36) | collective-permute-done | bytes 524320 | tf_op jit(solution)/shard_map/ppermute | solution.py:368
  483.6 9.3 %collective-permute-done.37 = bf16[2,128,512]{2,1,0:T(8,128)(2,1)S(1)} collective-permute-done((bf16[2,128,512]{2,1,0:T(8,128)(2,1)S(1)}, bf16[2,128,512]{2,1,0:T(8,128)(2,1)S(1)}, u32[]{:S(2)}, u32[]{:S(2)}) %collective-permute-start.37) | collective-permute-done | bytes 262176 | tf_op jit(solution)/shard_map/ppermute | solution.py:368
  493.7 5.9 collective-permute-done.38
  511.6 10.9 %collective-permute-done.54 = f32[6,1280]{1,0:T(8,128)S(1)} collective-permute-done((f32[6,1280]{1,0:T(8,128)S(1)}, f32[6,1280]{1,0:T(8,128)S(1)}, u32[]{:S(2)}, u32[]{:S(2)}) %collective-permute-start.54) | collective-permute-done | bytes 30752 | tf_op jit(solution)/shard_map/ppermute | solution.py:368
  536.4 7.4 %all-to-all-done.5 = bf16[8,128,256]{2,1,0:T(8,128)(2,1)S(1)} async-done(((bf16[8,128,256]{2,1,0:T(8,128)(2,1)}), bf16[8,128,256]{2,1,0:T(8,128)(2,1)S(1)}, u32[]{:S(2)}, u32[]{:S(2)}) %all-to-all-start.5) | async-done | bytes 524320 | tf_op jit(solution)/shard_map/all_to_all | solution.py:449
  575.0 17.3 %collective-permute-done.42 = bf16[1,256,1024]{2,1,0:T(8,128)(2,1)S(1)} collective-permute-done((bf16[1,256,1024]{2,1,0:T(8,128)(2,1)S(1)}, bf16[1,256,1024]{2,1,0:T(8,128)(2,1)S(1)}, u32[]{:S(2)}, u32[]{:S(2)}) %collective-permute-start.42) | collective-permute-done | bytes 524320 | tf_op jit(solution)/shard_map/ppermute | solution.py:368
  599.4 14.4 %collective-permute-done.45 = bf16[1024,512]{1,0:T(8,128)(2,1)S(1)} collective-permute-done((bf16[1024,512]{1,0:T(8,128)(2,1)S(1)}, bf16[1024,512]{1,0:T(8,128)(2,1)S(1)}, u32[]{:S(2)}, u32[]{:S(2)}) %collective-permute-start.45) | collective-permute-done | bytes 1048608 | tf_op jit(solution)/shard_map/ppermute | solution.py:368
  619.0 6.7 multiply_reduce_fusion.4
  625.7 6.1 multiply_reduce_fusion.5
  646.6 8.7 %fusion.75 = f32[1024,1,256]{2,0,1:T(8,128)S(1)} fusion(f32[256,1024]{0,1:T(8,128)S(1)} %copy.108, f32[]{:T(128)} %bitcast.100, pred[]{:T(512)} %bitcast.92, pred[]{:T(512)} %bitcast.91, pred[]{:T(512)} %bitcast.90, pred[]{:T(512)} %bitcast.89, pred[]{:T(512)} %bitcast.88, pred[]{:T(512)} %bitcast.87, pred[]{:T(512)} %bitcast.86, pred[]{:T(512)} %bitcast.85, ...), kind=kLoop, calls=%fused_computation.129 | loop fusion | flops 9699328 | bytes 8388624 | tf_op jit(solution)/shard_map/stack | solution.py:775
  655.3 8.6 %fusion.88 = f32[1024,1,256]{2,0,1:T(8,128)S(1)} fusion(f32[256,1024]{0,1:T(8,128)S(1)} %copy.109, f32[]{:T(128)} %bitcast.115, pred[]{:T(512)} %bitcast.114, pred[]{:T(512)} %bitcast.113, pred[]{:T(512)} %bitcast.112, pred[]{:T(512)} %bitcast.111, pred[]{:T(512)} %bitcast.110, pred[]{:T(512)} %bitcast.109, pred[]{:T(512)} %bitcast.108, pred[]{:T(512)} %bitcast.107, ...), kind=kLoop, calls=%fused_computation.142 | loop fusion | flops 9699328 | bytes 8388624 | tf_op jit(solution)/shard_map/stack | solution.py:775
  (483 shorter events, 249.9 us)
Async XLA Ops:
  13.8 42.6 %all-to-all-start = ((bf16[8,64,1024]{2,1,0:T(8,128)(2,1)}), bf16[8,64,1024]{2,1,0:T(8,128)(2,1)S(1)}, u32[]{:S(2)}, u32[]{:S(2)}) async-start(bf16[8,64,1024]{2,1,0:T(8,128)(2,1)} %pad_maximum_fusion.9), calls=%async_computation | async-start | bytes 2097152 | tf_op jit(solution)/shard_map/all_to_all | solution.py:449
  21.1 115.9 %all-gather.3.cloned.1.call-start = ((), (), s32[]{:S(2)}) async-start(), calls=%async_computation.8 | async-start | bytes 2654208 | tf_op jit(solution)/shard_map/all_gather | solution.py:490
  56.4 47.5 %all-to-all-start.1 = ((bf16[8,64,1024]{2,1,0:T(8,128)(2,1)}), bf16[8,64,1024]{2,1,0:T(8,128)(2,1)S(1)}, u32[]{:S(2)}, u32[]{:S(2)}) async-start(bf16[8,64,1024]{2,1,0:T(8,128)(2,1)} %pad_maximum_fusion.12), calls=%async_computation.1 | async-start | bytes 2097152 | tf_op jit(solution)/shard_map/all_to_all | solution.py:449
  60.0 166.5 %all-gather.5.cloned.1.call-start = ((), (), s32[]{:S(2)}) async-start(), calls=%async_computation.9 | async-start | bytes 4718592 | tf_op jit(solution)/shard_map/all_gather | solution.py:626
  67.3 37.0 %collective-permute-start.1 = (bf16[256,1024]{1,0:T(8,128)(2,1)}, bf16[256,1024]{1,0:T(8,128)(2,1)}, u32[]{:S(2)}, u32[]{:S(2)}) collective-permute-start(bf16[256,1024]{1,0:T(8,128)(2,1)} %fusion.97), channel_id=1, source_target_pairs={{0,2},{1,3},{2,0},{3,1},{4,6},{5,7},{6,4},{7,5},{8,10},{9,11},{10,... | collective-permute-start | bytes 1572872 | tf_op jit(solution)/shard_map/ppermute | solution.py:368
  68.8 38.2 %collective-permute-start = (bf16[256,1024]{1,0:T(8,128)(2,1)S(1)}, bf16[256,1024]{1,0:T(8,128)(2,1)}, u32[]{:S(2)}, u32[]{:S(2)}) collective-permute-start(bf16[256,1024]{1,0:T(8,128)(2,1)S(1)} %bitcast.269), channel_id=1, source_target_pairs={{0,2},{1,3},{2,0},{3,1},{4,6},{5,7},{6,4},{7,5},{8,10},{9,11},{10,... | collective-permute-start | bytes 1572872 | tf_op jit(solution)/shard_map/ppermute | solution.py:368
  109.0 28.0 %collective-permute-start.2 = (bf16[512,1024]{1,0:T(8,128)(2,1)}, bf16[512,1024]{1,0:T(8,128)(2,1)}, u32[]{:S(2)}, u32[]{:S(2)}) collective-permute-start(bf16[512,1024]{1,0:T(8,128)(2,1)} %pad_maximum_fusion.10.near_ref), channel_id=1, source_target_pairs={{0,1},{1,0},{2,3},{3,2},{4,5},{5,4},{6,7},{7,6},{8,9},{9,8},{10,11... | collective-permute-start | bytes 3145736 | tf_op jit(solution)/shard_map/ppermute | solution.py:368
  109.0 28.0 %collective-permute-start.3 = (bf16[512,1024]{1,0:T(8,128)(2,1)}, bf16[512,1024]{1,0:T(8,128)(2,1)}, u32[]{:S(2)}, u32[]{:S(2)}) collective-permute-start(bf16[512,1024]{1,0:T(8,128)(2,1)} %pad_maximum_fusion.11.grad_ref.refs_8_), channel_id=1, source_target_pairs={{0,1},{1,0},{2,3},{3,2},{4,5},{5,4},{6,7},{7,6},{8,9},{9,8},{10,11... | collective-permute-start | bytes 3145736 | tf_op jit(solution)/shard_map/ppermute | solution.py:368
  111.4 23.5 %collective-permute-start.5 = (bf16[256,1024]{1,0:T(8,128)(2,1)S(1)}, bf16[256,1024]{1,0:T(8,128)(2,1)}, u32[]{:S(2)}, u32[]{:S(2)}) collective-permute-start(bf16[256,1024]{1,0:T(8,128)(2,1)S(1)} %convert_element_type.338), channel_id=1, source_target_pairs={{0,2},{1,3},{2,0},{3,1},{4,6},{5,7},{6,4},{7,5},{8,10},{9,11},{10,... | collective-permute-start | bytes 1572872 | tf_op jit(solution)/shard_map/ppermute | solution.py:368
  141.1 359.2 %reduce-scatter.2.cloned.1.call-start = ((), (), s32[]{:S(2)}) async-start(), calls=%async_computation.10 | async-start | bytes 4718592 | tf_op jit(solution)/shard_map/reduce_scatter | solution.py:674
  168.7 23.1 %collective-permute-start.8 = (bf16[256,1024]{1,0:T(8,128)(2,1)S(1)}, bf16[256,1024]{1,0:T(8,128)(2,1)S(1)}, u32[]{:S(2)}, u32[]{:S(2)}) collective-permute-start(bf16[256,1024]{1,0:T(8,128)(2,1)S(1)} %slice.637), channel_id=1, source_target_pairs={{0,2},{1,3},{2,0},{3,1},{4,6},{5,7},{6,4},{7,5},{8,10},{9,11},{10,... | collective-permute-start | bytes 1572872 | tf_op jit(solution)/shard_map/ppermute | solution.py:368
  199.3 24.1 %collective-permute-start.12 = (bf16[256,1024]{1,0:T(8,128)(2,1)S(1)}, bf16[256,1024]{1,0:T(8,128)(2,1)S(1)}, u32[]{:S(2)}, u32[]{:S(2)}) collective-permute-start(bf16[256,1024]{1,0:T(8,128)(2,1)S(1)} %slice.636), channel_id=1, source_target_pairs={{0,2},{1,3},{2,0},{3,1},{4,6},{5,7},{6,4},{7,5},{8,10},{9,11},{10,... | collective-permute-start | bytes 1572872 | tf_op jit(solution)/shard_map/ppermute | solution.py:368
  258.3 24.2 %collective-permute-start.20 = (bf16[256,1024]{1,0:T(8,128)(2,1)}, bf16[256,1024]{1,0:T(8,128)(2,1)S(1)}, u32[]{:S(2)}, u32[]{:S(2)}) collective-permute-start(bf16[256,1024]{1,0:T(8,128)(2,1)} %slice.634), channel_id=1, source_target_pairs={{0,2},{1,3},{2,0},{3,1},{4,6},{5,7},{6,4},{7,5},{8,10},{9,11},{10,... | collective-permute-start | bytes 1572872 | tf_op jit(solution)/shard_map/ppermute | solution.py:368
  290.9 26.3 %collective-permute-start.21 = (bf16[256,1024]{1,0:T(8,128)(2,1)}, bf16[256,1024]{1,0:T(8,128)(2,1)}, u32[]{:S(2)}, u32[]{:S(2)}) collective-permute-start(bf16[256,1024]{1,0:T(8,128)(2,1)} %slice.633), channel_id=1, source_target_pairs={{0,2},{1,3},{2,0},{3,1},{4,6},{5,7},{6,4},{7,5},{8,10},{9,11},{10,... | collective-permute-start | bytes 1572872 | tf_op jit(solution)/shard_map/ppermute | solution.py:368
  292.4 23.5 %collective-permute-start.22 = (bf16[256,1024]{1,0:T(8,128)(2,1)}, bf16[256,1024]{1,0:T(8,128)(2,1)}, u32[]{:S(2)}, u32[]{:S(2)}) collective-permute-start(bf16[256,1024]{1,0:T(8,128)(2,1)} %convert_element_type.350), channel_id=1, source_target_pairs={{0,2},{1,3},{2,0},{3,1},{4,6},{5,7},{6,4},{7,5},{8,10},{9,11},{10,... | collective-permute-start | bytes 1572872 | tf_op jit(solution)/shard_map/ppermute | solution.py:368
  292.9 25.9 %collective-permute-start.23 = (bf16[512,1024]{1,0:T(8,128)(2,1)}, bf16[512,1024]{1,0:T(8,128)(2,1)}, u32[]{:S(2)}, u32[]{:S(2)}) collective-permute-start(bf16[512,1024]{1,0:T(8,128)(2,1)} %get-tuple-element.189), channel_id=1, source_target_pairs={{0,1},{1,0},{2,3},{3,2},{4,5},{5,4},{6,7},{7,6},{8,9},{9,8},{10,11... | collective-permute-start | bytes 3145736 | tf_op jit(solution)/shard_map/ppermute | solution.py:368
  324.1 27.6 %collective-permute-start.26 = (bf16[256,1024]{1,0:T(8,128)(2,1)S(1)}, bf16[256,1024]{1,0:T(8,128)(2,1)S(1)}, u32[]{:S(2)}, u32[]{:S(2)}) collective-permute-start(bf16[256,1024]{1,0:T(8,128)(2,1)S(1)} %slice.632), channel_id=1, source_target_pairs={{0,2},{1,3},{2,0},{3,1},{4,6},{5,7},{6,4},{7,5},{8,10},{9,11},{10,... | collective-permute-start | bytes 1572872 | tf_op jit(solution)/shard_map/ppermute | solution.py:368
  325.7 27.2 %collective-permute-start.25 = (bf16[256,1024]{1,0:T(8,128)(2,1)S(1)}, bf16[256,1024]{1,0:T(8,128)(2,1)S(1)}, u32[]{:S(2)}, u32[]{:S(2)}) collective-permute-start(bf16[256,1024]{1,0:T(8,128)(2,1)S(1)} %convert_element_type.353), channel_id=1, source_target_pairs={{0,2},{1,3},{2,0},{3,1},{4,6},{5,7},{6,4},{7,5},{8,10},{9,11},{10,... | collective-permute-start | bytes 1572872 | tf_op jit(solution)/shard_map/ppermute | solution.py:368
  358.5 55.1 %all-to-all-start.2 = ((bf16[8,64,1024]{2,1,0:T(8,128)(2,1)}), bf16[8,64,1024]{2,1,0:T(8,128)(2,1)}, u32[]{:S(2)}, u32[]{:S(2)}) async-start(bf16[8,64,1024]{2,1,0:T(8,128)(2,1)} %pad_maximum_fusion.19), calls=%async_computation.2 | async-start | bytes 2097152 | tf_op jit(solution)/shard_map/all_to_all | solution.py:449
  364.4 27.0 %collective-permute-start.29 = (bf16[256,1024]{1,0:T(8,128)(2,1)S(1)}, bf16[256,1024]{1,0:T(8,128)(2,1)S(1)}, u32[]{:S(2)}, u32[]{:S(2)}) collective-permute-start(bf16[256,1024]{1,0:T(8,128)(2,1)S(1)} %slice.631), channel_id=1, source_target_pairs={{0,2},{1,3},{2,0},{3,1},{4,6},{5,7},{6,4},{7,5},{8,10},{9,11},{10,... | collective-permute-start | bytes 1572872 | tf_op jit(solution)/shard_map/ppermute | solution.py:368
  416.1 26.3 %collective-permute-start.30 = (bf16[1,512,1024]{2,1,0:T(8,128)(2,1)}, bf16[1,512,1024]{2,1,0:T(8,128)(2,1)}, u32[]{:S(2)}, u32[]{:S(2)}) collective-permute-start(bf16[1,512,1024]{2,1,0:T(8,128)(2,1)} %bitcast.42), channel_id=1, source_target_pairs={{0,2},{1,3},{2,0},{3,1},{4,6},{5,7},{6,4},{7,5},{8,10},{9,11},{10,... | collective-permute-start | bytes 3145736 | tf_op jit(solution)/shard_map/ppermute | solution.py:368
  418.8 34.4 %all-to-all-start.3 = ((bf16[8,32,1024]{2,1,0:T(8,128)(2,1)}), bf16[8,32,1024]{2,1,0:T(8,128)(2,1)S(1)}, u32[]{:S(2)}, u32[]{:S(2)}) async-start(bf16[8,32,1024]{2,1,0:T(8,128)(2,1)} %bitcast.47), calls=%async_computation.3 | async-start | bytes 1048576 | tf_op jit(solution)/shard_map/all_to_all | solution.py:449
  424.9 28.2 %collective-permute-start.33 = (bf16[256,1024]{1,0:T(8,128)(2,1)S(1)}, bf16[256,1024]{1,0:T(8,128)(2,1)S(1)}, u32[]{:S(2)}, u32[]{:S(2)}) collective-permute-start(bf16[256,1024]{1,0:T(8,128)(2,1)S(1)} %slice.630), channel_id=1, source_target_pairs={{0,2},{1,3},{2,0},{3,1},{4,6},{5,7},{6,4},{7,5},{8,10},{9,11},{10,... | collective-permute-start | bytes 1572872 | tf_op jit(solution)/shard_map/ppermute | solution.py:368
  445.4 83.1 %collective-permute-start.31 = (bf16[2,512,1024]{2,1,0:T(8,128)(2,1)}, bf16[2,512,1024]{2,1,0:T(8,128)(2,1)}, u32[]{:S(2)}, u32[]{:S(2)}) collective-permute-start(bf16[2,512,1024]{2,1,0:T(8,128)(2,1)} %pad_maximum_fusion.3), channel_id=1, source_target_pairs={{0,1},{1,0},{2,3},{3,2},{4,5},{5,4},{6,7},{7,6},{8,9},{9,8},{10,11... | collective-permute-start | bytes 6291464 | tf_op jit(solution)/shard_map/ppermute | solution.py:368
  460.9 21.5 %collective-permute-start.36 = (bf16[4,128,512]{2,1,0:T(8,128)(2,1)S(1)}, bf16[4,128,512]{2,1,0:T(8,128)(2,1)S(1)}, u32[]{:S(2)}, u32[]{:S(2)}) collective-permute-start(bf16[4,128,512]{2,1,0:T(8,128)(2,1)S(1)} %dynamic-slice_bitcast_fusion.1), channel_id=1, source_target_pairs={{0,4},{4,0},{8,12},{12,8},{16,20},{20,16},{24,28},{28,24},{1,5},{5... | collective-permute-start | bytes 1572872 | tf_op jit(solution)/shard_map/ppermute | solution.py:368
  472.1 35.4 %collective-permute-start.53 = (f32[6,1280]{1,0:T(8,128)S(1)}, f32[6,1280]{1,0:T(8,128)S(1)}, u32[]{:S(2)}, u32[]{:S(2)}) collective-permute-start(f32[6,1280]{1,0:T(8,128)S(1)} %fusion.140), channel_id=1, source_target_pairs={{0,8},{4,12},{8,0},{12,4},{16,24},{20,28},{24,16},{28,20},{1,9},{5... | collective-permute-start | bytes 92168 | tf_op jit(solution)/shard_map/ppermute | solution.py:368
  502.7 22.2 %all-to-all-start.4 = ((bf16[8,128,256]{2,1,0:T(8,128)(2,1)}), bf16[8,128,256]{2,1,0:T(8,128)(2,1)}, u32[]{:S(2)}, u32[]{:S(2)}) async-start(bf16[8,128,256]{2,1,0:T(8,128)(2,1)} %get-tuple-element.230), calls=%async_computation.5 | async-start | bytes 1048576 | tf_op jit(solution)/shard_map/all_to_all | solution.py:449
  524.9 30.8 %collective-permute-start.35 = (bf16[2,256,1024]{2,1,0:T(8,128)(2,1)}, bf16[2,256,1024]{2,1,0:T(8,128)(2,1)}, u32[]{:S(2)}, u32[]{:S(2)}) collective-permute-start(bf16[2,256,1024]{2,1,0:T(8,128)(2,1)} %pad_maximum_fusion.20), channel_id=1, source_target_pairs={{0,1},{1,0},{2,3},{3,2},{4,5},{5,4},{6,7},{7,6},{8,9},{9,8},{10,11... | collective-permute-start | bytes 3145736 | tf_op jit(solution)/shard_map/ppermute | solution.py:368
  555.0 38.5 %collective-permute-start.47 = (bf16[1024,512]{1,0:T(8,128)(2,1)S(1)}, bf16[1024,512]{1,0:T(8,128)(2,1)}, u32[]{:S(2)}, u32[]{:S(2)}) collective-permute-start(bf16[1024,512]{1,0:T(8,128)(2,1)S(1)} %maximum_select_fusion.3), channel_id=1, source_target_pairs={{0,2},{1,3},{2,0},{3,1},{4,6},{5,7},{6,4},{7,5},{8,10},{9,11},{10,... | collective-permute-start | bytes 3145736 | tf_op jit(solution)/shard_map/ppermute | solution.py:368
  562.1 30.2 %collective-permute-start.42 = (bf16[1,256,1024]{2,1,0:T(8,128)(2,1)S(1)}, bf16[1,256,1024]{2,1,0:T(8,128)(2,1)S(1)}, u32[]{:S(2)}, u32[]{:S(2)}) collective-permute-start(bf16[1,256,1024]{2,1,0:T(8,128)(2,1)S(1)} %bitcast.278), channel_id=1, source_target_pairs={{0,2},{1,3},{2,0},{3,1},{4,6},{5,7},{6,4},{7,5},{8,10},{9,11},{10,... | collective-permute-start | bytes 1572872 | tf_op jit(solution)/shard_map/ppermute | solution.py:368
  569.5 44.4 %collective-permute-start.45 = (bf16[1024,512]{1,0:T(8,128)(2,1)S(1)}, bf16[1024,512]{1,0:T(8,128)(2,1)S(1)}, u32[]{:S(2)}, u32[]{:S(2)}) collective-permute-start(bf16[1024,512]{1,0:T(8,128)(2,1)S(1)} %maximum_select_fusion.2), channel_id=1, source_target_pairs={{0,2},{1,3},{2,0},{3,1},{4,6},{5,7},{6,4},{7,5},{8,10},{9,11},{10,... | collective-permute-start | bytes 3145736 | tf_op jit(solution)/shard_map/ppermute | solution.py:368
  593.5 73.5 %collective-permute-start.43 = (bf16[2,256,1024]{2,1,0:T(8,128)(2,1)}, bf16[2,256,1024]{2,1,0:T(8,128)(2,1)}, u32[]{:S(2)}, u32[]{:S(2)}) collective-permute-start(bf16[2,256,1024]{2,1,0:T(8,128)(2,1)} %pad_maximum_fusion.21), channel_id=1, source_target_pairs={{0,1},{1,0},{2,3},{3,2},{4,5},{5,4},{6,7},{7,6},{8,9},{9,8},{10,11... | collective-permute-start | bytes 3145736 | tf_op jit(solution)/shard_map/ppermute | solution.py:368
  (106 other events, 1127.8 us)
Sparse Core Ops, SparseCore 0:
  24.7 78.7 all-gather.2
  141.2 72.2 all-gather.4
  355.6 111.6 reduce-scatter.1

commit v3 on v2

--- a/solution.py
+++ b/solution.py
@@ -60,7 +60,7 @@
 
 TILE = 256
 STRIP = 64
-VMEM_BYTES = 56 * 1024 * 1024
+VMEM_BYTES = 24 * 1024 * 1024
 SMALL = pl.CostEstimate(flops=10**9, bytes_accessed=10**6, transcendentals=0)
 LARGE = pl.CostEstimate(flops=20 * 10**9, bytes_accessed=10**6, transcendentals=0)
 MEDIUM = pl.CostEstimate(flops=11 * 10**9, bytes_accessed=10**6, transcendentals=0)
@@ -137,7 +137,7 @@
         pick = jnp.where(wanted == place_col_ref[pl.ds(t * TILE, TILE), :], 1.0, 0.0).astype(low_type)
         part = dot(pick, out_ref[...]).astype(low_type)
         attended_ref[pl.ds(t * TILE, TILE), :] = part
-        branch = dot_nt(part, weights_ref[:, 3 * cols :])
+        branch = dot_nt(part, weights_ref[:, 3 * cols : 4 * cols])
         if t * TILE < half:
             keep_ref[pl.ds(t * TILE, TILE), :] = branch
         else:
@@ -146,7 +146,7 @@
 def attention_forward(near, far, norms, weights, bias, place, segment):
     rows = 2 * near.shape[0]
     width = near.shape[1]
-    cols = weights.shape[1] // 4
+    cols = bias.shape[1] // 3
     heads = cols // HEAD_DIM
     shape = jax.ShapeDtypeStruct
     return pl.pallas_call(
@@ -182,7 +182,9 @@
     for t in range(tiles):
         source = near_ref if t * TILE < half else far_ref
         part = source[pl.ds(t * TILE % half, TILE), :]
-        arrived[pl.ds(t * TILE, TILE), :] = dot(part, weights_ref[:, 3 * cols :]).astype(low_type)
+        arrived[pl.ds(t * TILE, TILE), :] = dot(
+            part, weights_ref[:, 3 * cols : 4 * cols]
+        ).astype(low_type)
     for t in range(tiles):
         wanted = lax.broadcasted_iota(jnp.int32, (TILE, rows), 0) + t * TILE
         pick = jnp.where(wanted == place_row_ref[...], 1.0, 0.0).astype(low_type)
@@ -235,7 +237,7 @@
 def attention_backward(near, far, weights, place, segment, qkv, out, lse):
     rows = 2 * near.shape[0]
     width = near.shape[1]
-    cols = weights.shape[1] // 4
+    cols = out.shape[1]
     heads = cols // HEAD_DIM
     shape = jax.ShapeDtypeStruct
     return pl.pallas_call(
@@ -302,28 +304,37 @@
     )(normed, grad, weights, bias)
 
 
-def grads_kernel(counts, *refs):
+def grads_kernel(groups, *refs):
     out_ref = refs[-1]
     for t in range(out_ref.shape[0] // TILE):
         rows = slice(t * TILE, (t + 1) * TILE)
         start = 0
-        place = 0
-        for count in counts:
+        for group in groups:
             total = 0.0
-            for g in range(count):
-                left, right = refs[place + g], refs[place + count + g]
-                total = total + dot_tn(left[:, rows], right[...])
+            for left, right, at, count in group:
+                total = total + dot_tn(refs[left][:, rows], refs[right][at : at + count, :])
             out_ref[rows, start : start + total.shape[1]] = total.astype(out_ref.dtype)
             start = start + total.shape[1]
-            place = place + 2 * count
 
 
 def grads_of(*groups):
     width = groups[0][0][0].shape[1]
     cols = sum(right[0].shape[1] for _, right in groups)
-    pieces = [piece for left, right in groups for piece in (*left, *right)]
+    pieces = []
+    plan = []
+    for left, right in groups:
+        start = len(pieces)
+        pieces.extend((*left, *right))
+        count = left[0].shape[0]
+        fit = right[0].shape[0] // count
+        plan.append(
+            [
+                (start + g, start + len(left) + g // fit, g % fit * count, count)
+                for g in range(len(left))
+            ]
+        )
     return pl.pallas_call(
-        functools.partial(grads_kernel, [len(left) for left, _ in groups]),
+        functools.partial(grads_kernel, plan),
         out_shape=jax.ShapeDtypeStruct((width, cols), low_type),
         in_specs=[whole_spec()] * len(pieces),
         out_specs=whole_spec(),
@@ -363,6 +374,155 @@
     )(block_of, *parts)
 
 
+def choose_kernel(cols, split, block_ref, first_ref, second_ref, *outs):
+    for s, out in enumerate(outs):
+        block = block_ref[s]
+
+        @pl.when(block < 0)
+        def _():
+            out[...] = jnp.zeros_like(out)
+
+        @pl.when((block >= 0) & (block < split))
+        def _():
+            lanes = pl.multiple_of(jnp.clip(block, 0, split - 1) * cols, cols)
+            out[...] = first_ref[:, pl.ds(lanes, cols)]
+
+        @pl.when(block >= split)
+        def _():
+            lanes = pl.multiple_of(jnp.maximum(block - split, 0) * cols, cols)
+            out[...] = second_ref[:, pl.ds(lanes, cols)]
+
+
+def choose_blocks(block_of, cols, first, second):
+    slot_count = block_of.shape[0]
+    return pl.pallas_call(
+        functools.partial(choose_kernel, cols, 4),
+        out_shape=tuple(
+            [jax.ShapeDtypeStruct((first.shape[0], cols), low_type) for _ in range(slot_count)]
+        ),
+        in_specs=[pl.BlockSpec(memory_space=pltpu.SMEM), whole_spec(), whole_spec()],
+        out_specs=tuple([whole_spec()] * slot_count),
+        compiler_params=pltpu.CompilerParams(vmem_limit_bytes=VMEM_BYTES),
+        cost_estimate=SMALL,
+    )(block_of, first, second)
+
+
+def precondition_kernel(slot, order, count, place_ref, near_ref, far_ref, *refs):
+    stats_refs = refs[:4]
+    new_left_ref, new_right_ref, direction_ref, square_ref = refs[4 + count : 8 + count]
+    halfway_ref, left_ref, right_ref, left_root_ref, right_root_ref, sems = refs[8 + count :]
+    held = (left_ref, right_ref, left_root_ref, right_root_ref)
+    copies = [
+        pltpu.make_async_copy(source.at[slot], target, sems.at[k])
+        for k, (source, target) in enumerate(zip(stats_refs, held))
+    ]
+    for k in (3, 2, 0, 1):
+        copies[k].start()
+    cols = near_ref.shape[2]
+    rows = left_ref.shape[0]
+    width = near_ref.shape[1]
+    place = place_ref[0]
+    own_rows = pl.ds(pl.multiple_of(place * rows, rows), rows)
+    pieces = [ref.at[k] for ref in (near_ref, far_ref) for k in range(near_ref.shape[0])]
+    lanes = [pl.ds(pl.multiple_of((place ^ j) * cols, cols), cols) for j in order]
+    copies[3].wait()
+    halfway = 0.0
+    for at, piece in zip(lanes, pieces):
+        halfway = halfway + dot_nt(piece[...], right_root_ref[:, at].astype(low_type))
+    halfway_ref[...] = halfway.astype(low_type)
+    copies[2].wait()
+    total = 0.0
+    for t in range(width // TILE):
+        here = slice(t * TILE, (t + 1) * TILE)
+        part = dot(left_root_ref[here, :].astype(low_type), halfway_ref[...])
+        direction_ref[here, :] = part
+        total = total + jnp.sum(part * part, axis=0, keepdims=True)
+    square_ref[...] = total
+    copies[0].wait()
+    left = stat_decay * left_ref[...]
+    for piece in pieces:
+        left = left + dot_nt(piece[own_rows, :], piece[...])
+    new_left_ref[0] = left
+    copies[1].wait()
+    for at, piece in zip(lanes, pieces):
+        new_right_ref[0, :, at] = stat_decay * right_ref[:, at] + dot_tn(
+            pieces[0][...], piece[...]
+        )
+
+
+def precondition(s, place, near, far, stats, before):
+    slot_count, rows, width = stats[0].shape
+    cols = near.shape[2]
+    shape = jax.ShapeDtypeStruct
+
+    def of_slot(array):
+        return pl.BlockSpec((1,) + array.shape[1:], lambda i: (s, 0, 0))
+
+    def all_of(dims):
+        return pl.BlockSpec(dims, lambda i: (0,) * len(dims))
+
+    return pl.pallas_call(
+        functools.partial(
+            precondition_kernel, s, near_order(lax.axis_size("mp")), len(before)
+        ),
+        grid=(1,),
+        out_shape=(
+            shape(stats[0].shape, f32),
+            shape(stats[1].shape, f32),
+            shape((width, cols), f32),
+            shape((1, cols), f32),
+        ),
+        in_specs=[pl.BlockSpec(memory_space=pltpu.SMEM), all_of(near.shape), all_of(far.shape)]
+        + [pl.BlockSpec(memory_space=pl.ANY)] * (4 + len(before)),
+        out_specs=(
+            of_slot(stats[0]),
+            of_slot(stats[1]),
+            all_of((width, cols)),
+            all_of((1, cols)),
+        ),
+        input_output_aliases={7 + k: k for k in range(len(before))},
+        scratch_shapes=[pltpu.VMEM((width, cols), low_type)]
+        + [pltpu.VMEM(array.shape[1:], f32) for array in stats]
+        + [pltpu.SemaphoreType.DMA((4,))],
+        compiler_params=pltpu.CompilerParams(vmem_limit_bytes=VMEM_BYTES),
+        cost_estimate=SMALL,
+    )(place, near, far, *stats, *before)
+
+
+def give_back_kernel(slot_ref, near_ref, far_ref, *refs):
+    out_ref = refs[-1]
+    half = near_ref.shape[0]
+    for t in range(out_ref.shape[1] // TILE):
+        here = slice(t * TILE, (t + 1) * TILE)
+        total = 0.0
+        for start, source in ((0, near_ref), (half, far_ref)):
+            wanted = lax.broadcasted_iota(jnp.int32, (TILE, half), 1) + start
+            pick = jnp.where(wanted == slot_ref[here, :], 1.0, 0.0).astype(low_type)
+            total = total + dot(pick, source[...])
+        out_ref[0, here, :] = total.astype(low_type)
+
+
+def give_back(micro, slots, near, far, micro_count, before):
+    rows, width = 2 * near.shape[0], near.shape[1]
+
+    def all_of(dims):
+        return pl.BlockSpec(dims, lambda i: (0,) * len(dims))
+
+    return [
+        pl.pallas_call(
+            give_back_kernel,
+            grid=(1,),
+            out_shape=jax.ShapeDtypeStruct((micro_count, rows, width), low_type),
+            in_specs=[all_of((rows, 1)), all_of(near.shape), all_of(far.shape)]
+            + [pl.BlockSpec(memory_space=pl.ANY)] * len(before),
+            out_specs=pl.BlockSpec((1, rows, width), lambda i: (micro, 0, 0)),
+            input_output_aliases={3 + k: k for k in range(len(before))},
+            compiler_params=pltpu.CompilerParams(vmem_limit_bytes=VMEM_BYTES),
+            cost_estimate=SMALL,
+        )(slots[:, None], near, far, *before)
+    ]
+
+
 def swap(values, axis, bit):
     count = lax.axis_size(axis)
     return lax.ppermute(values, axis, [(i, i ^ bit) for i in range(count)])
@@ -390,13 +550,22 @@
 
 
 def scatter_chips(keep, received):
-    values = keep + received.astype(f32)
     bit = 2
-    while bit < lax.axis_size("mp"):
+    count = lax.axis_size("mp")
+    if bit == count:
+        return keep + received.astype(f32)
+    half = keep.shape[0] // 2
+    sent = (keep[half:] + received[half:].astype(f32)).astype(low_type)
+    got = swap(sent, "mp", bit)
+    values = keep[:half] + received[:half].astype(f32)
+    bit *= 2
+    while bit < count:
+        values = values + got.astype(f32)
         half = values.shape[0] // 2
-        values = values[:half] + swap(values[half:].astype(low_type), "mp", bit).astype(f32)
+        got = swap(values[half:].astype(low_type), "mp", bit)
+        values, got = values[:half], got
         bit *= 2
-    return values
+    return values + got.astype(f32)
 
 
 def after(values, others):
@@ -407,20 +576,20 @@
     return lax.optimization_barrier(values)
 
 
-def scatter_grads(values):
-    count = lax.axis_size("dp")
-    index = lax.axis_index("dp")
-    blocks = values.reshape(count, -1, values.shape[-1])
-    bit = 1
-    width = count
-    while bit < count:
-        blocks = blocks.reshape(width // 2, 2, -1, values.shape[-1])
-        mine = lax.dynamic_index_in_dim(blocks, index // bit % 2, 1, keepdims=False)
-        other = lax.dynamic_index_in_dim(blocks, 1 - index // bit % 2, 1, keepdims=False)
-        blocks = mine.astype(f32) + swap(other.astype(low_type), "dp", bit).astype(f32)
+def scatter_step(blocks, bit):
+    index = lax.axis_index("dp") // bit % 2
+    blocks = blocks.reshape(-1, 2, *blocks.shape[1:])
+    mine = lax.dynamic_index_in_dim(blocks, index, 1, keepdims=False)
+    other = lax.dynamic_index_in_dim(blocks, 1 - index, 1, keepdims=False)
+    got = swap(other.astype(low_type), "dp", bit)
+    return mine.astype(f32) + got.astype(f32)
+
+
+def scatter_grads(blocks, bit):
+    while bit < lax.axis_size("dp"):
+        blocks = scatter_step(blocks, bit)
         bit *= 2
-        width //= 2
-    return blocks.reshape(-1, values.shape[-1])
+    return blocks[0].astype(low_type)
 
 
 def sum_over(values, axis):
@@ -429,20 +598,6 @@
         values = values + swap(values, axis, bit)
         bit *= 2
     return values
-
-
-def gather_columns(share, axis):
-    index = lax.axis_index(axis)
-    bit = 1
-    while bit < lax.axis_size(axis):
-        other = swap(share, axis, bit)
-        share = jnp.where(
-            (index & bit) != 0,
-            jnp.concatenate([other, share], axis=-1),
-            jnp.concatenate([share, other], axis=-1),
-        )
-        bit *= 2
-    return share
 
 
 def exchange(rows):
@@ -487,7 +642,15 @@
     shipped_one = jnp.concatenate(
         [shipped_one, jnp.pad(norm_columns, ((0, 0), (0, lanes - norm_columns.shape[1])))], axis=1
     )
-    gathered = lax.all_gather(shipped_one, "dp", axis=0, tiled=True)
+    placement_ids, shipped_one = together(placement_ids, shipped_one)
+    slot_count = left_stats.shape[0]
+    all_slots = slot_count * data_count
+    slot_match = block_slot_index[None, :] == jnp.arange(all_slots)[:, None]
+    filled = jnp.any(slot_match, axis=1)
+    block_of = jnp.sum(jnp.where(slot_match, jnp.arange(blocks)[None, :], 0), axis=1)
+    block_of = jnp.where(filled, block_of, -1)
+    own_blocks = lax.dynamic_slice_in_dim(block_of, data_index * slot_count, slot_count, 0)
+
     order = jnp.arange(rows_here)
     earlier = (order[:, None] < order[None, :]).astype(low_type)
     device_ids = jnp.arange(data_count)[:, None]
@@ -518,44 +681,39 @@
         place = place.reshape(model_count, own_rows)[model_index ^ jnp.array(near)]
         positions.append(place.reshape(rows_here))
 
-    def send_rows(micro, *given):
+    def pick_rows(given):
+        picked = []
+        for micro in range(micro_count):
+            rank, target = slots_mine[micro]
+            here = (rank // sub_rows) == model_index
+            slot = jnp.where(here, target * sub_rows + rank % sub_rows, -1)
+            pick = (slot[None, :] == jnp.arange(own_rows)[:, None]).astype(low_type)
+            rows = dot(pick, given[micro]).astype(low_type)
+            picked.append(rows.reshape(data_count, sub_rows, model_width))
+        return jnp.concatenate(picked, axis=1)
+
+    def arrived(picked):
+        got = exchange(picked).reshape(data_count, micro_count, sub_rows, model_width)
+        return [got[:, i].reshape(own_rows, model_width) for i in range(micro_count)]
+
+    def exchange_back(own):
+        sent = [rows.reshape(data_count, 1, sub_rows, model_width) for rows in own]
+        sent = jnp.concatenate(sent, axis=1)
+        got = exchange(sent.reshape(data_count, -1, model_width))
+        got = got.reshape(data_count, len(own), sub_rows, model_width)
+        return [got[:, i].reshape(own_rows, model_width) for i in range(len(own))]
+
+    def return_slots(micro):
         rank, target = slots_mine[micro]
-        here = (rank // sub_rows) == model_index
-        slot = jnp.where(here, target * sub_rows + rank % sub_rows, -1)
-        pick = (slot[None, :] == jnp.arange(own_rows)[:, None]).astype(low_type)
-        picked = [dot(pick, rows[micro]).astype(low_type) for rows in given]
-        picked = [rows.reshape(data_count, sub_rows, model_width) for rows in picked]
-        got = exchange(jnp.concatenate(picked, axis=1))
-        got = got.reshape(data_count, len(given), sub_rows, model_width)
-        return [got[:, i].reshape(own_rows, model_width).astype(f32) for i in range(len(given))]
-
-    def exchange_back(own):
-        sent = [rows.reshape(data_count, sub_rows, model_width) for rows in own]
-        return exchange(jnp.concatenate(sent, axis=1))
-
-    def return_rows(back, which):
-        back = back.reshape(data_count, len(which), sub_rows, model_width)
-        back = jnp.swapaxes(back, 0, 1).reshape(1, len(which) * own_rows, model_width)
-        bit = model_count // 2
-        while bit >= 1:
-            back = jnp.concatenate([back, swap(back, "mp", bit)], axis=0)
-            bit //= 2
-        returned = []
-        for i, micro in enumerate(which):
-            rank, target = slots_mine[micro]
-            block = jnp.sum(
-                jnp.where(
-                    ((rank // sub_rows) ^ model_index) == jnp.array(near)[:, None],
-                    jnp.arange(model_count)[:, None],
-                    0,
-                ),
-                axis=0,
-            )
-            slot = block * own_rows + target * sub_rows + rank % sub_rows
-            pick = (slot[:, None] == order[None, :]).astype(low_type)
-            rows = back[:, i * own_rows : (i + 1) * own_rows]
-            returned.append(dot(pick, rows.reshape(rows_here, model_width)).astype(low_type))
-        return jnp.stack(returned)
+        block = jnp.sum(
+            jnp.where(
+                ((rank // sub_rows) ^ model_index) == jnp.array(near)[:, None],
+                jnp.arange(model_count)[:, None],
+                0,
+            ),
+            axis=0,
+        )
+        return block * own_rows + target * sub_rows + rank % sub_rows
 
     micros = range(micro_count)
     bounds = [jnp.cumsum(lengths[i, 0]) for i in micros]
@@ -567,11 +725,7 @@
     )[None]
     bias_up = head_vectors[2:].reshape(1, -1)
     half = rows_here // 2
-
-    def arrived(i):
-        rows, grads = send_rows(i, tokens, cotangent)
-        keep = (positions[i][:own_rows] < bounds[i][-2]).astype(f32)[:, None]
-        return rows, grads * keep
+    halves = (slice(0, half), slice(half, rows_here))
 
     def attend(i, near, far):
         return attention_forward(
@@ -580,14 +734,6 @@
 
     def second_share(hidden):
         return layer_norm(hidden, norms[3], norms[4]).astype(low_type)
-
-    def feed_forward(near, far, grad_near, grad_far):
-        far_parts = mlp(far, grad_far, weights_two, bias_up, low_type)
-        near_parts = mlp(near, grad_near, weights_two, bias_up, f32)
-        active, grad_up, (feed_keep, feed_send), (back_keep, back_send), sums = zip(
-            near_parts, far_parts
-        )
-        return active, grad_up, feed_keep, feed_send, back_keep, back_send, sum(sums)
 
     def second_back(i, hidden, grad_normed):
         hidden_part, gain_rows = norm_back(hidden, norms[3], grad_normed)
@@ -611,109 +757,155 @@
         sums = [jnp.sum(gain_rows, axis=0), jnp.sum(grad_normed, axis=0)]
         return (grad_hidden + rows_part).astype(low_type), jnp.stack(sums)
 
-    rows_0, grad_0 = arrived(0)
-    rows_1, grad_1 = arrived(1)
-    x_0 = gather_chips(rows_0.astype(low_type))
-    g_0 = gather_chips(grad_0.astype(low_type))
-    x_0, g_0, rows_1, grad_1 = together(x_0, g_0, rows_1, grad_1)
+    picked, shipped_one = together(pick_rows(tokens), shipped_one)
+    gathered = lax.all_gather(shipped_one, "dp", axis=0, tiled=True)
+    x_0, x_1 = arrived(picked)
+    rows_0, rows_1 = x_0.astype(f32), x_1.astype(f32)
     rows_own = (rows_0, rows_1)
-    grad_out = (grad_0, grad_1)
-    xf_0, gf_0, gathered, shipped_two = together(
-        other_core(x_0), other_core(g_0), gathered, shipped_two
-    )
-    weights_one = gathered[:, : 4 * local_cols]
+    x_0 = gather_chips(x_0)
+    x_1 = gather_chips(x_1)
+    keep = [(positions[i][:own_rows] < bounds[i][-2])[:, None] for i in micros]
+    picked, x_0 = together(pick_rows(cotangent), x_0)
+    g_0, g_1 = (jnp.where(k, g, 0).astype(low_type) for g, k in zip(arrived(picked), keep))
+    grad_out = (g_0.astype(f32), g_1.astype(f32))
+    xf_0 = other_core(x_0)
+    xf_1 = other_core(x_1)
+    gathered, shipped_two, xf_0, xf_1, g_0, g_1 = together(
+        gathered, shipped_two, xf_0, xf_1, g_0, g_1
+    )
+    weights_one = gathered
     norms = jnp.swapaxes(gathered[:, 4 * local_cols :], 0, 1)[:6].astype(f32)
     weights_two = lax.all_gather(shipped_two, "dp", axis=0, tiled=True)
 
     keep_0, send_0, normed_0, *kept_0 = attend(0, x_0, xf_0)
-    x_1 = gather_chips(rows_1.astype(low_type))
-    g_1 = gather_chips(grad_1.astype(low_type))
-    keep_0, send_0, x_1, g_1 = together(keep_0, send_0, x_1, g_1)
-    core_0, xf_1 = together(other_core(send_0), other_core(x_1))
+    g_0 = gather_chips(g_0)
+    keep_0, send_0, g_0, g_1 = together(keep_0, send_0, g_0, g_1)
+    core_0, gf_0, g_1 = together(other_core(send_0), other_core(g_0), g_1)
+    branch_0 = scatter_chips(keep_0, core_0)
     keep_1, send_1, normed_1, *kept_1 = attend(1, x_1, xf_1)
-    branch_0 = scatter_chips(keep_0, core_0)
+    g_1 = gather_chips(g_1)
     keep_1, send_1, branch_0, g_1 = together(keep_1, send_1, branch_0, g_1)
-    core_1 = other_core(send_1)
-    gf_1 = other_core(g_1)
     hidden_0 = rows_0 + branch_0 + norms[2]
-    z_0 = second_share(hidden_0)
-    z_0, core_1, gf_1 = together(z_0, core_1, gf_1)
+    z_0, core_1, gf_1 = together(second_share(hidden_0), other_core(send_1), other_core(g_1))
     branch_1 = scatter_chips(keep_1, core_1)
     z_0 = gather_chips(z_0)
-    z_0, branch_1 = together(z_0, branch_1)
+    z_0, branch_1, weights_two, gf_0, gf_1 = together(z_0, branch_1, weights_two, gf_0, gf_1)
     hidden_1 = rows_1 + branch_1 + norms[2]
-    z_1, zf_0, weights_two = together(second_share(hidden_1), other_core(z_0), weights_two)
-
-    active_0, grad_up_0, feed_keep_0, feed_0, keep_0, send_0, up_sums_0 = feed_forward(
-        z_0, zf_0, g_0, gf_0
-    )
-    feed_0 = other_core(feed_0)
-    core_0 = other_core(send_0)
+    z_1, z_0 = together(second_share(hidden_1), z_0)
+
+    zf_0 = other_core(z_0)
+    near_parts = mlp(z_0, g_0, weights_two, bias_up, f32)
     z_1 = gather_chips(z_1)
-    grad_up_0, feed_0, core_0, z_1 = together(grad_up_0, feed_0, core_0, z_1)
-    zf_1, core_0, feed_0 = together(other_core(z_1), core_0, feed_0)
-    active_1, grad_up_1, feed_keep_1, feed_1, keep_1, send_1, up_sums_1 = feed_forward(
-        z_1, zf_1, g_1, gf_1
-    )
-    core_1 = other_core(send_1)
-    back_0 = scatter_chips(keep_0, core_0)
-    feed_0 = scatter_chips(feed_keep_0, feed_0)
-    grad_up_1, core_1, back_0, feed_0, feed_1 = together(
-        grad_up_1, core_1, back_0, feed_0, feed_1
-    )
+    zf_0, near_parts = together(zf_0, near_parts)
+    far_parts = mlp(zf_0, gf_0, weights_two, bias_up, low_type)
+    active_0, grad_up_0, feed_0, back_0, up_sums_0 = zip(near_parts, far_parts)
+    z_1, back_0, feed_0 = together(z_1, back_0, feed_0)
+    zf_1 = other_core(z_1)
+    core_0 = other_core(back_0[1])
+    near_parts = mlp(z_1, g_1, weights_two, bias_up, f32)
+    zf_1, core_0, near_parts = together(zf_1, core_0, near_parts)
+    back_0 = scatter_chips(back_0[0], core_0)
+    core_feed_0 = other_core(feed_0[1])
+    far_parts = mlp(zf_1, gf_1, weights_two, bias_up, low_type)
+    active_1, grad_up_1, feed_1, back_1, up_sums_1 = zip(near_parts, far_parts)
+    back_0, back_1, feed_1, core_feed_0 = together(back_0, back_1, feed_1, core_feed_0)
     hidden_grad_0, h_0, second_sums_0 = second_back(0, hidden_0, back_0)
-    h_0, core_1, grad_up_1, feed_1 = together(h_0, core_1, grad_up_1, feed_1)
+    h_0, grad_up_1, back_1 = together(h_0, grad_up_1, back_1)
+    h_0 = gather_chips(h_0)
     grads_two = grads_of(
         ([z_0, zf_0, z_1, zf_1], [*grad_up_0, *grad_up_1]),
         ([g_0, gf_0, g_1, gf_1], [*active_0, *active_1]),
     )
-    back_1 = scatter_chips(keep_1, core_1)
-    h_0 = gather_chips(h_0)
-    feed_1 = other_core(feed_1)
-    grads_two, back_1, h_0, feed_1 = together(grads_two, back_1, h_0, feed_1)
+    core_1 = other_core(back_1[1])
+    grads_two, h_0, core_1, core_feed_0 = together(grads_two, h_0, core_1, core_feed_0)
     summed_two = lax.psum_scatter(grads_two, "dp", scatter_dimension=0, tiled=True)
+    chosen = choose_blocks(own_blocks, local_cols, weights_one, weights_two)
+    hf_0, chosen, core_1, core_feed_0 = together(other_core(h_0), chosen, core_1, core_feed_0)
+
+    back_1 = scatter_chips(back_1[0], core_1)
+    output_0 = scatter_chips(feed_0[0], core_feed_0)
+    keep_0, send_0, grad_qkv_0, sums_0 = attend_back(0, h_0, hf_0, kept_0)
+    core_feed_1 = other_core(feed_1[1])
+    keep_0, send_0, back_1, output_0, core_feed_1 = together(
+        keep_0, send_0, back_1, output_0, core_feed_1
+    )
     hidden_grad_1, h_1, second_sums_1 = second_back(1, hidden_1, back_1)
-    hf_0, h_1, feed_1 = together(other_core(h_0), h_1, feed_1)
-
-    keep_0, send_0, grad_qkv_0, sums_0 = attend_back(0, h_0, hf_0, kept_0)
+    h_1, keep_0, send_0, output_0 = together(h_1, keep_0, send_0, output_0)
     h_1 = gather_chips(h_1)
-    feed_1 = scatter_chips(feed_keep_1, feed_1)
-    keep_0, send_0, h_1, feed_1, feed_0 = together(keep_0, send_0, h_1, feed_1, feed_0)
-    outputs_back = exchange_back(
-        [
-            (hidden_0 + feed_0 + norms[5]).astype(low_type),
-            (hidden_1 + feed_1 + norms[5]).astype(low_type),
-        ]
-    )
-    core_0, hf_1 = together(other_core(send_0), other_core(h_1))
+    core_0 = other_core(send_0)
+    output_0 = (hidden_0 + output_0 + norms[5]).astype(low_type)
+    h_1, core_0, output_0, core_feed_1 = together(h_1, core_0, output_0, core_feed_1)
+    output_0 = exchange_back([output_0])[0]
+    hf_1, core_0, core_feed_1 = together(other_core(h_1), core_0, core_feed_1)
+    normed_back_0 = scatter_chips(keep_0, core_0)
+    output_1 = scatter_chips(feed_1[0], core_feed_1)
+    grads_out = grads_of(([h_0, hf_0, h_1, hf_1], [kept_0[0], kept_1[0]]))
+    hf_1, grads_out = together(hf_1, grads_out)
+    blocks_out = scatter_step(grads_out.reshape(data_count, shard_rows, local_cols), 1)
     keep_1, send_1, grad_qkv_1, sums_1 = attend_back(1, h_1, hf_1, kept_1)
-    normed_back_0 = scatter_chips(keep_0, core_0)
-    keep_1, send_1, normed_back_0, outputs_back = together(
-        keep_1, send_1, normed_back_0, outputs_back
-    )
+    keep_1, send_1, normed_back_0, output_1, output_0, summed_two, blocks_out = together(
+        keep_1, send_1, normed_back_0, output_1, output_0, summed_two, blocks_out
+    )
+    core_1 = other_core(send_1)
+    grads_qkv = grads_of(([normed_0, normed_1], [grad_qkv_0, grad_qkv_1]))
+    core_1, grads_qkv = together(core_1, grads_qkv)
+    normed_back_1 = scatter_chips(keep_1, core_1)
     input_0, first_sums_0 = first_back(0, hidden_grad_0, normed_back_0)
-    input_0, core_1 = together(input_0, other_core(send_1))
-    inputs_back_0 = exchange_back([input_0])
-    grads_one = grads_of(
-        ([normed_0, normed_1], [grad_qkv_0, grad_qkv_1]),
-        (
-            [h_0, hf_0, h_1, hf_1],
-            [kept[0][rows] for kept in (kept_0, kept_1) for rows in (slice(0, half), slice(half, rows_here))],
-        ),
-    )
-    normed_back_1 = scatter_chips(keep_1, core_1)
-    grads_one, normed_back_1, inputs_back_0 = together(grads_one, normed_back_1, inputs_back_0)
+    output_1 = (hidden_1 + output_1 + norms[5]).astype(low_type)
+    cut = 3 * local_cols // 2 // 128 * 128
+    grads_one = [
+        scatter_step(part.reshape(data_count, shard_rows, -1), 1)
+        for part in (grads_qkv[:, :cut], grads_qkv[:, cut:])
+    ]
+    blocks_out = scatter_step(blocks_out, 2)
+    normed_back_1, grads_one, input_0, output_1, output_0, blocks_out = together(
+        normed_back_1, grads_one, input_0, output_1, output_0, blocks_out
+    )
+    input_0, output_1 = exchange_back([input_0, output_1])
     input_1, first_sums_1 = first_back(1, hidden_grad_1, normed_back_1)
-    summed_one = [
-        scatter_grads(grads_one[:, h * 2 * local_cols : (h + 1) * 2 * local_cols])
-        for h in range(2)
-    ]
+    summed_one = [scatter_grads(part, 2) for part in (*grads_one,)]
+    summed_one.append(scatter_grads(blocks_out, 4))
     norm_grads_own = jnp.concatenate(
         [first_sums_0 + first_sums_1, second_sums_0 + second_sums_1], axis=0
     )
     qkv_sums = sums_0 + sums_1
-    up_sums = [up_sums_0, up_sums_1]
-
+    up_sums = [*up_sums_0, *up_sums_1]
+
+    norm_grads_sum = sum_over(norm_grads_own, "mp")
+    output_0 = gather_chips(output_0)
+    summed_one, output_0, norm_grads_sum, input_1 = together(
+        summed_one, output_0, norm_grads_sum, input_1
+    )
+    slotted = to_slots(block_of, slot_count, local_cols, *summed_one, summed_two)
+    stats = (left_stats, right_stats, left_roots, right_roots)
+    place = model_index.astype(jnp.int32).reshape(1)
+    returns = [return_slots(i) for i in micros]
+
+    def own_slot(s):
+        return exchange(slotted[s]).reshape(1, model_width, local_cols)
+
+    owned_0 = own_slot(0)
+    outputs_given = give_back(0, returns[0], output_0, other_core(output_0), micro_count, [])
+    owned_0, outputs_given, slotted, input_0, output_1 = together(
+        owned_0, outputs_given, slotted, input_0, output_1
+    )
+    near_0 = gather_chips(owned_0)
+    owned = [owned_0] + [own_slot(s) for s in range(1, slot_count)]
+    near_0, owned, input_1, input_0, output_1 = together(
+        near_0, owned, input_1, input_0, output_1
+    )
+    input_1 = exchange_back([input_1])[0]
+    far_0 = other_core(near_0)
+    *fresh, direction, square = precondition(0, place, near_0, far_0, stats, [])
+    directions, squares = [direction], [square]
+    for s in range(1, slot_count):
+        near_part = gather_chips(owned[s])
+        near_part, fresh, input_0, output_1 = together(near_part, fresh, input_0, output_1)
+        *fresh, direction, square = precondition(
+            s, place, near_part, other_core(near_part), stats, fresh
+        )
+        directions.append(direction)
+        squares.append(square)
     head_own = jnp.concatenate(
         [
             qkv_sums[:, :local_cols],
@@ -722,64 +914,35 @@
         ],
         axis=0,
     )
-    vectors = jnp.concatenate([sum_over(norm_grads_own, "mp"), head_own], axis=1)
+    vectors = jnp.concatenate([norm_grads_sum, head_own], axis=1)
+    vectors, input_1 = together(vectors, input_1)
     vectors = sum_over(vectors, "dp")
     norm_all = vectors[:, :model_width]
     head_total = vectors[:, model_width:]
     norm_cols = norm_vectors.shape[1]
     norm_total = lax.dynamic_slice_in_dim(norm_all, data_index * norm_cols, norm_cols, 1)
 
-    slot_count = left_stats.shape[0]
-    all_slots = slot_count * data_count
-    slot_match = block_slot_index[None, :] == jnp.arange(all_slots)[:, None]
-    filled = jnp.any(slot_match, axis=1)
-    block_of = jnp.sum(jnp.where(slot_match, jnp.arange(blocks)[None, :], 0), axis=1)
-    summed = [part.astype(low_type) for part in (*summed_one, summed_two)]
-    owned = [
-        exchange(rows).reshape(model_width, local_cols)
-        for rows in to_slots(jnp.where(filled, block_of, -1), slot_count, local_cols, *summed)
-    ]
-    owned, input_1 = after(owned, input_1)
-    inputs_back_1 = exchange_back([input_1])
-    outputs_given = return_rows(outputs_back, micros)
-    inputs_given = jnp.concatenate(
-        [return_rows(inputs_back_0, [0]), return_rows(inputs_back_1, [1])], axis=0
-    )
-    whole = [gather_columns(owned[s], "mp") for s in range(slot_count)]
-    slot_match_own = lax.dynamic_slice_in_dim(slot_match, data_index * slot_count, slot_count, 0)
-    weights_all = jnp.concatenate([weights_one, weights_two], axis=1)
-
-    row_total_count = left_stats.shape[1]
-    lefts, rights, directions, squares, owned_weights = [], [], [], [], []
-    for s in range(slot_count):
-        grads = whole[s]
-        my_rows = lax.dynamic_slice_in_dim(
-            grads, model_index * row_total_count, row_total_count, 0
-        )
-        lefts.append(stat_decay * left_stats[s] + dot_nt(my_rows, grads))
-        rights.append(stat_decay * right_stats[s] + dot_tn(owned[s], grads))
-        halfway = dot_nt(grads.astype(f32), right_roots[s])
-        direction = dot(left_roots[s], halfway)
-        directions.append(direction)
-        squares.append(jnp.sum(direction * direction))
-        chosen = 0.0
-        for b in range(blocks):
-            chosen = chosen + jnp.where(
-                slot_match_own[s, b],
-                weights_all[:, b * local_cols : (b + 1) * local_cols].astype(f32),
-                0.0,
-            )
-        owned_weights.append(chosen)
+    input_0, output_1, input_1 = [gather_chips(rows) for rows in (input_0, output_1, input_1)]
+    inputs_given = give_back(0, returns[0], input_0, other_core(input_0), micro_count, [])
+    outputs_given = give_back(
+        1, returns[1], output_1, other_core(output_1), micro_count, outputs_given
+    )
+    inputs_given = give_back(
+        1, returns[1], input_1, other_core(input_1), micro_count, inputs_given
+    )[0]
+    outputs_given = outputs_given[0]
+    new_left, new_right = fresh
+    squares = [jnp.sum(square) for square in squares]
     square_total = sum_over(jnp.stack(squares).reshape(1, slot_count), "mp")[0]
     factor = lax.rsqrt(square_total / (model_width * model_width) + mean_eps)
     updated_blocks = jnp.stack(
         [
-            owned_weights[s] - matrix_rate * factor[s] * directions[s]
+            chosen[s].astype(f32) - matrix_rate * factor[s] * directions[s]
             for s in range(slot_count)
         ],
         axis=1,
     )
-    owned_grads = jnp.stack(owned, axis=1).astype(f32)
+    owned_grads = jnp.stack([rows[0] for rows in owned], axis=1).astype(f32)
     new_norm_state = stat_decay * norm_state + norm_total * norm_total
     new_norm_vectors = norm_vectors - vector_rate * norm_total / (
         jnp.sqrt(new_norm_state) + diag_eps
@@ -792,8 +955,8 @@
         outputs_given,
         inputs_given,
         owned_grads,
-        jnp.stack(lefts),
-        jnp.stack(rights),
+        new_left,
+        new_right,
         updated_blocks,
         norm_total,
         new_norm_state,

time: 689 us -> 630 us (0.914)
  waiting for transfers between devices: 239 us -> 201 us
  matrix products: 43.3 us -> 8.44 us
  local copies, waits for them, and re-layouts: 43.2 us -> 77.1 us
  other arithmetic: 110 us -> 78.9 us
  starting transfers between devices: 67.1 us -> 81.3 us
    unnamed x156 -> x259, local copies, waits for them, and re-layouts: 16.4 us -> 51.3 us
    all_to_all x7, waiting for transfers between devices: 94.3 us -> 59.7 us  [exchange(): return lax.all_to_all(rows, 'dp', split_axis=0, concat_axis=0, tiled=True)]
    dot_general x12 -> x6, matrix products: 35.4 us -> 8.44 us  [dot(): lax.dot_general(left, right, (((1,), (0,)), ((), ())), preferred_element_...]
    another operation x8 -> x5, other arithmetic: 26.3 us -> 2.07 us  [the longest x3 1.71 us: on_device(): jnp.stack([chosen[s].astype(f32) - matrix_rate * factor[s] * directions[s...]
    pallas_call x2 -> x10, Pallas kernels: 27.2 us -> 51.3 us  [the longest x4 19.2 us: give_back(): pl.pallas_call(give_back_kernel, grid=(1,), out_shape=jax.ShapeDtypeStruc...]
    concatenate x11 -> x4, other arithmetic: 17.5 us -> 3.18 us  [the longest x2 2.11 us: pick_rows(): return jnp.concatenate(picked, axis=1)]
    pallas_call x4, Pallas kernels: 37.1 us -> 23.5 us  [mlp(): pl.pallas_call(mlp_kernel, out_shape=(shape((rows, cols), low_type), shap...]
    ppermute x55 -> x60, starting transfers between devices: 36.6 us -> 46.3 us  [swap(): return lax.ppermute(values, axis, [(i, i ^ bit) for i in range(count)])]
  transfers between devices with their start and end apart: 65 -> 70, of which waited for: 26 -> 27; matrix products, arithmetic and copies ran while one was open for 23% -> 18% of each run, Pallas kernels for 24% -> 23%
where the time goes in v3:
time: 630 us; the launch traced here: 621 us
  waiting for transfers between devices  201 us (32%)
  Pallas kernels  157 us (25%)
  starting transfers between devices  81.3 us (13%)
  other arithmetic  78.9 us (13%)
  local copies, waits for them, and re-layouts  77.1 us (12%)
  between operations  17.5 us (3%)
  matrix products  8.44 us (1%)
    ppermute x60, waiting for transfers between devices, swap(): return lax.ppermute(values, axis, [(i, i ^ bit) for i in range(count)])  140 us
    all_to_all x7, waiting for transfers between devices, exchange(): return lax.all_to_all(rows, 'dp', split_axis=0, concat_axis=0, tiled=True)  59.7 us
    unnamed x259, local copies, waits for them, and re-layouts  51.3 us
    ppermute x60, starting transfers between devices, swap(): return lax.ppermute(values, axis, [(i, i ^ bit) for i in range(count)])  46.3 us
    pallas_call x2, Pallas kernels, attention_backward(): pl.pallas_call(attention_backward_kernel, out_shape=(shape((rows // 2, wi...  45.2 us
    pallas_call x2, Pallas kernels, attention_forward(): pl.pallas_call(attention_forward_kernel, out_shape=(shape((rows // 2, wid...  35.5 us
    all_to_all x7, starting transfers between devices, exchange(): return lax.all_to_all(rows, 'dp', split_axis=0, concat_axis=0, tiled=True)  34.9 us
    pallas_call x4, Pallas kernels, mlp(): pl.pallas_call(mlp_kernel, out_shape=(shape((rows, cols), low_type), shap...  23.5 us
  transfers between devices with their start and end apart: 70, of which 27 were waited for; matrix products, arithmetic and copies ran while one was open for 18% of the time, Pallas kernels for 23%

profile of v3, /device:TPU:0, one launch (start us, length us, event | category | flops | bytes accessed | tf_op | source)
XLA Modules:
  0.0 621.2 jit_solution(10132653460284615152)
XLA Ops:
  17.0 7.3 %all-to-all-start = ((bf16[8,64,1024]{2,1,0:T(8,128)(2,1)}), bf16[8,64,1024]{2,1,0:T(8,128)(2,1)S(1)}, u32[]{:S(2)}, u32[]{:S(2)}) async-start(bf16[8,64,1024]{2,1,0:T(8,128)(2,1)} %pad_maximum_fusion.2), calls=%async_computation | async-start | bytes 2097152 | tf_op jit(solution)/shard_map/all_to_all | solution.py:604
  27.3 32.2 %all-to-all-done = bf16[8,64,1024]{2,1,0:T(8,128)(2,1)S(1)} async-done(((bf16[8,64,1024]{2,1,0:T(8,128)(2,1)}), bf16[8,64,1024]{2,1,0:T(8,128)(2,1)S(1)}, u32[]{:S(2)}, u32[]{:S(2)}) %all-to-all-start) | async-done | bytes 1048608 | tf_op jit(solution)/shard_map/all_to_all | solution.py:604
  64.6 6.0 collective-permute-done
  70.7 5.5 all-to-all-start.1
  82.6 8.7 %collective-permute-done.1 = bf16[256,1024]{1,0:T(8,128)(2,1)} collective-permute-done((bf16[256,1024]{1,0:T(8,128)(2,1)S(1)}, bf16[256,1024]{1,0:T(8,128)(2,1)}, u32[]{:S(2)}, u32[]{:S(2)}) %collective-permute-start.1) | collective-permute-done | bytes 524320 | tf_op jit(solution)/shard_map/ppermute | solution.py:528
  96.7 12.6 %all-to-all-done.1 = bf16[8,64,1024]{2,1,0:T(8,128)(2,1)} async-done(((bf16[8,64,1024]{2,1,0:T(8,128)(2,1)}), bf16[8,64,1024]{2,1,0:T(8,128)(2,1)}, u32[]{:S(2)}, u32[]{:S(2)}) %all-to-all-start.1) | async-done | bytes 1048608 | tf_op jit(solution)/shard_map/all_to_all | solution.py:604
  120.5 19.0 %shard_map.266 = (f32[512,1024]{1,0:T(8,128)S(1)}, bf16[512,1024]{1,0:T(8,128)(2,1)}, bf16[1024,1024]{1,0:T(8,128)(2,1)S(1)}, bf16[1024,256]{1,0:T(8,128)(2,1)S(...) custom-call(bf16[512,1024]{1,0:T(8,128)(2,1)S(1)} %pad_maximum_fusion.3.near_ref, ...), custom_call_target="tpu_custom_call" | custom-call | flops 20000000000 | bytes 1000000 | tf_op jit(solution)/shard_map/pallas_call | solution.py:152
  153.8 16.5 %shard_map.265 = (f32[512,1024]{1,0:T(8,128)S(1)}, bf16[512,1024]{1,0:T(8,128)(2,1)S(1)}, bf16[1024,1024]{1,0:T(8,128)(2,1)S(1)}, bf16[1024,256]{1,0:T(8,128)(2,...) custom-call(bf16[512,1024]{1,0:T(8,128)(2,1)S(1)} %copy-done.28, ...), custom_call_target="tpu_custom_call" | custom-call | flops 20000000000 | bytes 1000000 | tf_op jit(solution)/shard_map/pallas_call | solution.py:152
  184.1 12.5 %collective-permute-done.11 = bf16[256,1024]{1,0:T(8,128)(2,1)S(1)} collective-permute-done((bf16[256,1024]{1,0:T(8,128)(2,1)S(1)}, bf16[256,1024]{1,0:T(8,128)(2,1)S(1)}, u32[]{:S(2)}, u32[]{:S(2)}) %collective-permute-start.11) | collective-permute-done | bytes 524320 | tf_op jit(solution)/shard_map/ppermute | solution.py:528
  197.6 9.4 %collective-permute-done.12 = bf16[256,1024]{1,0:T(8,128)(2,1)S(1)} collective-permute-done((bf16[256,1024]{1,0:T(8,128)(2,1)S(1)}, bf16[256,1024]{1,0:T(8,128)(2,1)S(1)}, u32[]{:S(2)}, u32[]{:S(2)}) %collective-permute-start.12) | collective-permute-done | bytes 524320 | tf_op jit(solution)/shard_map/ppermute | solution.py:528
  211.6 5.2 shard_map.267
  218.1 5.6 collective-permute-done.14
  223.8 6.8 %shard_map.268 = (bf16[512,1024]{1,0:T(8,128)(2,1)S(1)}, bf16[512,1024]{1,0:T(8,128)(2,1)S(1)}, bf16[512,1024]{1,0:T(8,128)(2,1)S(1)}, bf16[512,1024]{1,0:T(8,128)(2,1)S(1)}, f32[1,1024]{1,0:T(1,128)S(1)}) custom-call(bf16[512,1024]{1,0:T(8,128)(2,1)S(1)} %collective-permute-done.13.normed_ref.refs_1_, ...), custom_call_target="tpu_custom_call" | custom-call | flops 11000000512 | bytes 1000000 | tf_op jit(solution)/shard_map/pallas_call | solution.py:291
  231.2 5.2 shard_map.269
  240.3 6.3 %shard_map.270 = (bf16[512,1024]{1,0:T(8,128)(2,1)S(1)}, bf16[512,1024]{1,0:T(8,128)(2,1)S(1)}, bf16[512,1024]{1,0:T(8,128)(2,1)}, bf16[512,1024]{1,0:T(8,128)(2,1)}, f32[1,1024]{1,0:T(1,128)S(1)}) custom-call(bf16[512,1024]{1,0:T(8,128)(2,1)S(1)} %collective-permute-done.15.normed_ref.refs_3_, bf16[512,1024]{1,0:T(8,128)(2,1)S(1)} %copy-done.44, ...), custom_call_target="tpu_custom_call" | custom-call | flops 11000000512 | bytes 1000000 | tf_op jit(solution)/shard_map/pallas_call | solution.py:291
  246.7 7.0 %collective-permute-done.17 = bf16[256,1024]{1,0:T(8,128)(2,1)S(1)} collective-permute-done((bf16[256,1024]{1,0:T(8,128)(2,1)S(1)}, bf16[256,1024]{1,0:T(8,128)(2,1)S(1)}, u32[]{:S(2)}, u32[]{:S(2)}) %collective-permute-start.17) | collective-permute-done | bytes 524320 | tf_op jit(solution)/shard_map/ppermute | solution.py:528
  256.9 10.1 %shard_map.271 = bf16[1024,2048]{1,0:T(8,128)(2,1)S(1)} custom-call(bf16[512,1024]{1,0:T(8,128)(2,1)S(1)} %copy-done.26, bf16[512,1024]{1,0:T(8,128)(2,1)S(1)} %collective-permute-done.13.normed_ref.refs_1_, bf16[512,1024]{1,0:T(8,128)(2,1)S(1)} %pad_maximum_fusion.8.normed_ref.refs_2_, bf16[512,1024]{1,0:T(8,128)(2,1)S(1)} %collective-permute-done.15.normed_ref.refs_3_, ...), custom_call_target="tpu_custom_call" | custom-call | flops 11000000512 | bytes 1000000 | tf_op jit(solution)/shard_map/pallas_call | solution.py:336
  283.1 22.9 %shard_map.273 = (f32[512,1024]{1,0:T(8,128)S(1)}, bf16[512,1024]{1,0:T(8,128)(2,1)}, bf16[1024,768]{1,0:T(8,128)(2,1)S(1)}, f32[1,768]{1,0:T(1,128)S(1)}) custom-call(bf16[512,1024]{1,0:T(8,128)(2,1)S(1)} %pad_maximum_fusion.9.near_ref.refs_0_, bf16[512,1024]{1,0:T(8,128)(2,1)} %collective-permute-done.21.far_ref.refs_1_, ...), custom_call_target="tpu_custom_call" | custom-call | flops 20000000000 | bytes 1000000 | tf_op jit(solution)/shard_map/pallas_call | solution.py:243
  318.2 9.7 %collective-permute-done.25 = bf16[256,1024]{1,0:T(8,128)(2,1)} collective-permute-done((bf16[256,1024]{1,0:T(8,128)(2,1)}, bf16[256,1024]{1,0:T(8,128)(2,1)}, u32[]{:S(2)}, u32[]{:S(2)}) %collective-permute-start.25) | collective-permute-done | bytes 524320 | tf_op jit(solution)/shard_map/ppermute | solution.py:528
  349.8 22.2 %shard_map.275 = (f32[512,1024]{1,0:T(8,128)S(1)}, bf16[512,1024]{1,0:T(8,128)(2,1)S(1)}, bf16[1024,768]{1,0:T(8,128)(2,1)S(1)}, f32[1,768]{1,0:T(1,128)S(1)}) custom-call(bf16[512,1024]{1,0:T(8,128)(2,1)} %pad_maximum_fusion.10.refs_2_.near_ref, bf16[512,1024]{1,0:T(8,128)(2,1)} %collective-permute-done.27.refs_3_.far_ref, ...), custom_call_target="tpu_custom_call" | custom-call | flops 20000000000 | bytes 1000000 | tf_op jit(solution)/shard_map/pallas_call | solution.py:243
  392.5 9.0 %collective-permute-done.34 = bf16[4,128,384]{2,1,0:T(8,128)(2,1)S(1)} collective-permute-done((bf16[4,128,384]{2,1,0:T(8,128)(2,1)S(1)}, bf16[4,128,384]{2,1,0:T(8,128)(2,1)S(1)}, u32[]{:S(2)}, u32[]{:S(2)}) %collective-permute-start.34) | collective-permute-done | bytes 393248 | tf_op jit(solution)/shard_map/ppermute | solution.py:528
  401.6 7.9 %collective-permute-done.33 = bf16[4,128,384]{2,1,0:T(8,128)(2,1)S(1)} collective-permute-done((bf16[4,128,384]{2,1,0:T(8,128)(2,1)S(1)}, bf16[4,128,384]{2,1,0:T(8,128)(2,1)S(1)}, u32[]{:S(2)}, u32[]{:S(2)}) %collective-permute-start.33) | collective-permute-done | bytes 393248 | tf_op jit(solution)/shard_map/ppermute | solution.py:528
  437.5 18.4 %collective-permute-done.37 = bf16[1,128,384]{2,1,0:T(8,128)(2,1)S(1)} collective-permute-done((bf16[1,128,384]{2,1,0:T(8,128)(2,1)S(1)}, bf16[1,128,384]{2,1,0:T(8,128)(2,1)S(1)}, u32[]{:S(2)}, u32[]{:S(2)}) %collective-permute-start.37) | collective-permute-done | bytes 98336 | tf_op jit(solution)/shard_map/ppermute | solution.py:528
  474.0 4.9 all-to-all-done.3
  484.6 11.9 %collective-permute-done.45 = bf16[1,1024,256]{2,1,0:T(8,128)(2,1)S(1)} collective-permute-done((bf16[1,1024,256]{2,1,0:T(8,128)(2,1)S(1)}, bf16[1,1024,256]{2,1,0:T(8,128)(2,1)S(1)}, u32[]{:S(2)}, u32[]{:S(2)}) %collective-permute-start.45) | collective-permute-done | bytes 524320 | tf_op jit(solution)/shard_map/ppermute | solution.py:528
  497.5 5.6 all-to-all-start.6
  506.2 9.9 %all-to-all-done.6 = bf16[8,32,1024]{2,1,0:T(8,128)(2,1)S(1)} async-done(((bf16[8,32,1024]{2,1,0:T(8,128)(2,1)}), bf16[8,32,1024]{2,1,0:T(8,128)(2,1)S(1)}, u32[]{:S(2)}, u32[]{:S(2)}) %all-to-all-start.6) | async-done | bytes 524320 | tf_op jit(solution)/shard_map/all_to_all | solution.py:604
  534.1 7.1 %shard_map.279 = (f32[2,256,1024]{2,1,0:T(8,128)}, f32[2,256,1024]{2,1,0:T(8,128)}, f32[1024,256]{1,0:T(8,128)S(1)}, f32[1,256]{1,0:T(1,128)S(1)}) custom-call(s32[1]{0:T(128)} %bitcast.87.place_ref, bf16[2,1024,256]{2,1,0:T(8,128)(2,1)} %pad_maximum_fusion.13.near_ref, bf16[2,1024,256]{2,1,0:T(8,128)(2,1)} %collective-permute-done.47.far_ref, ...), custom_call_target="tpu_custom_call" | custom-call | flops 1000000000 | bytes 1000000 | tf_op jit(solution)/shard_map/pallas_call | solution.py:464
  552.1 16.7 %collective-permute-done.52 = bf16[256,1024]{1,0:T(8,128)(2,1)} collective-permute-done((bf16[256,1024]{1,0:T(8,128)(2,1)}, bf16[256,1024]{1,0:T(8,128)(2,1)}, u32[]{:S(2)}, u32[]{:S(2)}) %collective-permute-start.52) | collective-permute-done | bytes 524320 | tf_op jit(solution)/shard_map/ppermute | solution.py:528
  576.5 7.2 %shard_map.283 = (f32[2,256,1024]{2,1,0:T(8,128)}, f32[2,256,1024]{2,1,0:T(8,128)}, f32[1024,256]{1,0:T(8,128)S(1)}, f32[1,256]{1,0:T(1,128)S(1)}) custom-call(s32[1]{0:T(128)} %bitcast.87.place_ref, bf16[2,1024,256]{2,1,0:T(8,128)(2,1)} %pad_maximum_fusion.14.near_ref, ...), custom_call_target="tpu_custom_call", output_to_operand_aliasing={{0}: (7, {}), {1}: (8, {})} | custom-call | flops 1000000000 | bytes 1000000 | tf_op jit(solution)/shard_map/pallas_call | solution.py:464
  598.9 5.2 shard_map.281.refs_0_
  604.2 5.3 shard_map.280
  (588 shorter events, 263.9 us)
Async XLA Ops:
  17.0 42.6 %all-to-all-start = ((bf16[8,64,1024]{2,1,0:T(8,128)(2,1)}), bf16[8,64,1024]{2,1,0:T(8,128)(2,1)S(1)}, u32[]{:S(2)}, u32[]{:S(2)}) async-start(bf16[8,64,1024]{2,1,0:T(8,128)(2,1)} %pad_maximum_fusion.2), calls=%async_computation | async-start | bytes 2097152 | tf_op jit(solution)/shard_map/all_to_all | solution.py:604
  24.3 89.4 %all-gather.3.cloned.1.call-start = ((), (), s32[]{:S(2)}) async-start(), calls=%async_computation.8 | async-start | bytes 2654208 | tf_op jit(solution)/shard_map/all_gather | solution.py:761
  70.7 38.7 %all-to-all-start.1 = ((bf16[8,64,1024]{2,1,0:T(8,128)(2,1)}), bf16[8,64,1024]{2,1,0:T(8,128)(2,1)}, u32[]{:S(2)}, u32[]{:S(2)}) async-start(bf16[8,64,1024]{2,1,0:T(8,128)(2,1)} %pad_maximum_fusion.1), calls=%async_computation.1 | async-start | bytes 2097152 | tf_op jit(solution)/shard_map/all_to_all | solution.py:604
  76.2 132.1 %all-gather.5.cloned.1.call-start = ((), (), s32[]{:S(2)}) async-start(), calls=%async_computation.9 | async-start | bytes 4718592 | tf_op jit(solution)/shard_map/all_gather | solution.py:778
  92.4 20.3 %collective-permute-start.3 = (bf16[512,1024]{1,0:T(8,128)(2,1)S(1)}, bf16[512,1024]{1,0:T(8,128)(2,1)S(1)}, u32[]{:S(2)}, u32[]{:S(2)}) collective-permute-start(bf16[512,1024]{1,0:T(8,128)(2,1)S(1)} %pad_maximum_fusion.4.near_ref), channel_id=1, source_target_pairs={{0,1},{1,0},{2,3},{3,2},{4,5},{5,4},{6,7},{7,6},{8,9},{9,8},{10,11... | collective-permute-start | bytes 3145736 | tf_op jit(solution)/shard_map/ppermute | solution.py:528
  92.5 21.2 %collective-permute-start.2 = (bf16[512,1024]{1,0:T(8,128)(2,1)S(1)}, bf16[512,1024]{1,0:T(8,128)(2,1)}, u32[]{:S(2)}, u32[]{:S(2)}) collective-permute-start(bf16[512,1024]{1,0:T(8,128)(2,1)S(1)} %pad_maximum_fusion.3.near_ref), channel_id=1, source_target_pairs={{0,1},{1,0},{2,3},{3,2},{4,5},{5,4},{6,7},{7,6},{8,9},{9,8},{10,11... | collective-permute-start | bytes 3145736 | tf_op jit(solution)/shard_map/ppermute | solution.py:528
  113.7 268.7 %reduce-scatter.2.cloned.1.call-start = ((), (), s32[]{:S(2)}) async-start(), calls=%async_computation.10 | async-start | bytes 4718592 | tf_op jit(solution)/shard_map/reduce_scatter | solution.py:821
  117.0 27.5 %collective-permute-start.4 = (bf16[256,1024]{1,0:T(8,128)(2,1)}, bf16[256,1024]{1,0:T(8,128)(2,1)S(1)}, u32[]{:S(2)}, u32[]{:S(2)}) collective-permute-start(bf16[256,1024]{1,0:T(8,128)(2,1)} %bitcast_select_fusion), channel_id=1, source_target_pairs={{0,2},{1,3},{2,0},{3,1},{4,6},{5,7},{6,4},{7,5},{8,10},{9,11},{10,... | collective-permute-start | bytes 1572872 | tf_op jit(solution)/shard_map/ppermute | solution.py:528
  150.5 25.4 %collective-permute-start.7 = (bf16[256,1024]{1,0:T(8,128)(2,1)S(1)}, bf16[256,1024]{1,0:T(8,128)(2,1)S(1)}, u32[]{:S(2)}, u32[]{:S(2)}) collective-permute-start(bf16[256,1024]{1,0:T(8,128)(2,1)S(1)} %add_convert_fusion.11), channel_id=1, source_target_pairs={{0,2},{1,3},{2,0},{3,1},{4,6},{5,7},{6,4},{7,5},{8,10},{9,11},{10,... | collective-permute-start | bytes 1572872 | tf_op jit(solution)/shard_map/ppermute | solution.py:528
  151.1 24.6 %collective-permute-start.8 = (bf16[256,1024]{1,0:T(8,128)(2,1)}, bf16[256,1024]{1,0:T(8,128)(2,1)S(1)}, u32[]{:S(2)}, u32[]{:S(2)}) collective-permute-start(bf16[256,1024]{1,0:T(8,128)(2,1)} %bitcast_select_fusion.1), channel_id=1, source_target_pairs={{0,2},{1,3},{2,0},{3,1},{4,6},{5,7},{6,4},{7,5},{8,10},{9,11},{10,... | collective-permute-start | bytes 1572872 | tf_op jit(solution)/shard_map/ppermute | solution.py:528
  182.5 24.4 %collective-permute-start.12 = (bf16[256,1024]{1,0:T(8,128)(2,1)S(1)}, bf16[256,1024]{1,0:T(8,128)(2,1)S(1)}, u32[]{:S(2)}, u32[]{:S(2)}) collective-permute-start(bf16[256,1024]{1,0:T(8,128)(2,1)S(1)} %add_convert_fusion.9), channel_id=1, source_target_pairs={{0,2},{1,3},{2,0},{3,1},{4,6},{5,7},{6,4},{7,5},{8,10},{9,11},{10,... | collective-permute-start | bytes 1572872 | tf_op jit(solution)/shard_map/ppermute | solution.py:528
  231.2 22.7 %collective-permute-start.18 = (bf16[512,1024]{1,0:T(8,128)(2,1)S(1)}, bf16[512,1024]{1,0:T(8,128)(2,1)S(1)}, u32[]{:S(2)}, u32[]{:S(2)}) collective-permute-start(bf16[512,1024]{1,0:T(8,128)(2,1)S(1)} %get-tuple-element.258), channel_id=1, source_target_pairs={{0,1},{1,0},{2,3},{3,2},{4,5},{5,4},{6,7},{7,6},{8,9},{9,8},{10,11... | collective-permute-start | bytes 3145736 | tf_op jit(solution)/shard_map/ppermute | solution.py:528
  276.0 33.0 %collective-permute-start.24 = (bf16[512,1024]{1,0:T(8,128)(2,1)}, bf16[512,1024]{1,0:T(8,128)(2,1)}, u32[]{:S(2)}, u32[]{:S(2)}) collective-permute-start(bf16[512,1024]{1,0:T(8,128)(2,1)} %get-tuple-element.288), channel_id=1, source_target_pairs={{0,1},{1,0},{2,3},{3,2},{4,5},{5,4},{6,7},{7,6},{8,9},{9,8},{10,11... | collective-permute-start | bytes 3145736 | tf_op jit(solution)/shard_map/ppermute | solution.py:528
  278.2 27.8 %collective-permute-start.23 = (bf16[256,1024]{1,0:T(8,128)(2,1)S(1)}, bf16[256,1024]{1,0:T(8,128)(2,1)S(1)}, u32[]{:S(2)}, u32[]{:S(2)}) collective-permute-start(bf16[256,1024]{1,0:T(8,128)(2,1)S(1)} %add_convert_fusion.5), channel_id=1, source_target_pairs={{0,2},{1,3},{2,0},{3,1},{4,6},{5,7},{6,4},{7,5},{8,10},{9,11},{10,... | collective-permute-start | bytes 1572872 | tf_op jit(solution)/shard_map/ppermute | solution.py:528
  280.2 27.3 %collective-permute-start.22 = (bf16[256,1024]{1,0:T(8,128)(2,1)S(1)}, bf16[256,1024]{1,0:T(8,128)(2,1)S(1)}, u32[]{:S(2)}, u32[]{:S(2)}) collective-permute-start(bf16[256,1024]{1,0:T(8,128)(2,1)S(1)} %add_convert_fusion.6), channel_id=1, source_target_pairs={{0,2},{1,3},{2,0},{3,1},{4,6},{5,7},{6,4},{7,5},{8,10},{9,11},{10,... | collective-permute-start | bytes 1572872 | tf_op jit(solution)/shard_map/ppermute | solution.py:528
  333.2 49.2 %all-to-all-start.2 = ((bf16[8,32,1024]{2,1,0:T(8,128)(2,1)}), bf16[8,32,1024]{2,1,0:T(8,128)(2,1)}, u32[]{:S(2)}, u32[]{:S(2)}) async-start(bf16[8,32,1024]{2,1,0:T(8,128)(2,1)} %bitcast.247), calls=%async_computation.2 | async-start | bytes 1048576 | tf_op jit(solution)/shard_map/all_to_all | solution.py:604
  343.3 33.7 %collective-permute-start.30 = (bf16[4,128,256]{2,1,0:T(8,128)(2,1)S(1)}, bf16[4,128,256]{2,1,0:T(8,128)(2,1)S(1)}, u32[]{:S(2)}, u32[]{:S(2)}) collective-permute-start(bf16[4,128,256]{2,1,0:T(8,128)(2,1)S(1)} %dynamic-slice_bitcast_fusion.2), channel_id=1, source_target_pairs={{0,4},{4,0},{8,12},{12,8},{16,20},{20,16},{24,28},{28,24},{1,5},{5... | collective-permute-start | bytes 786440 | tf_op jit(solution)/shard_map/ppermute | solution.py:528
  346.4 31.4 %collective-permute-start.29 = (bf16[256,1024]{1,0:T(8,128)(2,1)S(1)}, bf16[256,1024]{1,0:T(8,128)(2,1)S(1)}, u32[]{:S(2)}, u32[]{:S(2)}) collective-permute-start(bf16[256,1024]{1,0:T(8,128)(2,1)S(1)} %add_convert_fusion.2), channel_id=1, source_target_pairs={{0,2},{1,3},{2,0},{3,1},{4,6},{5,7},{6,4},{7,5},{8,10},{9,11},{10,... | collective-permute-start | bytes 1572872 | tf_op jit(solution)/shard_map/ppermute | solution.py:528
  348.3 31.8 %collective-permute-start.28 = (bf16[256,1024]{1,0:T(8,128)(2,1)S(1)}, bf16[256,1024]{1,0:T(8,128)(2,1)S(1)}, u32[]{:S(2)}, u32[]{:S(2)}) collective-permute-start(bf16[256,1024]{1,0:T(8,128)(2,1)S(1)} %add_convert_fusion.3), channel_id=1, source_target_pairs={{0,2},{1,3},{2,0},{3,1},{4,6},{5,7},{6,4},{7,5},{8,10},{9,11},{10,... | collective-permute-start | bytes 1572872 | tf_op jit(solution)/shard_map/ppermute | solution.py:528
  411.2 20.3 %collective-permute-start.40 = (bf16[1,128,256]{2,1,0:T(8,128)(2,1)S(1)}, bf16[1,128,256]{2,1,0:T(8,128)(2,1)}, u32[]{:S(2)}, u32[]{:S(2)}) collective-permute-start(bf16[1,128,256]{2,1,0:T(8,128)(2,1)S(1)} %dynamic-slice_convert_fusion.2), channel_id=1, source_target_pairs={{0,16},{4,20},{8,24},{12,28},{16,0},{20,4},{24,8},{28,12},{1,17},{... | collective-permute-start | bytes 196616 | tf_op jit(solution)/shard_map/ppermute | solution.py:528
  417.0 39.9 %collective-permute-start.41 = (bf16[256,1024]{1,0:T(8,128)(2,1)}, bf16[256,1024]{1,0:T(8,128)(2,1)}, u32[]{:S(2)}, u32[]{:S(2)}) collective-permute-start(bf16[256,1024]{1,0:T(8,128)(2,1)} %bitcast.40), channel_id=1, source_target_pairs={{0,2},{1,3},{2,0},{3,1},{4,6},{5,7},{6,4},{7,5},{8,10},{9,11},{10,... | collective-permute-start | bytes 1572872 | tf_op jit(solution)/shard_map/ppermute | solution.py:528
  418.7 41.4 %all-to-all-start.4 = ((bf16[8,64,1024]{2,1,0:T(8,128)(2,1)}), bf16[8,64,1024]{2,1,0:T(8,128)(2,1)}, u32[]{:S(2)}, u32[]{:S(2)}) async-start(bf16[8,64,1024]{2,1,0:T(8,128)(2,1)} %bitcast.238), calls=%async_computation.5 | async-start | bytes 2097152 | tf_op jit(solution)/shard_map/all_to_all | solution.py:604
  433.4 22.4 %collective-permute-start.37 = (bf16[1,128,384]{2,1,0:T(8,128)(2,1)S(1)}, bf16[1,128,384]{2,1,0:T(8,128)(2,1)S(1)}, u32[]{:S(2)}, u32[]{:S(2)}) collective-permute-start(bf16[1,128,384]{2,1,0:T(8,128)(2,1)S(1)} %dynamic-slice_convert_fusion.1), channel_id=1, source_target_pairs={{0,16},{4,20},{8,24},{12,28},{16,0},{20,4},{24,8},{28,12},{1,17},{... | collective-permute-start | bytes 294920 | tf_op jit(solution)/shard_map/ppermute | solution.py:528
  435.0 21.9 %collective-permute-start.39 = (bf16[1,128,384]{2,1,0:T(8,128)(2,1)S(1)}, bf16[1,128,384]{2,1,0:T(8,128)(2,1)S(1)}, u32[]{:S(2)}, u32[]{:S(2)}) collective-permute-start(bf16[1,128,384]{2,1,0:T(8,128)(2,1)S(1)} %dynamic-slice_convert_fusion), channel_id=1, source_target_pairs={{0,16},{4,20},{8,24},{12,28},{16,0},{20,4},{24,8},{28,12},{1,17},{... | collective-permute-start | bytes 294920 | tf_op jit(solution)/shard_map/ppermute | solution.py:528
  504.3 26.4 %collective-permute-start.47 = (bf16[2,1024,256]{2,1,0:T(8,128)(2,1)}, bf16[2,1024,256]{2,1,0:T(8,128)(2,1)}, u32[]{:S(2)}, u32[]{:S(2)}) collective-permute-start(bf16[2,1024,256]{2,1,0:T(8,128)(2,1)} %pad_maximum_fusion.13.near_ref), channel_id=1, source_target_pairs={{0,1},{1,0},{2,3},{3,2},{4,5},{5,4},{6,7},{7,6},{8,9},{9,8},{10,11... | collective-permute-start | bytes 3145736 | tf_op jit(solution)/shard_map/ppermute | solution.py:528
  524.2 26.0 %collective-permute-start.50 = (bf16[256,1024]{1,0:T(8,128)(2,1)}, bf16[256,1024]{1,0:T(8,128)(2,1)}, u32[]{:S(2)}, u32[]{:S(2)}) collective-permute-start(bf16[256,1024]{1,0:T(8,128)(2,1)} %bitcast.249), channel_id=1, source_target_pairs={{0,2},{1,3},{2,0},{3,1},{4,6},{5,7},{6,4},{7,5},{8,10},{9,11},{10,... | collective-permute-start | bytes 1572872 | tf_op jit(solution)/shard_map/ppermute | solution.py:528
  542.2 30.9 %collective-permute-start.54 = (bf16[2,1024,256]{2,1,0:T(8,128)(2,1)}, bf16[2,1024,256]{2,1,0:T(8,128)(2,1)}, u32[]{:S(2)}, u32[]{:S(2)}) collective-permute-start(bf16[2,1024,256]{2,1,0:T(8,128)(2,1)} %pad_maximum_fusion.14.near_ref), channel_id=1, source_target_pairs={{0,1},{1,0},{2,3},{3,2},{4,5},{5,4},{6,7},{7,6},{8,9},{9,8},{10,11... | collective-permute-start | bytes 3145736 | tf_op jit(solution)/shard_map/ppermute | solution.py:528
  542.9 27.8 %collective-permute-start.48 = (bf16[256,1024]{1,0:T(8,128)(2,1)}, bf16[256,1024]{1,0:T(8,128)(2,1)}, u32[]{:S(2)}, u32[]{:S(2)}) collective-permute-start(bf16[256,1024]{1,0:T(8,128)(2,1)} %bitcast.85), channel_id=1, source_target_pairs={{0,2},{1,3},{2,0},{3,1},{4,6},{5,7},{6,4},{7,5},{8,10},{9,11},{10,... | collective-permute-start | bytes 1572872 | tf_op jit(solution)/shard_map/ppermute | solution.py:528
  544.3 24.5 %collective-permute-start.52 = (bf16[256,1024]{1,0:T(8,128)(2,1)}, bf16[256,1024]{1,0:T(8,128)(2,1)}, u32[]{:S(2)}, u32[]{:S(2)}) collective-permute-start(bf16[256,1024]{1,0:T(8,128)(2,1)} %bitcast.84), channel_id=1, source_target_pairs={{0,2},{1,3},{2,0},{3,1},{4,6},{5,7},{6,4},{7,5},{8,10},{9,11},{10,... | collective-permute-start | bytes 1572872 | tf_op jit(solution)/shard_map/ppermute | solution.py:528
  552.1 57.4 %collective-permute-start.51 = (bf16[512,1024]{1,0:T(8,128)(2,1)}, bf16[512,1024]{1,0:T(8,128)(2,1)}, u32[]{:S(2)}, u32[]{:S(2)}) collective-permute-start(bf16[512,1024]{1,0:T(8,128)(2,1)} %constant_dynamic-update-slice_fusion.2.near_ref), channel_id=1, source_target_pairs={{0,1},{1,0},{2,3},{3,2},{4,5},{5,4},{6,7},{7,6},{8,9},{9,8},{10,11... | collective-permute-start | bytes 3145736 | tf_op jit(solution)/shard_map/ppermute | solution.py:528
  570.7 28.3 %collective-permute-start.53 = (bf16[512,1024]{1,0:T(8,128)(2,1)}, bf16[512,1024]{1,0:T(8,128)(2,1)}, u32[]{:S(2)}, u32[]{:S(2)}) collective-permute-start(bf16[512,1024]{1,0:T(8,128)(2,1)} %constant_dynamic-update-slice_fusion.4.near_ref), channel_id=1, source_target_pairs={{0,1},{1,0},{2,3},{3,2},{4,5},{5,4},{6,7},{7,6},{8,9},{9,8},{10,11... | collective-permute-start | bytes 3145736 | tf_op jit(solution)/shard_map/ppermute | solution.py:528
  572.6 31.6 %collective-permute-start.49 = (bf16[512,1024]{1,0:T(8,128)(2,1)}, bf16[512,1024]{1,0:T(8,128)(2,1)}, u32[]{:S(2)}, u32[]{:S(2)}) collective-permute-start(bf16[512,1024]{1,0:T(8,128)(2,1)} %constant_dynamic-update-slice_fusion.near_ref), channel_id=1, source_target_pairs={{0,1},{1,0},{2,3},{3,2},{4,5},{5,4},{6,7},{7,6},{8,9},{9,8},{10,11... | collective-permute-start | bytes 3145736 | tf_op jit(solution)/shard_map/ppermute | solution.py:528
  (161 other events, 1412.6 us)
Sparse Core Ops, SparseCore 0:
  27.8 77.8 all-gather.2
  113.8 72.1 all-gather.4
  276.6 94.0 reduce-scatter.1

commit v4 on v3

--- a/solution.py
+++ b/solution.py
@@ -60,7 +60,7 @@
 
 TILE = 256
 STRIP = 64
-VMEM_BYTES = 24 * 1024 * 1024
+VMEM_BYTES = 20 * 1024 * 1024
 SMALL = pl.CostEstimate(flops=10**9, bytes_accessed=10**6, transcendentals=0)
 LARGE = pl.CostEstimate(flops=20 * 10**9, bytes_accessed=10**6, transcendentals=0)
 MEDIUM = pl.CostEstimate(flops=11 * 10**9, bytes_accessed=10**6, transcendentals=0)
@@ -339,22 +339,23 @@
         in_specs=[whole_spec()] * len(pieces),
         out_specs=whole_spec(),
         compiler_params=pltpu.CompilerParams(vmem_limit_bytes=VMEM_BYTES),
-        cost_estimate=MEDIUM,
+        cost_estimate=MEDIUM if cols > 1024 else SMALL,
     )(*pieces)
 
 
 def slots_kernel(cols, slot_count, block_ref, *refs):
-    outs, held = refs[-1 - slot_count : -1], refs[-1]
+    *parts, out, held = refs
+    rows = held.shape[0]
     start = 0
-    for part in refs[: -1 - slot_count]:
+    for part in parts:
         held[:, start : start + part.shape[1]] = part[...]
         start = start + part.shape[1]
     for s in range(block_ref.shape[0]):
-        out = outs[s % slot_count]
         block = block_ref[s]
         lanes = pl.ds(pl.multiple_of(jnp.maximum(block, 0) * cols, cols), cols)
-        rows = held[:, lanes]
-        out[s // slot_count] = jnp.where(block >= 0, rows, jnp.zeros_like(rows))
+        taken = held[:, lanes]
+        at = s % slot_count * rows
+        out[s // slot_count, at : at + rows, :] = jnp.where(block >= 0, taken, jnp.zeros_like(taken))
 
 
 def to_slots(block_of, slot_count, cols, *parts):
@@ -363,11 +364,9 @@
     width = sum(part.shape[1] for part in parts)
     return pl.pallas_call(
         functools.partial(slots_kernel, cols, slot_count),
-        out_shape=tuple(
-            [jax.ShapeDtypeStruct((count, rows, cols), low_type) for _ in range(slot_count)]
-        ),
+        out_shape=jax.ShapeDtypeStruct((count, slot_count * rows, cols), low_type),
         in_specs=[pl.BlockSpec(memory_space=pltpu.SMEM)] + [whole_spec()] * len(parts),
-        out_specs=tuple([whole_spec()] * slot_count),
+        out_specs=whole_spec(),
         scratch_shapes=[pltpu.VMEM((rows, width), low_type)],
         compiler_params=pltpu.CompilerParams(vmem_limit_bytes=VMEM_BYTES),
         cost_estimate=SMALL,
@@ -407,86 +406,71 @@
     )(block_of, first, second)
 
 
-def precondition_kernel(slot, order, count, place_ref, near_ref, far_ref, *refs):
-    stats_refs = refs[:4]
-    new_left_ref, new_right_ref, direction_ref, square_ref = refs[4 + count : 8 + count]
-    halfway_ref, left_ref, right_ref, left_root_ref, right_root_ref, sems = refs[8 + count :]
-    held = (left_ref, right_ref, left_root_ref, right_root_ref)
-    copies = [
-        pltpu.make_async_copy(source.at[slot], target, sems.at[k])
-        for k, (source, target) in enumerate(zip(stats_refs, held))
+def precondition_kernel(
+    order, place_ref, near_ref, far_ref, left_ref, right_ref, left_root_ref, right_root_ref, *refs
+):
+    new_left_ref, new_right_ref, direction_ref, square_ref, halfway_ref = refs
+    count, parts, rows_part, cols = near_ref.shape
+    width = parts * rows_part
+    rows = left_ref.shape[1]
+    place = place_ref[0]
+    pieces = [
+        ref[k].reshape(width, cols) for ref in (near_ref, far_ref) for k in range(count)
     ]
-    for k in (3, 2, 0, 1):
-        copies[k].start()
-    cols = near_ref.shape[2]
-    rows = left_ref.shape[0]
-    width = near_ref.shape[1]
-    place = place_ref[0]
-    own_rows = pl.ds(pl.multiple_of(place * rows, rows), rows)
-    pieces = [ref.at[k] for ref in (near_ref, far_ref) for k in range(near_ref.shape[0])]
     lanes = [pl.ds(pl.multiple_of((place ^ j) * cols, cols), cols) for j in order]
-    copies[3].wait()
     halfway = 0.0
     for at, piece in zip(lanes, pieces):
-        halfway = halfway + dot_nt(piece[...], right_root_ref[:, at].astype(low_type))
+        halfway = halfway + dot_nt(piece, right_root_ref[0, :, at].astype(low_type))
     halfway_ref[...] = halfway.astype(low_type)
-    copies[2].wait()
     total = 0.0
     for t in range(width // TILE):
         here = slice(t * TILE, (t + 1) * TILE)
-        part = dot(left_root_ref[here, :].astype(low_type), halfway_ref[...])
-        direction_ref[here, :] = part
+        part = dot(left_root_ref[0, here, :].astype(low_type), halfway_ref[...])
+        direction_ref[0, here, :] = part
         total = total + jnp.sum(part * part, axis=0, keepdims=True)
-    square_ref[...] = total
-    copies[0].wait()
-    left = stat_decay * left_ref[...]
-    for piece in pieces:
-        left = left + dot_nt(piece[own_rows, :], piece[...])
+    square_ref[0] = total
+    left = stat_decay * left_ref[0]
+    groups = rows // rows_part
+    for g, piece in enumerate(pieces):
+        ref = near_ref if g < count else far_ref
+        own = ref[g % count, pl.ds(place * groups, groups)].reshape(rows, cols)
+        left = left + dot_nt(own, piece)
     new_left_ref[0] = left
-    copies[1].wait()
     for at, piece in zip(lanes, pieces):
-        new_right_ref[0, :, at] = stat_decay * right_ref[:, at] + dot_tn(
-            pieces[0][...], piece[...]
-        )
-
-
-def precondition(s, place, near, far, stats, before):
+        new_right_ref[0, :, at] = stat_decay * right_ref[0, :, at] + dot_tn(pieces[0], piece)
+
+
+def precondition(place, near, far, stats):
     slot_count, rows, width = stats[0].shape
-    cols = near.shape[2]
+    count, parts, held_rows, cols = near.shape
+    rows_part = held_rows // slot_count
     shape = jax.ShapeDtypeStruct
 
-    def of_slot(array):
-        return pl.BlockSpec((1,) + array.shape[1:], lambda i: (s, 0, 0))
-
-    def all_of(dims):
-        return pl.BlockSpec(dims, lambda i: (0,) * len(dims))
-
+    def of_slot(dims):
+        return pl.BlockSpec((1,) + dims[1:], lambda s: (s, 0, 0))
+
+    pieces_spec = pl.BlockSpec((count, parts, rows_part, cols), lambda s: (0, 0, s, 0))
     return pl.pallas_call(
-        functools.partial(
-            precondition_kernel, s, near_order(lax.axis_size("mp")), len(before)
-        ),
-        grid=(1,),
+        functools.partial(precondition_kernel, near_order(lax.axis_size("mp"))),
+        grid=(slot_count,),
         out_shape=(
             shape(stats[0].shape, f32),
             shape(stats[1].shape, f32),
-            shape((width, cols), f32),
-            shape((1, cols), f32),
+            shape((slot_count, width, cols), f32),
+            shape((slot_count, 1, cols), f32),
         ),
-        in_specs=[pl.BlockSpec(memory_space=pltpu.SMEM), all_of(near.shape), all_of(far.shape)]
-        + [pl.BlockSpec(memory_space=pl.ANY)] * (4 + len(before)),
+        in_specs=[pl.BlockSpec(memory_space=pltpu.SMEM), pieces_spec, pieces_spec]
+        + [of_slot(array.shape) for array in stats],
         out_specs=(
-            of_slot(stats[0]),
-            of_slot(stats[1]),
-            all_of((width, cols)),
-            all_of((1, cols)),
+            of_slot(stats[0].shape),
+            of_slot(stats[1].shape),
+            of_slot((slot_count, width, cols)),
+            of_slot((slot_count, 1, cols)),
         ),
-        input_output_aliases={7 + k: k for k in range(len(before))},
-        scratch_shapes=[pltpu.VMEM((width, cols), low_type)]
-        + [pltpu.VMEM(array.shape[1:], f32) for array in stats]
-        + [pltpu.SemaphoreType.DMA((4,))],
-        compiler_params=pltpu.CompilerParams(vmem_limit_bytes=VMEM_BYTES),
-        cost_estimate=SMALL,
-    )(place, near, far, *stats, *before)
+        scratch_shapes=[pltpu.VMEM((width, cols), low_type)],
+        compiler_params=pltpu.CompilerParams(vmem_limit_bytes=2 * VMEM_BYTES),
+        cost_estimate=MEDIUM,
+    )(place, near, far, *stats)
 
 
 def give_back_kernel(slot_ref, near_ref, far_ref, *refs):
@@ -592,8 +576,7 @@
     return blocks[0].astype(low_type)
 
 
-def sum_over(values, axis):
-    bit = 1
+def sum_over(values, axis, bit=1):
     while bit < lax.axis_size(axis):
         values = values + swap(values, axis, bit)
         bit *= 2
@@ -852,16 +835,18 @@
     normed_back_1 = scatter_chips(keep_1, core_1)
     input_0, first_sums_0 = first_back(0, hidden_grad_0, normed_back_0)
     output_1 = (hidden_1 + output_1 + norms[5]).astype(low_type)
+    input_0, output_1 = exchange_back([input_0, output_1])
     cut = 3 * local_cols // 2 // 128 * 128
     grads_one = [
         scatter_step(part.reshape(data_count, shard_rows, -1), 1)
         for part in (grads_qkv[:, :cut], grads_qkv[:, cut:])
     ]
     blocks_out = scatter_step(blocks_out, 2)
+    output_0 = gather_chips(output_0)
     normed_back_1, grads_one, input_0, output_1, output_0, blocks_out = together(
         normed_back_1, grads_one, input_0, output_1, output_0, blocks_out
     )
-    input_0, output_1 = exchange_back([input_0, output_1])
+    input_0, output_1 = gather_chips(input_0), gather_chips(output_1)
     input_1, first_sums_1 = first_back(1, hidden_grad_1, normed_back_1)
     summed_one = [scatter_grads(part, 2) for part in (*grads_one,)]
     summed_one.append(scatter_grads(blocks_out, 4))
@@ -871,41 +856,23 @@
     qkv_sums = sums_0 + sums_1
     up_sums = [*up_sums_0, *up_sums_1]
 
-    norm_grads_sum = sum_over(norm_grads_own, "mp")
-    output_0 = gather_chips(output_0)
-    summed_one, output_0, norm_grads_sum, input_1 = together(
-        summed_one, output_0, norm_grads_sum, input_1
-    )
-    slotted = to_slots(block_of, slot_count, local_cols, *summed_one, summed_two)
+    summed_one, input_1, norm_grads_own = together(summed_one, input_1, norm_grads_own)
+    owned = exchange(
+        to_slots(block_of, slot_count, local_cols, *summed_one, summed_two)
+    )
     stats = (left_stats, right_stats, left_roots, right_roots)
     place = model_index.astype(jnp.int32).reshape(1)
     returns = [return_slots(i) for i in micros]
-
-    def own_slot(s):
-        return exchange(slotted[s]).reshape(1, model_width, local_cols)
-
-    owned_0 = own_slot(0)
     outputs_given = give_back(0, returns[0], output_0, other_core(output_0), micro_count, [])
-    owned_0, outputs_given, slotted, input_0, output_1 = together(
-        owned_0, outputs_given, slotted, input_0, output_1
-    )
-    near_0 = gather_chips(owned_0)
-    owned = [owned_0] + [own_slot(s) for s in range(1, slot_count)]
-    near_0, owned, input_1, input_0, output_1 = together(
-        near_0, owned, input_1, input_0, output_1
+    inputs_given = give_back(0, returns[0], input_0, other_core(input_0), micro_count, [])
+    outputs_given = give_back(
+        1, returns[1], output_1, other_core(output_1), micro_count, outputs_given
+    )
+    norm_grads_sum = sum_over(norm_grads_own, "mp")
+    owned, outputs_given, inputs_given, norm_grads_sum, input_1 = together(
+        owned, outputs_given, inputs_given, norm_grads_sum, input_1
     )
     input_1 = exchange_back([input_1])[0]
-    far_0 = other_core(near_0)
-    *fresh, direction, square = precondition(0, place, near_0, far_0, stats, [])
-    directions, squares = [direction], [square]
-    for s in range(1, slot_count):
-        near_part = gather_chips(owned[s])
-        near_part, fresh, input_0, output_1 = together(near_part, fresh, input_0, output_1)
-        *fresh, direction, square = precondition(
-            s, place, near_part, other_core(near_part), stats, fresh
-        )
-        directions.append(direction)
-        squares.append(square)
     head_own = jnp.concatenate(
         [
             qkv_sums[:, :local_cols],
@@ -915,25 +882,26 @@
         axis=0,
     )
     vectors = jnp.concatenate([norm_grads_sum, head_own], axis=1)
-    vectors, input_1 = together(vectors, input_1)
+    owned_grads = owned.reshape(data_count, slot_count, shard_rows, local_cols)
+    owned_grads = jnp.swapaxes(owned_grads, 1, 2).reshape(model_width, slot_count, local_cols)
+    owned_grads = owned_grads.astype(f32)
+    near_part = gather_chips(owned[None])
+    near_part, input_1, owned_grads = together(near_part, input_1, owned_grads)
+    far_part = other_core(near_part)
+    new_left, new_right, directions, squares = precondition(place, near_part, far_part, stats)
+    squares, input_1, vectors = together(squares, input_1, vectors)
+    input_1 = gather_chips(input_1)
     vectors = sum_over(vectors, "dp")
+    inputs_given = give_back(
+        1, returns[1], input_1, other_core(input_1), micro_count, inputs_given
+    )[0]
+    outputs_given = outputs_given[0]
     norm_all = vectors[:, :model_width]
     head_total = vectors[:, model_width:]
     norm_cols = norm_vectors.shape[1]
     norm_total = lax.dynamic_slice_in_dim(norm_all, data_index * norm_cols, norm_cols, 1)
-
-    input_0, output_1, input_1 = [gather_chips(rows) for rows in (input_0, output_1, input_1)]
-    inputs_given = give_back(0, returns[0], input_0, other_core(input_0), micro_count, [])
-    outputs_given = give_back(
-        1, returns[1], output_1, other_core(output_1), micro_count, outputs_given
-    )
-    inputs_given = give_back(
-        1, returns[1], input_1, other_core(input_1), micro_count, inputs_given
-    )[0]
-    outputs_given = outputs_given[0]
-    new_left, new_right = fresh
-    squares = [jnp.sum(square) for square in squares]
-    square_total = sum_over(jnp.stack(squares).reshape(1, slot_count), "mp")[0]
+    squares = jnp.sum(squares, axis=(1, 2))
+    square_total = sum_over(squares.reshape(1, slot_count), "mp")[0]
     factor = lax.rsqrt(square_total / (model_width * model_width) + mean_eps)
     updated_blocks = jnp.stack(
         [
@@ -942,7 +910,6 @@
         ],
         axis=1,
     )
-    owned_grads = jnp.stack([rows[0] for rows in owned], axis=1).astype(f32)
     new_norm_state = stat_decay * norm_state + norm_total * norm_total
     new_norm_vectors = norm_vectors - vector_rate * norm_total / (
         jnp.sqrt(new_norm_state) + diag_eps

time: 630 us -> 584 us (0.927)
  waiting for transfers between devices: 201 us -> 181 us
  local copies, waits for them, and re-layouts: 77.1 us -> 68.6 us
  other arithmetic: 78.9 us -> 70.9 us
    all_to_all x7 -> x6, waiting for transfers between devices: 59.7 us -> 45.3 us  [exchange(): return lax.all_to_all(rows, 'dp', split_axis=0, concat_axis=0, tiled=True)]
    unnamed x259 -> x242, local copies, waits for them, and re-layouts: 51.3 us -> 42.8 us
    ppermute x60 -> x58, waiting for transfers between devices: 140 us -> 135 us  [swap(): return lax.ppermute(values, axis, [(i, i ^ bit) for i in range(count)])]
    pallas_call x2 -> x1, Pallas kernels: 14.3 us -> 10.7 us  [precondition(): pl.pallas_call(functools.partial(precondition_kernel, near_order(lax.axis...]
    all_to_all x7 -> x6, starting transfers between devices: 34.9 us -> 31.9 us  [exchange(): return lax.all_to_all(rows, 'dp', split_axis=0, concat_axis=0, tiled=True)]
    ppermute x60 -> x58, starting transfers between devices: 46.3 us -> 45.6 us  [swap(): return lax.ppermute(values, axis, [(i, i ^ bit) for i in range(count)])]
  transfers between devices with their start and end apart: 70 -> 67, of which waited for: 27 -> 26; matrix products, arithmetic and copies ran while one was open for 18% -> 17% of each run, Pallas kernels for 23% -> 23%
where the time goes in v4:
time: 584 us; the launch traced here: 575 us
  waiting for transfers between devices  181 us (31%)
  Pallas kernels  151 us (26%)
  starting transfers between devices  77.7 us (13%)
  other arithmetic  70.9 us (12%)
  local copies, waits for them, and re-layouts  68.6 us (12%)
  between operations  17.8 us (3%)
  matrix products  9.24 us (2%)
    ppermute x58, waiting for transfers between devices, swap(): return lax.ppermute(values, axis, [(i, i ^ bit) for i in range(count)])  135 us
    ppermute x58, starting transfers between devices, swap(): return lax.ppermute(values, axis, [(i, i ^ bit) for i in range(count)])  45.6 us
    all_to_all x6, waiting for transfers between devices, exchange(): return lax.all_to_all(rows, 'dp', split_axis=0, concat_axis=0, tiled=True)  45.3 us
    pallas_call x2, Pallas kernels, attention_backward(): pl.pallas_call(attention_backward_kernel, out_shape=(shape((rows // 2, wi...  43.2 us
    unnamed x242, local copies, waits for them, and re-layouts  42.8 us
    pallas_call x2, Pallas kernels, attention_forward(): pl.pallas_call(attention_forward_kernel, out_shape=(shape((rows // 2, wid...  35.6 us
    all_to_all x6, starting transfers between devices, exchange(): return lax.all_to_all(rows, 'dp', split_axis=0, concat_axis=0, tiled=True)  31.9 us
    pallas_call x4, Pallas kernels, mlp(): pl.pallas_call(mlp_kernel, out_shape=(shape((rows, cols), low_type), shap...  23.5 us
  transfers between devices with their start and end apart: 67, of which 26 were waited for; matrix products, arithmetic and copies ran while one was open for 17% of the time, Pallas kernels for 23%

profile of v4, /device:TPU:0, one launch (start us, length us, event | category | flops | bytes accessed | tf_op | source)
XLA Modules:
  0.0 575.4 jit_solution(5106004327531907282)
XLA Ops:
  16.1 7.3 %all-to-all-start = ((bf16[8,64,1024]{2,1,0:T(8,128)(2,1)}), bf16[8,64,1024]{2,1,0:T(8,128)(2,1)S(1)}, u32[]{:S(2)}, u32[]{:S(2)}) async-start(bf16[8,64,1024]{2,1,0:T(8,128)(2,1)} %pad_maximum_fusion.3), calls=%async_computation | async-start | bytes 2097152 | tf_op jit(solution)/shard_map/all_to_all | solution.py:587
  27.2 31.5 %all-to-all-done = bf16[8,64,1024]{2,1,0:T(8,128)(2,1)S(1)} async-done(((bf16[8,64,1024]{2,1,0:T(8,128)(2,1)}), bf16[8,64,1024]{2,1,0:T(8,128)(2,1)S(1)}, u32[]{:S(2)}, u32[]{:S(2)}) %all-to-all-start) | async-done | bytes 1048608 | tf_op jit(solution)/shard_map/all_to_all | solution.py:587
  63.7 6.0 %collective-permute-done = bf16[256,1024]{1,0:T(8,128)(2,1)S(1)} collective-permute-done((bf16[256,1024]{1,0:T(8,128)(2,1)S(1)}, bf16[256,1024]{1,0:T(8,128)(2,1)S(1)}, u32[]{:S(2)}, u32[]{:S(2)}) %collective-permute-start) | collective-permute-done | bytes 524320 | tf_op jit(solution)/shard_map/ppermute | solution.py:512
  69.8 5.4 all-to-all-start.1
  81.8 8.5 %collective-permute-done.1 = bf16[256,1024]{1,0:T(8,128)(2,1)S(1)} collective-permute-done((bf16[256,1024]{1,0:T(8,128)(2,1)S(1)}, bf16[256,1024]{1,0:T(8,128)(2,1)S(1)}, u32[]{:S(2)}, u32[]{:S(2)}) %collective-permute-start.1) | collective-permute-done | bytes 524320 | tf_op jit(solution)/shard_map/ppermute | solution.py:512
  94.6 13.9 %all-to-all-done.1 = bf16[8,64,1024]{2,1,0:T(8,128)(2,1)} async-done(((bf16[8,64,1024]{2,1,0:T(8,128)(2,1)}), bf16[8,64,1024]{2,1,0:T(8,128)(2,1)}, u32[]{:S(2)}, u32[]{:S(2)}) %all-to-all-start.1) | async-done | bytes 1048608 | tf_op jit(solution)/shard_map/all_to_all | solution.py:587
  119.7 19.0 %shard_map.266 = (f32[512,1024]{1,0:T(8,128)S(1)}, bf16[512,1024]{1,0:T(8,128)(2,1)}, bf16[1024,1024]{1,0:T(8,128)(2,1)S(1)}, bf16[1024,256]{1,0:T(8,128)(2,1)S(...) custom-call(bf16[512,1024]{1,0:T(8,128)(2,1)S(1)} %pad_maximum_fusion.4.near_ref, ...), custom_call_target="tpu_custom_call" | custom-call | flops 20000000000 | bytes 1000000 | tf_op jit(solution)/shard_map/pallas_call | solution.py:152
  153.1 16.5 %shard_map.265 = (f32[512,1024]{1,0:T(8,128)S(1)}, bf16[512,1024]{1,0:T(8,128)(2,1)S(1)}, bf16[1024,1024]{1,0:T(8,128)(2,1)S(1)}, bf16[1024,256]{1,0:T(8,128)(2,...) custom-call(bf16[512,1024]{1,0:T(8,128)(2,1)S(1)} %copy-done.30, ...), custom_call_target="tpu_custom_call" | custom-call | flops 20000000000 | bytes 1000000 | tf_op jit(solution)/shard_map/pallas_call | solution.py:152
  183.3 12.5 %collective-permute-done.11 = bf16[256,1024]{1,0:T(8,128)(2,1)S(1)} collective-permute-done((bf16[256,1024]{1,0:T(8,128)(2,1)S(1)}, bf16[256,1024]{1,0:T(8,128)(2,1)S(1)}, u32[]{:S(2)}, u32[]{:S(2)}) %collective-permute-start.11) | collective-permute-done | bytes 524320 | tf_op jit(solution)/shard_map/ppermute | solution.py:512
  196.9 9.4 %collective-permute-done.12 = bf16[256,1024]{1,0:T(8,128)(2,1)S(1)} collective-permute-done((bf16[256,1024]{1,0:T(8,128)(2,1)S(1)}, bf16[256,1024]{1,0:T(8,128)(2,1)S(1)}, u32[]{:S(2)}, u32[]{:S(2)}) %collective-permute-start.12) | collective-permute-done | bytes 524320 | tf_op jit(solution)/shard_map/ppermute | solution.py:512
  210.8 5.2 shard_map.267
  217.4 5.6 collective-permute-done.14
  223.0 6.8 %shard_map.268 = (bf16[512,1024]{1,0:T(8,128)(2,1)S(1)}, bf16[512,1024]{1,0:T(8,128)(2,1)S(1)}, bf16[512,1024]{1,0:T(8,128)(2,1)S(1)}, bf16[512,1024]{1,0:T(8,128)(2,1)S(1)}, f32[1,1024]{1,0:T(1,128)S(1)}) custom-call(bf16[512,1024]{1,0:T(8,128)(2,1)S(1)} %collective-permute-done.13.normed_ref.refs_1_, ...), custom_call_target="tpu_custom_call" | custom-call | flops 11000000512 | bytes 1000000 | tf_op jit(solution)/shard_map/pallas_call | solution.py:291
  230.5 5.2 shard_map.269
  239.0 6.3 %shard_map.270 = (bf16[512,1024]{1,0:T(8,128)(2,1)S(1)}, bf16[512,1024]{1,0:T(8,128)(2,1)S(1)}, bf16[512,1024]{1,0:T(8,128)(2,1)}, bf16[512,1024]{1,0:T(8,128)(2,1)}, f32[1,1024]{1,0:T(1,128)S(1)}) custom-call(bf16[512,1024]{1,0:T(8,128)(2,1)S(1)} %collective-permute-done.15.normed_ref.refs_3_, bf16[512,1024]{1,0:T(8,128)(2,1)S(1)} %copy-done.51, ...), custom_call_target="tpu_custom_call" | custom-call | flops 11000000512 | bytes 1000000 | tf_op jit(solution)/shard_map/pallas_call | solution.py:291
  245.4 6.2 %collective-permute-done.17 = bf16[256,1024]{1,0:T(8,128)(2,1)S(1)} collective-permute-done((bf16[256,1024]{1,0:T(8,128)(2,1)S(1)}, bf16[256,1024]{1,0:T(8,128)(2,1)S(1)}, u32[]{:S(2)}, u32[]{:S(2)}) %collective-permute-start.17) | collective-permute-done | bytes 524320 | tf_op jit(solution)/shard_map/ppermute | solution.py:512
  254.7 10.1 %shard_map.271 = bf16[1024,2048]{1,0:T(8,128)(2,1)S(1)} custom-call(bf16[512,1024]{1,0:T(8,128)(2,1)S(1)} %copy-done.28, bf16[512,1024]{1,0:T(8,128)(2,1)S(1)} %collective-permute-done.13.normed_ref.refs_1_, bf16[512,1024]{1,0:T(8,128)(2,1)S(1)} %pad_maximum_fusion.9.normed_ref.refs_2_, bf16[512,1024]{1,0:T(8,128)(2,1)S(1)} %collective-permute-done.15.normed_ref.refs_3_, ...), custom_call_target="tpu_custom_call" | custom-call | flops 11000000512 | bytes 1000000 | tf_op jit(solution)/shard_map/pallas_call | solution.py:336
  281.2 22.9 %shard_map.273 = (f32[512,1024]{1,0:T(8,128)S(1)}, bf16[512,1024]{1,0:T(8,128)(2,1)}, bf16[1024,768]{1,0:T(8,128)(2,1)S(1)}, f32[1,768]{1,0:T(1,128)S(1)}) custom-call(bf16[512,1024]{1,0:T(8,128)(2,1)S(1)} %pad_maximum_fusion.10.near_ref.refs_0_, bf16[512,1024]{1,0:T(8,128)(2,1)} %collective-permute-done.21.far_ref.refs_1_, ...), custom_call_target="tpu_custom_call" | custom-call | flops 20000000000 | bytes 1000000 | tf_op jit(solution)/shard_map/pallas_call | solution.py:243
  313.8 11.3 %collective-permute-done.25 = bf16[256,1024]{1,0:T(8,128)(2,1)} collective-permute-done((bf16[256,1024]{1,0:T(8,128)(2,1)}, bf16[256,1024]{1,0:T(8,128)(2,1)}, u32[]{:S(2)}, u32[]{:S(2)}) %collective-permute-start.25) | collective-permute-done | bytes 524320 | tf_op jit(solution)/shard_map/ppermute | solution.py:512
  329.5 4.5 all-to-all-start.2
  345.5 20.3 %shard_map.275 = (f32[512,1024]{1,0:T(8,128)S(1)}, bf16[512,1024]{1,0:T(8,128)(2,1)S(1)}, bf16[1024,768]{1,0:T(8,128)(2,1)S(1)}, f32[1,768]{1,0:T(1,128)S(1)}) custom-call(bf16[512,1024]{1,0:T(8,128)(2,1)S(1)} %pad_maximum_fusion.11.refs_2_.near_ref, bf16[512,1024]{1,0:T(8,128)(2,1)S(1)} %collective-permute-done.27.refs_3_.far_ref, ...), custom_call_target="tpu_custom_call" | custom-call | flops 20000000000 | bytes 1000000 | tf_op jit(solution)/shard_map/pallas_call | solution.py:243
  394.8 8.5 %collective-permute-done.35 = bf16[256,1024]{1,0:T(8,128)(2,1)S(1)} collective-permute-done((bf16[256,1024]{1,0:T(8,128)(2,1)}, bf16[256,1024]{1,0:T(8,128)(2,1)S(1)}, u32[]{:S(2)}, u32[]{:S(2)}) %collective-permute-start.35) | collective-permute-done | bytes 524320 | tf_op jit(solution)/shard_map/ppermute | solution.py:512
  404.4 7.1 %collective-permute-done.34 = bf16[4,128,384]{2,1,0:T(8,128)(2,1)S(1)} collective-permute-done((bf16[4,128,384]{2,1,0:T(8,128)(2,1)S(1)}, bf16[4,128,384]{2,1,0:T(8,128)(2,1)S(1)}, u32[]{:S(2)}, u32[]{:S(2)}) %collective-permute-start.34) | collective-permute-done | bytes 393248 | tf_op jit(solution)/shard_map/ppermute | solution.py:512
  412.4 6.7 %collective-permute-done.33 = bf16[4,128,384]{2,1,0:T(8,128)(2,1)S(1)} collective-permute-done((bf16[4,128,384]{2,1,0:T(8,128)(2,1)S(1)}, bf16[4,128,384]{2,1,0:T(8,128)(2,1)S(1)}, u32[]{:S(2)}, u32[]{:S(2)}) %collective-permute-start.33) | collective-permute-done | bytes 393248 | tf_op jit(solution)/shard_map/ppermute | solution.py:512
  441.6 5.5 collective-permute-done.40
  470.4 4.9 shard_map.278.refs_0_
  475.3 4.9 shard_map.280.refs_0_
  480.3 5.2 shard_map.279
  486.1 6.2 %all-to-all-start.5 = ((bf16[8,32,1024]{2,1,0:T(8,128)(2,1)}), bf16[8,32,1024]{2,1,0:T(8,128)(2,1)S(1)}, u32[]{:S(2)}, u32[]{:S(2)}) async-start(bf16[8,32,1024]{2,1,0:T(8,128)(2,1)} %bitcast.87), calls=%async_computation.6 | async-start | bytes 1048576 | tf_op jit(solution)/shard_map/all_to_all | solution.py:587
  496.7 13.4 %collective-permute-done.49 = bf16[1,8,256,256]{3,2,1,0:T(8,128)(2,1)S(1)} collective-permute-done((bf16[1,8,256,256]{3,2,1,0:T(8,128)(2,1)}, bf16[1,8,256,256]{3,2,1,0:T(8,128)(2,1)S(1)}, u32[]{:S(2)}, u32[]{:S(2)}) %collective-permute-start.49) | collective-permute-done | bytes 1048608 | tf_op jit(solution)/shard_map/ppermute | solution.py:512
  523.7 10.7 %shard_map.281 = (f32[2,256,1024]{2,1,0:T(8,128)}, f32[2,256,1024]{2,1,0:T(8,128)}, f32[2,1024,256]{2,1,0:T(8,128)S(1)}, f32[2,1,256]{2,1,0:T(1,128)S(1)}) custom-call(s32[1]{0:T(128)} %bitcast.85.place_ref, bf16[2,8,256,256]{3,2,1,0:T(8,128)(2,1)S(1)} %copy-done.23, bf16[2,8,256,256]{3,2,1,0:T(8,128)(2,1)} %collective-permute-done.50.far_ref, ...), custom_call_target="tpu_custom_call" | custom-call | flops 11000000512 | bytes 1000000 | tf_op jit(solution)/shard_map/pallas_call | solution.py:453
  539.6 11.8 %collective-permute-done.54 = f32[1,2]{1,0:T(1,128)S(1)} collective-permute-done((f32[1,2]{1,0:T(1,128)S(1)}, f32[1,2]{1,0:T(1,128)S(1)}, u32[]{:S(2)}, u32[]{:S(2)}) %collective-permute-start.54) | collective-permute-done | bytes 40 | tf_op jit(solution)/shard_map/ppermute | solution.py:512
  (561 shorter events, 238.2 us)
Async XLA Ops:
  16.1 42.6 %all-to-all-start = ((bf16[8,64,1024]{2,1,0:T(8,128)(2,1)}), bf16[8,64,1024]{2,1,0:T(8,128)(2,1)S(1)}, u32[]{:S(2)}, u32[]{:S(2)}) async-start(bf16[8,64,1024]{2,1,0:T(8,128)(2,1)} %pad_maximum_fusion.3), calls=%async_computation | async-start | bytes 2097152 | tf_op jit(solution)/shard_map/all_to_all | solution.py:587
  23.4 89.4 %all-gather.3.cloned.1.call-start = ((), (), s32[]{:S(2)}) async-start(), calls=%async_computation.7 | async-start | bytes 2654208 | tf_op jit(solution)/shard_map/all_gather | solution.py:744
  69.8 38.7 %all-to-all-start.1 = ((bf16[8,64,1024]{2,1,0:T(8,128)(2,1)}), bf16[8,64,1024]{2,1,0:T(8,128)(2,1)}, u32[]{:S(2)}, u32[]{:S(2)}) async-start(bf16[8,64,1024]{2,1,0:T(8,128)(2,1)} %pad_maximum_fusion.2), calls=%async_computation.1 | async-start | bytes 2097152 | tf_op jit(solution)/shard_map/all_to_all | solution.py:587
  75.2 132.3 %all-gather.5.cloned.1.call-start = ((), (), s32[]{:S(2)}) async-start(), calls=%async_computation.8 | async-start | bytes 4718592 | tf_op jit(solution)/shard_map/all_gather | solution.py:761
  90.3 21.5 %collective-permute-start.3 = (bf16[512,1024]{1,0:T(8,128)(2,1)S(1)}, bf16[512,1024]{1,0:T(8,128)(2,1)S(1)}, u32[]{:S(2)}, u32[]{:S(2)}) collective-permute-start(bf16[512,1024]{1,0:T(8,128)(2,1)S(1)} %pad_maximum_fusion.5.near_ref), channel_id=1, source_target_pairs={{0,1},{1,0},{2,3},{3,2},{4,5},{5,4},{6,7},{7,6},{8,9},{9,8},{10,11... | collective-permute-start | bytes 3145736 | tf_op jit(solution)/shard_map/ppermute | solution.py:512
  90.4 22.4 %collective-permute-start.2 = (bf16[512,1024]{1,0:T(8,128)(2,1)S(1)}, bf16[512,1024]{1,0:T(8,128)(2,1)}, u32[]{:S(2)}, u32[]{:S(2)}) collective-permute-start(bf16[512,1024]{1,0:T(8,128)(2,1)S(1)} %pad_maximum_fusion.4.near_ref), channel_id=1, source_target_pairs={{0,1},{1,0},{2,3},{3,2},{4,5},{5,4},{6,7},{7,6},{8,9},{9,8},{10,11... | collective-permute-start | bytes 3145736 | tf_op jit(solution)/shard_map/ppermute | solution.py:512
  112.8 263.3 %reduce-scatter.2.cloned.1.call-start = ((), (), s32[]{:S(2)}) async-start(), calls=%async_computation.9 | async-start | bytes 4718592 | tf_op jit(solution)/shard_map/reduce_scatter | solution.py:804
  116.1 26.9 %collective-permute-start.4 = (bf16[256,1024]{1,0:T(8,128)(2,1)}, bf16[256,1024]{1,0:T(8,128)(2,1)S(1)}, u32[]{:S(2)}, u32[]{:S(2)}) collective-permute-start(bf16[256,1024]{1,0:T(8,128)(2,1)} %bitcast_select_fusion), channel_id=1, source_target_pairs={{0,2},{1,3},{2,0},{3,1},{4,6},{5,7},{6,4},{7,5},{8,10},{9,11},{10,... | collective-permute-start | bytes 1572872 | tf_op jit(solution)/shard_map/ppermute | solution.py:512
  149.7 25.4 %collective-permute-start.7 = (bf16[256,1024]{1,0:T(8,128)(2,1)S(1)}, bf16[256,1024]{1,0:T(8,128)(2,1)S(1)}, u32[]{:S(2)}, u32[]{:S(2)}) collective-permute-start(bf16[256,1024]{1,0:T(8,128)(2,1)S(1)} %add_convert_fusion.11), channel_id=1, source_target_pairs={{0,2},{1,3},{2,0},{3,1},{4,6},{5,7},{6,4},{7,5},{8,10},{9,11},{10,... | collective-permute-start | bytes 1572872 | tf_op jit(solution)/shard_map/ppermute | solution.py:512
  150.4 24.6 %collective-permute-start.8 = (bf16[256,1024]{1,0:T(8,128)(2,1)}, bf16[256,1024]{1,0:T(8,128)(2,1)S(1)}, u32[]{:S(2)}, u32[]{:S(2)}) collective-permute-start(bf16[256,1024]{1,0:T(8,128)(2,1)} %bitcast_select_fusion.1), channel_id=1, source_target_pairs={{0,2},{1,3},{2,0},{3,1},{4,6},{5,7},{6,4},{7,5},{8,10},{9,11},{10,... | collective-permute-start | bytes 1572872 | tf_op jit(solution)/shard_map/ppermute | solution.py:512
  181.8 24.5 %collective-permute-start.12 = (bf16[256,1024]{1,0:T(8,128)(2,1)S(1)}, bf16[256,1024]{1,0:T(8,128)(2,1)S(1)}, u32[]{:S(2)}, u32[]{:S(2)}) collective-permute-start(bf16[256,1024]{1,0:T(8,128)(2,1)S(1)} %add_convert_fusion.9), channel_id=1, source_target_pairs={{0,2},{1,3},{2,0},{3,1},{4,6},{5,7},{6,4},{7,5},{8,10},{9,11},{10,... | collective-permute-start | bytes 1572872 | tf_op jit(solution)/shard_map/ppermute | solution.py:512
  230.4 21.4 %collective-permute-start.18 = (bf16[512,1024]{1,0:T(8,128)(2,1)S(1)}, bf16[512,1024]{1,0:T(8,128)(2,1)S(1)}, u32[]{:S(2)}, u32[]{:S(2)}) collective-permute-start(bf16[512,1024]{1,0:T(8,128)(2,1)S(1)} %get-tuple-element.244), channel_id=1, source_target_pairs={{0,1},{1,0},{2,3},{3,2},{4,5},{5,4},{6,7},{7,6},{8,9},{9,8},{10,11... | collective-permute-start | bytes 3145736 | tf_op jit(solution)/shard_map/ppermute | solution.py:512
  274.0 33.0 %collective-permute-start.24 = (bf16[512,1024]{1,0:T(8,128)(2,1)}, bf16[512,1024]{1,0:T(8,128)(2,1)}, u32[]{:S(2)}, u32[]{:S(2)}) collective-permute-start(bf16[512,1024]{1,0:T(8,128)(2,1)} %get-tuple-element.274), channel_id=1, source_target_pairs={{0,1},{1,0},{2,3},{3,2},{4,5},{5,4},{6,7},{7,6},{8,9},{9,8},{10,11... | collective-permute-start | bytes 3145736 | tf_op jit(solution)/shard_map/ppermute | solution.py:512
  276.3 27.8 %collective-permute-start.23 = (bf16[256,1024]{1,0:T(8,128)(2,1)S(1)}, bf16[256,1024]{1,0:T(8,128)(2,1)S(1)}, u32[]{:S(2)}, u32[]{:S(2)}) collective-permute-start(bf16[256,1024]{1,0:T(8,128)(2,1)S(1)} %add_convert_fusion.5), channel_id=1, source_target_pairs={{0,2},{1,3},{2,0},{3,1},{4,6},{5,7},{6,4},{7,5},{8,10},{9,11},{10,... | collective-permute-start | bytes 1572872 | tf_op jit(solution)/shard_map/ppermute | solution.py:512
  278.3 27.2 %collective-permute-start.22 = (bf16[256,1024]{1,0:T(8,128)(2,1)S(1)}, bf16[256,1024]{1,0:T(8,128)(2,1)S(1)}, u32[]{:S(2)}, u32[]{:S(2)}) collective-permute-start(bf16[256,1024]{1,0:T(8,128)(2,1)S(1)} %add_convert_fusion.6), channel_id=1, source_target_pairs={{0,2},{1,3},{2,0},{3,1},{4,6},{5,7},{6,4},{7,5},{8,10},{9,11},{10,... | collective-permute-start | bytes 1572872 | tf_op jit(solution)/shard_map/ppermute | solution.py:512
  329.5 46.7 %all-to-all-start.2 = ((bf16[8,32,1024]{2,1,0:T(8,128)(2,1)}), bf16[8,32,1024]{2,1,0:T(8,128)(2,1)}, u32[]{:S(2)}, u32[]{:S(2)}) async-start(bf16[8,32,1024]{2,1,0:T(8,128)(2,1)} %bitcast.250), calls=%async_computation.2 | async-start | bytes 1048576 | tf_op jit(solution)/shard_map/all_to_all | solution.py:587
  338.9 31.7 %collective-permute-start.30 = (bf16[4,128,256]{2,1,0:T(8,128)(2,1)S(1)}, bf16[4,128,256]{2,1,0:T(8,128)(2,1)S(1)}, u32[]{:S(2)}, u32[]{:S(2)}) collective-permute-start(bf16[4,128,256]{2,1,0:T(8,128)(2,1)S(1)} %dynamic-slice_bitcast_fusion.2), channel_id=1, source_target_pairs={{0,4},{4,0},{8,12},{12,8},{16,20},{20,16},{24,28},{28,24},{1,5},{5... | collective-permute-start | bytes 786440 | tf_op jit(solution)/shard_map/ppermute | solution.py:512
  342.1 29.5 %collective-permute-start.29 = (bf16[256,1024]{1,0:T(8,128)(2,1)S(1)}, bf16[256,1024]{1,0:T(8,128)(2,1)S(1)}, u32[]{:S(2)}, u32[]{:S(2)}) collective-permute-start(bf16[256,1024]{1,0:T(8,128)(2,1)S(1)} %add_convert_fusion.2), channel_id=1, source_target_pairs={{0,2},{1,3},{2,0},{3,1},{4,6},{5,7},{6,4},{7,5},{8,10},{9,11},{10,... | collective-permute-start | bytes 1572872 | tf_op jit(solution)/shard_map/ppermute | solution.py:512
  344.0 29.8 %collective-permute-start.28 = (bf16[256,1024]{1,0:T(8,128)(2,1)S(1)}, bf16[256,1024]{1,0:T(8,128)(2,1)S(1)}, u32[]{:S(2)}, u32[]{:S(2)}) collective-permute-start(bf16[256,1024]{1,0:T(8,128)(2,1)S(1)} %add_convert_fusion.3), channel_id=1, source_target_pairs={{0,2},{1,3},{2,0},{3,1},{4,6},{5,7},{6,4},{7,5},{8,10},{9,11},{10,... | collective-permute-start | bytes 1572872 | tf_op jit(solution)/shard_map/ppermute | solution.py:512
  384.0 38.5 %all-to-all-start.3 = ((bf16[8,64,1024]{2,1,0:T(8,128)(2,1)}), bf16[8,64,1024]{2,1,0:T(8,128)(2,1)}, u32[]{:S(2)}, u32[]{:S(2)}) async-start(bf16[8,64,1024]{2,1,0:T(8,128)(2,1)} %bitcast.241), calls=%async_computation.4 | async-start | bytes 2097152 | tf_op jit(solution)/shard_map/all_to_all | solution.py:587
  389.8 21.7 %collective-permute-start.34 = (bf16[4,128,384]{2,1,0:T(8,128)(2,1)S(1)}, bf16[4,128,384]{2,1,0:T(8,128)(2,1)S(1)}, u32[]{:S(2)}, u32[]{:S(2)}) collective-permute-start(bf16[4,128,384]{2,1,0:T(8,128)(2,1)S(1)} %dynamic-slice_bitcast_fusion), channel_id=1, source_target_pairs={{0,4},{4,0},{8,12},{12,8},{16,20},{20,16},{24,28},{28,24},{1,5},{5... | collective-permute-start | bytes 1179656 | tf_op jit(solution)/shard_map/ppermute | solution.py:512
  391.8 27.4 %collective-permute-start.33 = (bf16[4,128,384]{2,1,0:T(8,128)(2,1)S(1)}, bf16[4,128,384]{2,1,0:T(8,128)(2,1)S(1)}, u32[]{:S(2)}, u32[]{:S(2)}) collective-permute-start(bf16[4,128,384]{2,1,0:T(8,128)(2,1)S(1)} %dynamic-slice_bitcast_fusion.1), channel_id=1, source_target_pairs={{0,4},{4,0},{8,12},{12,8},{16,20},{20,16},{24,28},{28,24},{1,5},{5... | collective-permute-start | bytes 1179656 | tf_op jit(solution)/shard_map/ppermute | solution.py:512
  393.2 26.9 %collective-permute-start.32 = (bf16[256,1024]{1,0:T(8,128)(2,1)S(1)}, bf16[256,1024]{1,0:T(8,128)(2,1)S(1)}, u32[]{:S(2)}, u32[]{:S(2)}) collective-permute-start(bf16[256,1024]{1,0:T(8,128)(2,1)S(1)} %add_convert_fusion.1), channel_id=1, source_target_pairs={{0,2},{1,3},{2,0},{3,1},{4,6},{5,7},{6,4},{7,5},{8,10},{9,11},{10,... | collective-permute-start | bytes 1572872 | tf_op jit(solution)/shard_map/ppermute | solution.py:512
  430.1 28.5 %collective-permute-start.42 = (bf16[256,1024]{1,0:T(8,128)(2,1)}, bf16[256,1024]{1,0:T(8,128)(2,1)}, u32[]{:S(2)}, u32[]{:S(2)}) collective-permute-start(bf16[256,1024]{1,0:T(8,128)(2,1)} %bitcast.54), channel_id=1, source_target_pairs={{0,2},{1,3},{2,0},{3,1},{4,6},{5,7},{6,4},{7,5},{8,10},{9,11},{10,... | collective-permute-start | bytes 1572872 | tf_op jit(solution)/shard_map/ppermute | solution.py:512
  430.7 26.2 %collective-permute-start.45 = (bf16[256,1024]{1,0:T(8,128)(2,1)}, bf16[256,1024]{1,0:T(8,128)(2,1)}, u32[]{:S(2)}, u32[]{:S(2)}) collective-permute-start(bf16[256,1024]{1,0:T(8,128)(2,1)} %bitcast.53), channel_id=1, source_target_pairs={{0,2},{1,3},{2,0},{3,1},{4,6},{5,7},{6,4},{7,5},{8,10},{9,11},{10,... | collective-permute-start | bytes 1572872 | tf_op jit(solution)/shard_map/ppermute | solution.py:512
  448.9 36.6 %all-to-all-start.4 = ((bf16[8,256,256]{2,1,0:T(8,128)(2,1)}), bf16[8,256,256]{2,1,0:T(8,128)(2,1)}, u32[]{:S(2)}, u32[]{:S(2)}) async-start(bf16[8,256,256]{2,1,0:T(8,128)(2,1)} %shard_map.277), calls=%async_computation.5 | async-start | bytes 2097152 | tf_op jit(solution)/shard_map/all_to_all | solution.py:587
  453.9 16.5 %collective-permute-start.44 = (bf16[512,1024]{1,0:T(8,128)(2,1)S(1)}, bf16[512,1024]{1,0:T(8,128)(2,1)}, u32[]{:S(2)}, u32[]{:S(2)}) collective-permute-start(bf16[512,1024]{1,0:T(8,128)(2,1)S(1)} %pad_maximum_fusion.13.near_ref), channel_id=1, source_target_pairs={{0,1},{1,0},{2,3},{3,2},{4,5},{5,4},{6,7},{7,6},{8,9},{9,8},{10,11... | collective-permute-start | bytes 3145736 | tf_op jit(solution)/shard_map/ppermute | solution.py:512
  458.1 17.3 %collective-permute-start.46 = (bf16[512,1024]{1,0:T(8,128)(2,1)S(1)}, bf16[512,1024]{1,0:T(8,128)(2,1)}, u32[]{:S(2)}, u32[]{:S(2)}) collective-permute-start(bf16[512,1024]{1,0:T(8,128)(2,1)S(1)} %constant_dynamic-update-slice_fusion.2.near_ref), channel_id=1, source_target_pairs={{0,1},{1,0},{2,3},{3,2},{4,5},{5,4},{6,7},{7,6},{8,9},{9,8},{10,11... | collective-permute-start | bytes 3145736 | tf_op jit(solution)/shard_map/ppermute | solution.py:512
  460.5 19.8 %collective-permute-start.43 = (bf16[512,1024]{1,0:T(8,128)(2,1)}, bf16[512,1024]{1,0:T(8,128)(2,1)}, u32[]{:S(2)}, u32[]{:S(2)}) collective-permute-start(bf16[512,1024]{1,0:T(8,128)(2,1)} %constant_dynamic-update-slice_fusion.near_ref), channel_id=1, source_target_pairs={{0,1},{1,0},{2,3},{3,2},{4,5},{5,4},{6,7},{7,6},{8,9},{9,8},{10,11... | collective-permute-start | bytes 3145736 | tf_op jit(solution)/shard_map/ppermute | solution.py:512
  485.5 24.6 %collective-permute-start.49 = (bf16[1,8,256,256]{3,2,1,0:T(8,128)(2,1)}, bf16[1,8,256,256]{3,2,1,0:T(8,128)(2,1)S(1)}, u32[]{:S(2)}, u32[]{:S(2)}) collective-permute-start(bf16[1,8,256,256]{3,2,1,0:T(8,128)(2,1)} %bitcast.86), channel_id=1, source_target_pairs={{0,2},{1,3},{2,0},{3,1},{4,6},{5,7},{6,4},{7,5},{8,10},{9,11},{10,... | collective-permute-start | bytes 3145736 | tf_op jit(solution)/shard_map/ppermute | solution.py:512
  486.1 26.7 %all-to-all-start.5 = ((bf16[8,32,1024]{2,1,0:T(8,128)(2,1)}), bf16[8,32,1024]{2,1,0:T(8,128)(2,1)S(1)}, u32[]{:S(2)}, u32[]{:S(2)}) async-start(bf16[8,32,1024]{2,1,0:T(8,128)(2,1)} %bitcast.87), calls=%async_computation.6 | async-start | bytes 1048576 | tf_op jit(solution)/shard_map/all_to_all | solution.py:587
  535.9 17.5 %collective-permute-start.55 = (f32[6,1280]{1,0:T(8,128)S(1)}, f32[6,1280]{1,0:T(8,128)S(1)}, u32[]{:S(2)}, u32[]{:S(2)}) collective-permute-start(f32[6,1280]{1,0:T(8,128)S(1)} %maximum_maximum_fusion), channel_id=1, source_target_pairs={{0,4},{4,0},{8,12},{12,8},{16,20},{20,16},{24,28},{28,24},{1,5},{5... | collective-permute-start | bytes 92168 | tf_op jit(solution)/shard_map/ppermute | solution.py:512
  (150 other events, 1139.9 us)
Sparse Core Ops, SparseCore 0:
  27.0 77.8 all-gather.2
  112.9 72.1 all-gather.4
  274.7 92.8 reduce-scatter.1

commit v5 on v4

--- a/solution.py
+++ b/solution.py
@@ -60,7 +60,7 @@
 
 TILE = 256
 STRIP = 64
-VMEM_BYTES = 20 * 1024 * 1024
+VMEM_BYTES = 28 * 1024 * 1024
 SMALL = pl.CostEstimate(flops=10**9, bytes_accessed=10**6, transcendentals=0)
 LARGE = pl.CostEstimate(flops=20 * 10**9, bytes_accessed=10**6, transcendentals=0)
 MEDIUM = pl.CostEstimate(flops=11 * 10**9, bytes_accessed=10**6, transcendentals=0)
@@ -106,13 +106,13 @@
         value_lanes = slice(2 * cols + h * HEAD_DIM, 2 * cols + (h + 1) * HEAD_DIM)
         for t in range(tiles):
             here = slice(t * TILE, (t + 1) * TILE)
-            query = qkv_ref[here, lanes]
+            query = qkv_ref[here, lanes] * jnp.asarray(scale, low_type)
             seg_q = seg_col_ref[here, :]
             scores = []
             top = None
             for c in range(t + 1):
                 there = slice(c * TILE, (c + 1) * TILE)
-                s = dot_nt(query, qkv_ref[there, key_lanes]) * scale
+                s = dot_nt(query, qkv_ref[there, key_lanes])
                 allowed = seg_q == seg_row_ref[:, there]
                 if c == t:
                     allowed = allowed & (
@@ -197,7 +197,7 @@
         grad_value[...] = jnp.zeros_like(grad_value)
         for t in range(tiles):
             here = slice(t * TILE, (t + 1) * TILE)
-            query = qkv_ref[here, lanes]
+            query = qkv_ref[here, lanes] * jnp.asarray(scale, low_type)
             grad = placed[here, lanes]
             row_total = jnp.sum(grad.astype(f32) * out_ref[here, lanes].astype(f32), axis=1, keepdims=True)
             seg_q = seg_col_ref[here, :]
@@ -206,7 +206,7 @@
             for c in range(t + 1):
                 there = slice(c * TILE, (c + 1) * TILE)
                 key = qkv_ref[there, key_lanes]
-                s = dot_nt(query, key) * scale
+                s = dot_nt(query, key)
                 allowed = seg_q == seg_row_ref[:, there]
                 if c == t:
                     allowed = allowed & (
@@ -220,7 +220,7 @@
                 grad_key[there, :] += dot_tn(ds, query)
                 grad_value[there, :] += dot_tn(p.astype(low_type), grad)
             moved[here, lanes] = (grad_query * scale).astype(low_type)
-        moved[:, key_lanes] = (grad_key[...] * scale).astype(low_type)
+        moved[:, key_lanes] = grad_key[...].astype(low_type)
         moved[:, value_lanes] = grad_value[...].astype(low_type)
     sums_ref[...] = jnp.sum(moved[...].astype(f32), axis=0, keepdims=True)
     for t in range(tiles):

time: 584 us -> 576 us (0.986)
  local copies, waits for them, and re-layouts: 68.6 us -> 60.4 us
    unnamed x242 -> x226, local copies, waits for them, and re-layouts: 42.8 us -> 34.6 us
where the time goes in v5:
time: 576 us; the launch traced here: 568 us
  waiting for transfers between devices  180 us (31%)
  Pallas kernels  152 us (26%)
  starting transfers between devices  77.9 us (14%)
  other arithmetic  71 us (12%)
  local copies, waits for them, and re-layouts  60.4 us (10%)
  between operations  17.4 us (3%)
  matrix products  9.25 us (2%)
    ppermute x58, waiting for transfers between devices, swap(): return lax.ppermute(values, axis, [(i, i ^ bit) for i in range(count)])  134 us
    ppermute x58, starting transfers between devices, swap(): return lax.ppermute(values, axis, [(i, i ^ bit) for i in range(count)])  45.7 us
    all_to_all x6, waiting for transfers between devices, exchange(): return lax.all_to_all(rows, 'dp', split_axis=0, concat_axis=0, tiled=True)  45.4 us
    pallas_call x2, Pallas kernels, attention_backward(): pl.pallas_call(attention_backward_kernel, out_shape=(shape((rows // 2, wi...  42.6 us
    pallas_call x2, Pallas kernels, attention_forward(): pl.pallas_call(attention_forward_kernel, out_shape=(shape((rows // 2, wid...  35.8 us
    unnamed x226, local copies, waits for them, and re-layouts  34.6 us
    all_to_all x6, starting transfers between devices, exchange(): return lax.all_to_all(rows, 'dp', split_axis=0, concat_axis=0, tiled=True)  32.1 us
    pallas_call x4, Pallas kernels, mlp(): pl.pallas_call(mlp_kernel, out_shape=(shape((rows, cols), low_type), shap...  23.5 us
  transfers between devices with their start and end apart: 67, of which 26 were waited for; matrix products, arithmetic and copies ran while one was open for 17% of the time, Pallas kernels for 23%

profile of v5, /device:TPU:0, one launch (start us, length us, event | category | flops | bytes accessed | tf_op | source)
XLA Modules:
  0.0 568.2 jit_solution(16051106710163550124)
XLA Ops:
  16.1 7.3 %all-to-all-start = ((bf16[8,64,1024]{2,1,0:T(8,128)(2,1)}), bf16[8,64,1024]{2,1,0:T(8,128)(2,1)S(1)}, u32[]{:S(2)}, u32[]{:S(2)}) async-start(bf16[8,64,1024]{2,1,0:T(8,128)(2,1)} %pad_maximum_fusion.3), calls=%async_computation | async-start | bytes 2097152 | tf_op jit(solution)/shard_map/all_to_all | solution.py:587
  27.2 31.4 %all-to-all-done = bf16[8,64,1024]{2,1,0:T(8,128)(2,1)S(1)} async-done(((bf16[8,64,1024]{2,1,0:T(8,128)(2,1)}), bf16[8,64,1024]{2,1,0:T(8,128)(2,1)S(1)}, u32[]{:S(2)}, u32[]{:S(2)}) %all-to-all-start) | async-done | bytes 1048608 | tf_op jit(solution)/shard_map/all_to_all | solution.py:587
  63.7 6.0 %collective-permute-done = bf16[256,1024]{1,0:T(8,128)(2,1)S(1)} collective-permute-done((bf16[256,1024]{1,0:T(8,128)(2,1)S(1)}, bf16[256,1024]{1,0:T(8,128)(2,1)S(1)}, u32[]{:S(2)}, u32[]{:S(2)}) %collective-permute-start) | collective-permute-done | bytes 524320 | tf_op jit(solution)/shard_map/ppermute | solution.py:512
  69.8 5.4 all-to-all-start.1
  81.7 8.5 %collective-permute-done.1 = bf16[256,1024]{1,0:T(8,128)(2,1)S(1)} collective-permute-done((bf16[256,1024]{1,0:T(8,128)(2,1)S(1)}, bf16[256,1024]{1,0:T(8,128)(2,1)S(1)}, u32[]{:S(2)}, u32[]{:S(2)}) %collective-permute-start.1) | collective-permute-done | bytes 524320 | tf_op jit(solution)/shard_map/ppermute | solution.py:512
  94.5 13.9 %all-to-all-done.1 = bf16[8,64,1024]{2,1,0:T(8,128)(2,1)} async-done(((bf16[8,64,1024]{2,1,0:T(8,128)(2,1)}), bf16[8,64,1024]{2,1,0:T(8,128)(2,1)}, u32[]{:S(2)}, u32[]{:S(2)}) %all-to-all-start.1) | async-done | bytes 1048608 | tf_op jit(solution)/shard_map/all_to_all | solution.py:587
  119.6 19.1 %shard_map.266 = (f32[512,1024]{1,0:T(8,128)S(1)}, bf16[512,1024]{1,0:T(8,128)(2,1)}, bf16[1024,1024]{1,0:T(8,128)(2,1)S(1)}, bf16[1024,256]{1,0:T(8,128)(2,1)S(...) custom-call(bf16[512,1024]{1,0:T(8,128)(2,1)S(1)} %pad_maximum_fusion.4.near_ref, ...), custom_call_target="tpu_custom_call" | custom-call | flops 20000000000 | bytes 1000000 | tf_op jit(solution)/shard_map/pallas_call | solution.py:152
  153.1 16.6 %shard_map.265 = (f32[512,1024]{1,0:T(8,128)S(1)}, bf16[512,1024]{1,0:T(8,128)(2,1)S(1)}, bf16[1024,1024]{1,0:T(8,128)(2,1)S(1)}, bf16[1024,256]{1,0:T(8,128)(2,...) custom-call(bf16[512,1024]{1,0:T(8,128)(2,1)S(1)} %copy-done.27, ...), custom_call_target="tpu_custom_call" | custom-call | flops 20000000000 | bytes 1000000 | tf_op jit(solution)/shard_map/pallas_call | solution.py:152
  183.3 12.5 %collective-permute-done.11 = bf16[256,1024]{1,0:T(8,128)(2,1)S(1)} collective-permute-done((bf16[256,1024]{1,0:T(8,128)(2,1)S(1)}, bf16[256,1024]{1,0:T(8,128)(2,1)S(1)}, u32[]{:S(2)}, u32[]{:S(2)}) %collective-permute-start.11) | collective-permute-done | bytes 524320 | tf_op jit(solution)/shard_map/ppermute | solution.py:512
  196.9 9.4 %collective-permute-done.12 = bf16[256,1024]{1,0:T(8,128)(2,1)S(1)} collective-permute-done((bf16[256,1024]{1,0:T(8,128)(2,1)S(1)}, bf16[256,1024]{1,0:T(8,128)(2,1)S(1)}, u32[]{:S(2)}, u32[]{:S(2)}) %collective-permute-start.12) | collective-permute-done | bytes 524320 | tf_op jit(solution)/shard_map/ppermute | solution.py:512
  210.8 5.2 shard_map.267
  217.4 5.5 collective-permute-done.14
  223.1 6.8 %shard_map.268 = (bf16[512,1024]{1,0:T(8,128)(2,1)S(1)}, bf16[512,1024]{1,0:T(8,128)(2,1)S(1)}, bf16[512,1024]{1,0:T(8,128)(2,1)S(1)}, bf16[512,1024]{1,0:T(8,128)(2,1)S(1)}, f32[1,1024]{1,0:T(1,128)S(1)}) custom-call(bf16[512,1024]{1,0:T(8,128)(2,1)S(1)} %collective-permute-done.13.normed_ref.refs_1_, ...), custom_call_target="tpu_custom_call" | custom-call | flops 11000000512 | bytes 1000000 | tf_op jit(solution)/shard_map/pallas_call | solution.py:291
  230.5 5.2 shard_map.269
  239.0 6.3 %shard_map.270 = (bf16[512,1024]{1,0:T(8,128)(2,1)S(1)}, bf16[512,1024]{1,0:T(8,128)(2,1)S(1)}, bf16[512,1024]{1,0:T(8,128)(2,1)}, bf16[512,1024]{1,0:T(8,128)(2,1)}, f32[1,1024]{1,0:T(1,128)S(1)}) custom-call(bf16[512,1024]{1,0:T(8,128)(2,1)S(1)} %collective-permute-done.15.normed_ref.refs_3_, bf16[512,1024]{1,0:T(8,128)(2,1)S(1)} %copy-done.45, ...), custom_call_target="tpu_custom_call" | custom-call | flops 11000000512 | bytes 1000000 | tf_op jit(solution)/shard_map/pallas_call | solution.py:291
  245.3 6.2 %collective-permute-done.17 = bf16[256,1024]{1,0:T(8,128)(2,1)S(1)} collective-permute-done((bf16[256,1024]{1,0:T(8,128)(2,1)S(1)}, bf16[256,1024]{1,0:T(8,128)(2,1)S(1)}, u32[]{:S(2)}, u32[]{:S(2)}) %collective-permute-start.17) | collective-permute-done | bytes 524320 | tf_op jit(solution)/shard_map/ppermute | solution.py:512
  254.4 10.5 %shard_map.271 = bf16[1024,2048]{1,0:T(8,128)(2,1)S(1)} custom-call(bf16[512,1024]{1,0:T(8,128)(2,1)S(1)} %copy-done.25, bf16[512,1024]{1,0:T(8,128)(2,1)S(1)} %collective-permute-done.13.normed_ref.refs_1_, bf16[512,1024]{1,0:T(8,128)(2,1)S(1)} %pad_maximum_fusion.9.normed_ref.refs_2_, bf16[512,1024]{1,0:T(8,128)(2,1)S(1)} %collective-permute-done.15.normed_ref.refs_3_, ...), custom_call_target="tpu_custom_call" | custom-call | flops 11000000512 | bytes 1000000 | tf_op jit(solution)/shard_map/pallas_call | solution.py:336
  281.2 22.6 %shard_map.273 = (f32[512,1024]{1,0:T(8,128)S(1)}, bf16[512,1024]{1,0:T(8,128)(2,1)}, bf16[1024,768]{1,0:T(8,128)(2,1)S(1)}, f32[1,768]{1,0:T(1,128)S(1)}) custom-call(bf16[512,1024]{1,0:T(8,128)(2,1)S(1)} %pad_maximum_fusion.10.near_ref.refs_0_, bf16[512,1024]{1,0:T(8,128)(2,1)} %collective-permute-done.21.far_ref.refs_1_, ...), custom_call_target="tpu_custom_call" | custom-call | flops 20000000000 | bytes 1000000 | tf_op jit(solution)/shard_map/pallas_call | solution.py:243
  313.6 11.3 %collective-permute-done.25 = bf16[256,1024]{1,0:T(8,128)(2,1)} collective-permute-done((bf16[256,1024]{1,0:T(8,128)(2,1)}, bf16[256,1024]{1,0:T(8,128)(2,1)}, u32[]{:S(2)}, u32[]{:S(2)}) %collective-permute-start.25) | collective-permute-done | bytes 524320 | tf_op jit(solution)/shard_map/ppermute | solution.py:512
  329.2 4.6 all-to-all-start.2
  345.3 20.0 %shard_map.275 = (f32[512,1024]{1,0:T(8,128)S(1)}, bf16[512,1024]{1,0:T(8,128)(2,1)S(1)}, bf16[1024,768]{1,0:T(8,128)(2,1)S(1)}, f32[1,768]{1,0:T(1,128)S(1)}) custom-call(bf16[512,1024]{1,0:T(8,128)(2,1)S(1)} %pad_maximum_fusion.11.refs_2_.near_ref, bf16[512,1024]{1,0:T(8,128)(2,1)S(1)} %collective-permute-done.27.refs_3_.far_ref, ...), custom_call_target="tpu_custom_call" | custom-call | flops 20000000000 | bytes 1000000 | tf_op jit(solution)/shard_map/pallas_call | solution.py:243
  394.2 8.5 %collective-permute-done.35 = bf16[256,1024]{1,0:T(8,128)(2,1)S(1)} collective-permute-done((bf16[256,1024]{1,0:T(8,128)(2,1)}, bf16[256,1024]{1,0:T(8,128)(2,1)S(1)}, u32[]{:S(2)}, u32[]{:S(2)}) %collective-permute-start.35) | collective-permute-done | bytes 524320 | tf_op jit(solution)/shard_map/ppermute | solution.py:512
  403.8 7.1 %collective-permute-done.34 = bf16[4,128,384]{2,1,0:T(8,128)(2,1)S(1)} collective-permute-done((bf16[4,128,384]{2,1,0:T(8,128)(2,1)S(1)}, bf16[4,128,384]{2,1,0:T(8,128)(2,1)S(1)}, u32[]{:S(2)}, u32[]{:S(2)}) %collective-permute-start.34) | collective-permute-done | bytes 393248 | tf_op jit(solution)/shard_map/ppermute | solution.py:512
  411.0 7.6 %collective-permute-done.33 = bf16[4,128,384]{2,1,0:T(8,128)(2,1)S(1)} collective-permute-done((bf16[4,128,384]{2,1,0:T(8,128)(2,1)S(1)}, bf16[4,128,384]{2,1,0:T(8,128)(2,1)S(1)}, u32[]{:S(2)}, u32[]{:S(2)}) %collective-permute-start.33) | collective-permute-done | bytes 393248 | tf_op jit(solution)/shard_map/ppermute | solution.py:512
  440.1 5.6 collective-permute-done.40
  468.9 4.9 shard_map.278.refs_0_
  473.8 4.9 shard_map.280.refs_0_
  478.8 5.3 shard_map.279
  484.7 6.2 %all-to-all-start.5 = ((bf16[8,32,1024]{2,1,0:T(8,128)(2,1)}), bf16[8,32,1024]{2,1,0:T(8,128)(2,1)S(1)}, u32[]{:S(2)}, u32[]{:S(2)}) async-start(bf16[8,32,1024]{2,1,0:T(8,128)(2,1)} %bitcast.87), calls=%async_computation.6 | async-start | bytes 1048576 | tf_op jit(solution)/shard_map/all_to_all | solution.py:587
  495.2 13.4 %collective-permute-done.49 = bf16[1,8,256,256]{3,2,1,0:T(8,128)(2,1)S(1)} collective-permute-done((bf16[1,8,256,256]{3,2,1,0:T(8,128)(2,1)}, bf16[1,8,256,256]{3,2,1,0:T(8,128)(2,1)S(1)}, u32[]{:S(2)}, u32[]{:S(2)}) %collective-permute-start.49) | collective-permute-done | bytes 1048608 | tf_op jit(solution)/shard_map/ppermute | solution.py:512
  515.8 11.9 %shard_map.281 = (f32[2,256,1024]{2,1,0:T(8,128)}, f32[2,256,1024]{2,1,0:T(8,128)}, f32[2,1024,256]{2,1,0:T(8,128)}, f32[2,1,256]{2,1,0:T(1,128)}) custom-call(s32[1]{0:T(128)} %bitcast.85.place_ref, bf16[2,8,256,256]{3,2,1,0:T(8,128)(2,1)} %pad_maximum_fusion.near_ref, bf16[2,8,256,256]{3,2,1,0:T(8,128)(2,1)} %collective-permute-done.50.far_ref, ...), custom_call_target="tpu_custom_call" | custom-call | flops 11000000512 | bytes 1000000 | tf_op jit(solution)/shard_map/pallas_call | solution.py:453
  532.4 11.8 %collective-permute-done.54 = f32[1,2]{1,0:T(1,128)S(1)} collective-permute-done((f32[1,2]{1,0:T(1,128)S(1)}, f32[1,2]{1,0:T(1,128)S(1)}, u32[]{:S(2)}, u32[]{:S(2)}) %collective-permute-start.54) | collective-permute-done | bytes 40 | tf_op jit(solution)/shard_map/ppermute | solution.py:512
  (545 shorter events, 229.3 us)
Async XLA Ops:
  16.1 42.6 %all-to-all-start = ((bf16[8,64,1024]{2,1,0:T(8,128)(2,1)}), bf16[8,64,1024]{2,1,0:T(8,128)(2,1)S(1)}, u32[]{:S(2)}, u32[]{:S(2)}) async-start(bf16[8,64,1024]{2,1,0:T(8,128)(2,1)} %pad_maximum_fusion.3), calls=%async_computation | async-start | bytes 2097152 | tf_op jit(solution)/shard_map/all_to_all | solution.py:587
  23.4 89.4 %all-gather.3.cloned.1.call-start = ((), (), s32[]{:S(2)}) async-start(), calls=%async_computation.7 | async-start | bytes 2654208 | tf_op jit(solution)/shard_map/all_gather | solution.py:744
  69.8 38.7 %all-to-all-start.1 = ((bf16[8,64,1024]{2,1,0:T(8,128)(2,1)}), bf16[8,64,1024]{2,1,0:T(8,128)(2,1)}, u32[]{:S(2)}, u32[]{:S(2)}) async-start(bf16[8,64,1024]{2,1,0:T(8,128)(2,1)} %pad_maximum_fusion.2), calls=%async_computation.1 | async-start | bytes 2097152 | tf_op jit(solution)/shard_map/all_to_all | solution.py:587
  75.2 132.3 %all-gather.5.cloned.1.call-start = ((), (), s32[]{:S(2)}) async-start(), calls=%async_computation.8 | async-start | bytes 4718592 | tf_op jit(solution)/shard_map/all_gather | solution.py:761
  90.3 21.5 %collective-permute-start.3 = (bf16[512,1024]{1,0:T(8,128)(2,1)S(1)}, bf16[512,1024]{1,0:T(8,128)(2,1)S(1)}, u32[]{:S(2)}, u32[]{:S(2)}) collective-permute-start(bf16[512,1024]{1,0:T(8,128)(2,1)S(1)} %pad_maximum_fusion.5.near_ref), channel_id=1, source_target_pairs={{0,1},{1,0},{2,3},{3,2},{4,5},{5,4},{6,7},{7,6},{8,9},{9,8},{10,11... | collective-permute-start | bytes 3145736 | tf_op jit(solution)/shard_map/ppermute | solution.py:512
  90.4 22.4 %collective-permute-start.2 = (bf16[512,1024]{1,0:T(8,128)(2,1)S(1)}, bf16[512,1024]{1,0:T(8,128)(2,1)}, u32[]{:S(2)}, u32[]{:S(2)}) collective-permute-start(bf16[512,1024]{1,0:T(8,128)(2,1)S(1)} %pad_maximum_fusion.4.near_ref), channel_id=1, source_target_pairs={{0,1},{1,0},{2,3},{3,2},{4,5},{5,4},{6,7},{7,6},{8,9},{9,8},{10,11... | collective-permute-start | bytes 3145736 | tf_op jit(solution)/shard_map/ppermute | solution.py:512
  112.8 262.9 %reduce-scatter.2.cloned.1.call-start = ((), (), s32[]{:S(2)}) async-start(), calls=%async_computation.9 | async-start | bytes 4718592 | tf_op jit(solution)/shard_map/reduce_scatter | solution.py:804
  116.0 27.0 %collective-permute-start.4 = (bf16[256,1024]{1,0:T(8,128)(2,1)}, bf16[256,1024]{1,0:T(8,128)(2,1)S(1)}, u32[]{:S(2)}, u32[]{:S(2)}) collective-permute-start(bf16[256,1024]{1,0:T(8,128)(2,1)} %bitcast_select_fusion), channel_id=1, source_target_pairs={{0,2},{1,3},{2,0},{3,1},{4,6},{5,7},{6,4},{7,5},{8,10},{9,11},{10,... | collective-permute-start | bytes 1572872 | tf_op jit(solution)/shard_map/ppermute | solution.py:512
  149.7 25.4 %collective-permute-start.7 = (bf16[256,1024]{1,0:T(8,128)(2,1)S(1)}, bf16[256,1024]{1,0:T(8,128)(2,1)S(1)}, u32[]{:S(2)}, u32[]{:S(2)}) collective-permute-start(bf16[256,1024]{1,0:T(8,128)(2,1)S(1)} %add_convert_fusion.11), channel_id=1, source_target_pairs={{0,2},{1,3},{2,0},{3,1},{4,6},{5,7},{6,4},{7,5},{8,10},{9,11},{10,... | collective-permute-start | bytes 1572872 | tf_op jit(solution)/shard_map/ppermute | solution.py:512
  150.4 24.6 %collective-permute-start.8 = (bf16[256,1024]{1,0:T(8,128)(2,1)}, bf16[256,1024]{1,0:T(8,128)(2,1)S(1)}, u32[]{:S(2)}, u32[]{:S(2)}) collective-permute-start(bf16[256,1024]{1,0:T(8,128)(2,1)} %bitcast_select_fusion.1), channel_id=1, source_target_pairs={{0,2},{1,3},{2,0},{3,1},{4,6},{5,7},{6,4},{7,5},{8,10},{9,11},{10,... | collective-permute-start | bytes 1572872 | tf_op jit(solution)/shard_map/ppermute | solution.py:512
  181.8 24.5 %collective-permute-start.12 = (bf16[256,1024]{1,0:T(8,128)(2,1)S(1)}, bf16[256,1024]{1,0:T(8,128)(2,1)S(1)}, u32[]{:S(2)}, u32[]{:S(2)}) collective-permute-start(bf16[256,1024]{1,0:T(8,128)(2,1)S(1)} %add_convert_fusion.9), channel_id=1, source_target_pairs={{0,2},{1,3},{2,0},{3,1},{4,6},{5,7},{6,4},{7,5},{8,10},{9,11},{10,... | collective-permute-start | bytes 1572872 | tf_op jit(solution)/shard_map/ppermute | solution.py:512
  230.4 21.4 %collective-permute-start.18 = (bf16[512,1024]{1,0:T(8,128)(2,1)S(1)}, bf16[512,1024]{1,0:T(8,128)(2,1)S(1)}, u32[]{:S(2)}, u32[]{:S(2)}) collective-permute-start(bf16[512,1024]{1,0:T(8,128)(2,1)S(1)} %get-tuple-element.244), channel_id=1, source_target_pairs={{0,1},{1,0},{2,3},{3,2},{4,5},{5,4},{6,7},{7,6},{8,9},{9,8},{10,11... | collective-permute-start | bytes 3145736 | tf_op jit(solution)/shard_map/ppermute | solution.py:512
  274.1 32.7 %collective-permute-start.24 = (bf16[512,1024]{1,0:T(8,128)(2,1)}, bf16[512,1024]{1,0:T(8,128)(2,1)}, u32[]{:S(2)}, u32[]{:S(2)}) collective-permute-start(bf16[512,1024]{1,0:T(8,128)(2,1)} %get-tuple-element.274), channel_id=1, source_target_pairs={{0,1},{1,0},{2,3},{3,2},{4,5},{5,4},{6,7},{7,6},{8,9},{9,8},{10,11... | collective-permute-start | bytes 3145736 | tf_op jit(solution)/shard_map/ppermute | solution.py:512
  276.4 27.5 %collective-permute-start.23 = (bf16[256,1024]{1,0:T(8,128)(2,1)S(1)}, bf16[256,1024]{1,0:T(8,128)(2,1)S(1)}, u32[]{:S(2)}, u32[]{:S(2)}) collective-permute-start(bf16[256,1024]{1,0:T(8,128)(2,1)S(1)} %add_convert_fusion.5), channel_id=1, source_target_pairs={{0,2},{1,3},{2,0},{3,1},{4,6},{5,7},{6,4},{7,5},{8,10},{9,11},{10,... | collective-permute-start | bytes 1572872 | tf_op jit(solution)/shard_map/ppermute | solution.py:512
  278.4 26.9 %collective-permute-start.22 = (bf16[256,1024]{1,0:T(8,128)(2,1)S(1)}, bf16[256,1024]{1,0:T(8,128)(2,1)S(1)}, u32[]{:S(2)}, u32[]{:S(2)}) collective-permute-start(bf16[256,1024]{1,0:T(8,128)(2,1)S(1)} %add_convert_fusion.6), channel_id=1, source_target_pairs={{0,2},{1,3},{2,0},{3,1},{4,6},{5,7},{6,4},{7,5},{8,10},{9,11},{10,... | collective-permute-start | bytes 1572872 | tf_op jit(solution)/shard_map/ppermute | solution.py:512
  329.2 46.4 %all-to-all-start.2 = ((bf16[8,32,1024]{2,1,0:T(8,128)(2,1)}), bf16[8,32,1024]{2,1,0:T(8,128)(2,1)}, u32[]{:S(2)}, u32[]{:S(2)}) async-start(bf16[8,32,1024]{2,1,0:T(8,128)(2,1)} %bitcast.250), calls=%async_computation.2 | async-start | bytes 1048576 | tf_op jit(solution)/shard_map/all_to_all | solution.py:587
  338.8 31.3 %collective-permute-start.30 = (bf16[4,128,256]{2,1,0:T(8,128)(2,1)S(1)}, bf16[4,128,256]{2,1,0:T(8,128)(2,1)S(1)}, u32[]{:S(2)}, u32[]{:S(2)}) collective-permute-start(bf16[4,128,256]{2,1,0:T(8,128)(2,1)S(1)} %dynamic-slice_bitcast_fusion.2), channel_id=1, source_target_pairs={{0,4},{4,0},{8,12},{12,8},{16,20},{20,16},{24,28},{28,24},{1,5},{5... | collective-permute-start | bytes 786440 | tf_op jit(solution)/shard_map/ppermute | solution.py:512
  341.9 29.1 %collective-permute-start.29 = (bf16[256,1024]{1,0:T(8,128)(2,1)S(1)}, bf16[256,1024]{1,0:T(8,128)(2,1)S(1)}, u32[]{:S(2)}, u32[]{:S(2)}) collective-permute-start(bf16[256,1024]{1,0:T(8,128)(2,1)S(1)} %add_convert_fusion.2), channel_id=1, source_target_pairs={{0,2},{1,3},{2,0},{3,1},{4,6},{5,7},{6,4},{7,5},{8,10},{9,11},{10,... | collective-permute-start | bytes 1572872 | tf_op jit(solution)/shard_map/ppermute | solution.py:512
  343.8 29.4 %collective-permute-start.28 = (bf16[256,1024]{1,0:T(8,128)(2,1)S(1)}, bf16[256,1024]{1,0:T(8,128)(2,1)S(1)}, u32[]{:S(2)}, u32[]{:S(2)}) collective-permute-start(bf16[256,1024]{1,0:T(8,128)(2,1)S(1)} %add_convert_fusion.3), channel_id=1, source_target_pairs={{0,2},{1,3},{2,0},{3,1},{4,6},{5,7},{6,4},{7,5},{8,10},{9,11},{10,... | collective-permute-start | bytes 1572872 | tf_op jit(solution)/shard_map/ppermute | solution.py:512
  383.2 37.7 %all-to-all-start.3 = ((bf16[8,64,1024]{2,1,0:T(8,128)(2,1)}), bf16[8,64,1024]{2,1,0:T(8,128)(2,1)}, u32[]{:S(2)}, u32[]{:S(2)}) async-start(bf16[8,64,1024]{2,1,0:T(8,128)(2,1)} %bitcast.241), calls=%async_computation.4 | async-start | bytes 2097152 | tf_op jit(solution)/shard_map/all_to_all | solution.py:587
  389.3 21.6 %collective-permute-start.34 = (bf16[4,128,384]{2,1,0:T(8,128)(2,1)S(1)}, bf16[4,128,384]{2,1,0:T(8,128)(2,1)S(1)}, u32[]{:S(2)}, u32[]{:S(2)}) collective-permute-start(bf16[4,128,384]{2,1,0:T(8,128)(2,1)S(1)} %dynamic-slice_bitcast_fusion), channel_id=1, source_target_pairs={{0,4},{4,0},{8,12},{12,8},{16,20},{20,16},{24,28},{28,24},{1,5},{5... | collective-permute-start | bytes 1179656 | tf_op jit(solution)/shard_map/ppermute | solution.py:512
  391.2 27.4 %collective-permute-start.33 = (bf16[4,128,384]{2,1,0:T(8,128)(2,1)S(1)}, bf16[4,128,384]{2,1,0:T(8,128)(2,1)S(1)}, u32[]{:S(2)}, u32[]{:S(2)}) collective-permute-start(bf16[4,128,384]{2,1,0:T(8,128)(2,1)S(1)} %dynamic-slice_bitcast_fusion.1), channel_id=1, source_target_pairs={{0,4},{4,0},{8,12},{12,8},{16,20},{20,16},{24,28},{28,24},{1,5},{5... | collective-permute-start | bytes 1179656 | tf_op jit(solution)/shard_map/ppermute | solution.py:512
  392.7 26.9 %collective-permute-start.32 = (bf16[256,1024]{1,0:T(8,128)(2,1)S(1)}, bf16[256,1024]{1,0:T(8,128)(2,1)S(1)}, u32[]{:S(2)}, u32[]{:S(2)}) collective-permute-start(bf16[256,1024]{1,0:T(8,128)(2,1)S(1)} %add_convert_fusion.1), channel_id=1, source_target_pairs={{0,2},{1,3},{2,0},{3,1},{4,6},{5,7},{6,4},{7,5},{8,10},{9,11},{10,... | collective-permute-start | bytes 1572872 | tf_op jit(solution)/shard_map/ppermute | solution.py:512
  428.6 28.5 %collective-permute-start.42 = (bf16[256,1024]{1,0:T(8,128)(2,1)}, bf16[256,1024]{1,0:T(8,128)(2,1)}, u32[]{:S(2)}, u32[]{:S(2)}) collective-permute-start(bf16[256,1024]{1,0:T(8,128)(2,1)} %bitcast.54), channel_id=1, source_target_pairs={{0,2},{1,3},{2,0},{3,1},{4,6},{5,7},{6,4},{7,5},{8,10},{9,11},{10,... | collective-permute-start | bytes 1572872 | tf_op jit(solution)/shard_map/ppermute | solution.py:512
  429.2 26.2 %collective-permute-start.45 = (bf16[256,1024]{1,0:T(8,128)(2,1)}, bf16[256,1024]{1,0:T(8,128)(2,1)}, u32[]{:S(2)}, u32[]{:S(2)}) collective-permute-start(bf16[256,1024]{1,0:T(8,128)(2,1)} %bitcast.53), channel_id=1, source_target_pairs={{0,2},{1,3},{2,0},{3,1},{4,6},{5,7},{6,4},{7,5},{8,10},{9,11},{10,... | collective-permute-start | bytes 1572872 | tf_op jit(solution)/shard_map/ppermute | solution.py:512
  447.4 36.7 %all-to-all-start.4 = ((bf16[8,256,256]{2,1,0:T(8,128)(2,1)}), bf16[8,256,256]{2,1,0:T(8,128)(2,1)}, u32[]{:S(2)}, u32[]{:S(2)}) async-start(bf16[8,256,256]{2,1,0:T(8,128)(2,1)} %shard_map.277), calls=%async_computation.5 | async-start | bytes 2097152 | tf_op jit(solution)/shard_map/all_to_all | solution.py:587
  452.4 16.5 %collective-permute-start.44 = (bf16[512,1024]{1,0:T(8,128)(2,1)S(1)}, bf16[512,1024]{1,0:T(8,128)(2,1)}, u32[]{:S(2)}, u32[]{:S(2)}) collective-permute-start(bf16[512,1024]{1,0:T(8,128)(2,1)S(1)} %pad_maximum_fusion.13.near_ref), channel_id=1, source_target_pairs={{0,1},{1,0},{2,3},{3,2},{4,5},{5,4},{6,7},{7,6},{8,9},{9,8},{10,11... | collective-permute-start | bytes 3145736 | tf_op jit(solution)/shard_map/ppermute | solution.py:512
  456.5 17.3 %collective-permute-start.46 = (bf16[512,1024]{1,0:T(8,128)(2,1)S(1)}, bf16[512,1024]{1,0:T(8,128)(2,1)}, u32[]{:S(2)}, u32[]{:S(2)}) collective-permute-start(bf16[512,1024]{1,0:T(8,128)(2,1)S(1)} %constant_dynamic-update-slice_fusion.2.near_ref), channel_id=1, source_target_pairs={{0,1},{1,0},{2,3},{3,2},{4,5},{5,4},{6,7},{7,6},{8,9},{9,8},{10,11... | collective-permute-start | bytes 3145736 | tf_op jit(solution)/shard_map/ppermute | solution.py:512
  458.9 19.8 %collective-permute-start.43 = (bf16[512,1024]{1,0:T(8,128)(2,1)}, bf16[512,1024]{1,0:T(8,128)(2,1)}, u32[]{:S(2)}, u32[]{:S(2)}) collective-permute-start(bf16[512,1024]{1,0:T(8,128)(2,1)} %constant_dynamic-update-slice_fusion.near_ref), channel_id=1, source_target_pairs={{0,1},{1,0},{2,3},{3,2},{4,5},{5,4},{6,7},{7,6},{8,9},{9,8},{10,11... | collective-permute-start | bytes 3145736 | tf_op jit(solution)/shard_map/ppermute | solution.py:512
  484.0 24.6 %collective-permute-start.49 = (bf16[1,8,256,256]{3,2,1,0:T(8,128)(2,1)}, bf16[1,8,256,256]{3,2,1,0:T(8,128)(2,1)S(1)}, u32[]{:S(2)}, u32[]{:S(2)}) collective-permute-start(bf16[1,8,256,256]{3,2,1,0:T(8,128)(2,1)} %bitcast.86), channel_id=1, source_target_pairs={{0,2},{1,3},{2,0},{3,1},{4,6},{5,7},{6,4},{7,5},{8,10},{9,11},{10,... | collective-permute-start | bytes 3145736 | tf_op jit(solution)/shard_map/ppermute | solution.py:512
  484.7 26.7 %all-to-all-start.5 = ((bf16[8,32,1024]{2,1,0:T(8,128)(2,1)}), bf16[8,32,1024]{2,1,0:T(8,128)(2,1)S(1)}, u32[]{:S(2)}, u32[]{:S(2)}) async-start(bf16[8,32,1024]{2,1,0:T(8,128)(2,1)} %bitcast.87), calls=%async_computation.6 | async-start | bytes 1048576 | tf_op jit(solution)/shard_map/all_to_all | solution.py:587
  528.7 17.5 %collective-permute-start.55 = (f32[6,1280]{1,0:T(8,128)S(1)}, f32[6,1280]{1,0:T(8,128)S(1)}, u32[]{:S(2)}, u32[]{:S(2)}) collective-permute-start(f32[6,1280]{1,0:T(8,128)S(1)} %maximum_maximum_fusion), channel_id=1, source_target_pairs={{0,4},{4,0},{8,12},{12,8},{16,20},{20,16},{24,28},{28,24},{1,5},{5... | collective-permute-start | bytes 92168 | tf_op jit(solution)/shard_map/ppermute | solution.py:512
  (142 other events, 1086.6 us)
Sparse Core Ops, SparseCore 0:
  26.9 77.8 all-gather.2
  112.9 72.2 all-gather.4
  274.8 92.6 reduce-scatter.1

commit v6 on v5

--- a/solution.py
+++ b/solution.py
@@ -143,7 +143,7 @@
         else:
             send_ref[pl.ds(t * TILE - half, TILE), :] = branch.astype(low_type)
 
-def attention_forward(near, far, norms, weights, bias, place, segment):
+def attention_forward(near, far, norms, weights, bias, place, segment, place_col, segment_col):
     rows = 2 * near.shape[0]
     width = near.shape[1]
     cols = bias.shape[1] // 3
@@ -165,7 +165,7 @@
         scratch_shapes=[pltpu.VMEM((rows, 3 * cols), low_type)],
         compiler_params=pltpu.CompilerParams(vmem_limit_bytes=VMEM_BYTES),
         cost_estimate=LARGE,
-    )(near, far, norms, weights, bias, place[None, :], place[:, None], segment[None, :], segment[:, None])
+    )(near, far, norms, weights, bias, place[None, :], place_col, segment[None, :], segment_col)
 
 def attention_backward_kernel(
     near_ref, far_ref, weights_ref, place_row_ref, place_col_ref, seg_row_ref, seg_col_ref,
@@ -234,7 +234,8 @@
         else:
             send_ref[pl.ds(t * TILE - half, TILE), :] = normed.astype(low_type)
 
-def attention_backward(near, far, weights, place, segment, qkv, out, lse):
+def attention_backward(near, far, weights, place, segment, columns, qkv, out, lse):
+    place_col, segment_col = columns
     rows = 2 * near.shape[0]
     width = near.shape[1]
     cols = out.shape[1]
@@ -259,7 +260,7 @@
         ],
         compiler_params=pltpu.CompilerParams(vmem_limit_bytes=VMEM_BYTES),
         cost_estimate=LARGE,
-    )(near, far, weights, place[None, :], place[:, None], segment[None, :], segment[:, None], qkv, out, lse)
+    )(near, far, weights, place[None, :], place_col, segment[None, :], segment_col, qkv, out, lse)
 
 def mlp_kernel(normed_ref, grad_ref, weights_ref, bias_ref, active_ref, grad_up_ref, feed_ref, back_ref, sums_ref):
     rows, width = normed_ref.shape
@@ -712,7 +713,7 @@
 
     def attend(i, near, far):
         return attention_forward(
-            near, far, norms[:2], weights_one, bias_qkv, positions[i], segments[i]
+            near, far, norms[:2], weights_one, bias_qkv, positions[i], segments[i], *columns[i]
         )
 
     def second_share(hidden):
@@ -732,7 +733,7 @@
     def attend_back(i, near, far, kept):
         _, qkv, out, lse = kept
         return attention_backward(
-            near, far, weights_one, positions[i], segments[i], qkv, out, lse
+            near, far, weights_one, positions[i], segments[i], columns[i], qkv, out, lse
         )
 
     def first_back(i, grad_hidden, grad_normed):
@@ -745,6 +746,8 @@
     x_0, x_1 = arrived(picked)
     rows_0, rows_1 = x_0.astype(f32), x_1.astype(f32)
     rows_own = (rows_0, rows_1)
+    columns = [(positions[i][:, None], segments[i][:, None]) for i in micros]
+    x_0, columns = together(x_0, columns)
     x_0 = gather_chips(x_0)
     x_1 = gather_chips(x_1)
     keep = [(positions[i][:own_rows] < bounds[i][-2])[:, None] for i in micros]
@@ -889,8 +892,12 @@
     near_part, input_1, owned_grads = together(near_part, input_1, owned_grads)
     far_part = other_core(near_part)
     new_left, new_right, directions, squares = precondition(place, near_part, far_part, stats)
-    squares, input_1, vectors = together(squares, input_1, vectors)
+    input_1, squares = together(input_1, squares)
+    squares = jnp.sum(squares, axis=(1, 2))
+    square_total = sum_over(squares.reshape(1, slot_count), "mp")[0]
+    square_total, input_1 = together(square_total, input_1)
     input_1 = gather_chips(input_1)
+    vectors, input_1 = together(vectors, input_1)
     vectors = sum_over(vectors, "dp")
     inputs_given = give_back(
         1, returns[1], input_1, other_core(input_1), micro_count, inputs_given
@@ -900,8 +907,6 @@
     head_total = vectors[:, model_width:]
     norm_cols = norm_vectors.shape[1]
     norm_total = lax.dynamic_slice_in_dim(norm_all, data_index * norm_cols, norm_cols, 1)
-    squares = jnp.sum(squares, axis=(1, 2))
-    square_total = sum_over(squares.reshape(1, slot_count), "mp")[0]
     factor = lax.rsqrt(square_total / (model_width * model_width) + mean_eps)
     updated_blocks = jnp.stack(
         [

time: 576 us -> 581 us (level)
  waiting for transfers between devices: 180 us -> 186 us
    unnamed x226 -> x229, local copies, waits for them, and re-layouts: 34.6 us -> 34.4 us
  transfers between devices with their start and end apart: 67 -> 67, of which waited for: 26 -> 29; matrix products, arithmetic and copies ran while one was open for 17% -> 16% of each run, Pallas kernels for 23% -> 23%
where the time goes in v6:
time: 581 us; the launch traced here: 573 us
  waiting for transfers between devices  186 us (32%)
  Pallas kernels  153 us (26%)
  starting transfers between devices  76.7 us (13%)
  other arithmetic  71 us (12%)
  local copies, waits for them, and re-layouts  61.2 us (11%)
  between operations  17.4 us (3%)
  matrix products  7.27 us (1%)
    ppermute x58, waiting for transfers between devices, swap(): return lax.ppermute(values, axis, [(i, i ^ bit) for i in range(count)])  139 us
    all_to_all x6, waiting for transfers between devices, exchange(): return lax.all_to_all(rows, 'dp', split_axis=0, concat_axis=0, tiled=True)  46.9 us
    ppermute x58, starting transfers between devices, swap(): return lax.ppermute(values, axis, [(i, i ^ bit) for i in range(count)])  44.4 us
    pallas_call x2, Pallas kernels, attention_backward(): pl.pallas_call(attention_backward_kernel, out_shape=(shape((rows // 2, wi...  42.7 us
    pallas_call x2, Pallas kernels, attention_forward(): pl.pallas_call(attention_forward_kernel, out_shape=(shape((rows // 2, wid...  35.9 us
    unnamed x229, local copies, waits for them, and re-layouts  34.4 us
    all_to_all x6, starting transfers between devices, exchange(): return lax.all_to_all(rows, 'dp', split_axis=0, concat_axis=0, tiled=True)  32.2 us
    pallas_call x4, Pallas kernels, mlp(): pl.pallas_call(mlp_kernel, out_shape=(shape((rows, cols), low_type), shap...  24.1 us
  transfers between devices with their start and end apart: 67, of which 29 were waited for; matrix products, arithmetic and copies ran while one was open for 16% of the time, Pallas kernels for 23%

profile of v6, /device:TPU:0, one launch (start us, length us, event | category | flops | bytes accessed | tf_op | source)
XLA Modules:
  0.0 572.7 jit_solution(3865687379618481197)
XLA Ops:
  16.1 7.3 %all-to-all-start = ((bf16[8,64,1024]{2,1,0:T(8,128)(2,1)}), bf16[8,64,1024]{2,1,0:T(8,128)(2,1)S(1)}, u32[]{:S(2)}, u32[]{:S(2)}) async-start(bf16[8,64,1024]{2,1,0:T(8,128)(2,1)} %pad_maximum_fusion.3), calls=%async_computation | async-start | bytes 2097152 | tf_op jit(solution)/shard_map/all_to_all | solution.py:588
  27.3 31.4 %all-to-all-done = bf16[8,64,1024]{2,1,0:T(8,128)(2,1)S(1)} async-done(((bf16[8,64,1024]{2,1,0:T(8,128)(2,1)}), bf16[8,64,1024]{2,1,0:T(8,128)(2,1)S(1)}, u32[]{:S(2)}, u32[]{:S(2)}) %all-to-all-start) | async-done | bytes 1048608 | tf_op jit(solution)/shard_map/all_to_all | solution.py:588
  64.8 4.9 collective-permute-done
  69.8 5.4 all-to-all-start.1
  78.0 10.0 %collective-permute-done.1 = bf16[256,1024]{1,0:T(8,128)(2,1)S(1)} collective-permute-done((bf16[256,1024]{1,0:T(8,128)(2,1)S(1)}, bf16[256,1024]{1,0:T(8,128)(2,1)S(1)}, u32[]{:S(2)}, u32[]{:S(2)}) %collective-permute-start.1) | collective-permute-done | bytes 524320 | tf_op jit(solution)/shard_map/ppermute | solution.py:513
  93.0 15.4 %all-to-all-done.1 = bf16[8,64,1024]{2,1,0:T(8,128)(2,1)} async-done(((bf16[8,64,1024]{2,1,0:T(8,128)(2,1)}), bf16[8,64,1024]{2,1,0:T(8,128)(2,1)}, u32[]{:S(2)}, u32[]{:S(2)}) %all-to-all-start.1) | async-done | bytes 1048608 | tf_op jit(solution)/shard_map/all_to_all | solution.py:588
  119.1 19.2 %shard_map.266 = (f32[512,1024]{1,0:T(8,128)S(1)}, bf16[512,1024]{1,0:T(8,128)(2,1)}, bf16[1024,1024]{1,0:T(8,128)(2,1)S(1)}, bf16[1024,256]{1,0:T(8,128)(2,1)S(...) custom-call(bf16[512,1024]{1,0:T(8,128)(2,1)S(1)} %copy-done.29, ...), custom_call_target="tpu_custom_call" | custom-call | flops 20000000000 | bytes 1000000 | tf_op jit(solution)/shard_map/pallas_call | solution.py:152
  152.5 16.7 %shard_map.265 = (f32[512,1024]{1,0:T(8,128)S(1)}, bf16[512,1024]{1,0:T(8,128)(2,1)S(1)}, bf16[1024,1024]{1,0:T(8,128)(2,1)S(1)}, bf16[1024,256]{1,0:T(8,128)(2,...) custom-call(bf16[512,1024]{1,0:T(8,128)(2,1)S(1)} %copy-done.27, ...), custom_call_target="tpu_custom_call" | custom-call | flops 20000000000 | bytes 1000000 | tf_op jit(solution)/shard_map/pallas_call | solution.py:152
  182.8 12.5 %collective-permute-done.11 = bf16[256,1024]{1,0:T(8,128)(2,1)S(1)} collective-permute-done((bf16[256,1024]{1,0:T(8,128)(2,1)S(1)}, bf16[256,1024]{1,0:T(8,128)(2,1)S(1)}, u32[]{:S(2)}, u32[]{:S(2)}) %collective-permute-start.11) | collective-permute-done | bytes 524320 | tf_op jit(solution)/shard_map/ppermute | solution.py:513
  196.3 9.4 %collective-permute-done.12 = bf16[256,1024]{1,0:T(8,128)(2,1)S(1)} collective-permute-done((bf16[256,1024]{1,0:T(8,128)(2,1)S(1)}, bf16[256,1024]{1,0:T(8,128)(2,1)S(1)}, u32[]{:S(2)}, u32[]{:S(2)}) %collective-permute-start.12) | collective-permute-done | bytes 524320 | tf_op jit(solution)/shard_map/ppermute | solution.py:513
  210.3 5.4 shard_map.267
  217.0 5.4 collective-permute-done.14
  222.5 6.9 %shard_map.268 = (bf16[512,1024]{1,0:T(8,128)(2,1)S(1)}, bf16[512,1024]{1,0:T(8,128)(2,1)S(1)}, bf16[512,1024]{1,0:T(8,128)(2,1)S(1)}, bf16[512,1024]{1,0:T(8,128)(2,1)S(1)}, f32[1,1024]{1,0:T(1,128)S(1)}) custom-call(bf16[512,1024]{1,0:T(8,128)(2,1)S(1)} %collective-permute-done.13.normed_ref.refs_1_, ...), custom_call_target="tpu_custom_call" | custom-call | flops 11000000512 | bytes 1000000 | tf_op jit(solution)/shard_map/pallas_call | solution.py:292
  230.1 5.4 shard_map.269
  238.7 6.5 %shard_map.270 = (bf16[512,1024]{1,0:T(8,128)(2,1)S(1)}, bf16[512,1024]{1,0:T(8,128)(2,1)S(1)}, bf16[512,1024]{1,0:T(8,128)(2,1)}, bf16[512,1024]{1,0:T(8,128)(2,1)}, f32[1,1024]{1,0:T(1,128)S(1)}) custom-call(bf16[512,1024]{1,0:T(8,128)(2,1)S(1)} %collective-permute-done.15.normed_ref.refs_3_, bf16[512,1024]{1,0:T(8,128)(2,1)S(1)} %copy-done.47, ...), custom_call_target="tpu_custom_call" | custom-call | flops 11000000512 | bytes 1000000 | tf_op jit(solution)/shard_map/pallas_call | solution.py:292
  245.2 6.0 %collective-permute-done.17 = bf16[256,1024]{1,0:T(8,128)(2,1)S(1)} collective-permute-done((bf16[256,1024]{1,0:T(8,128)(2,1)S(1)}, bf16[256,1024]{1,0:T(8,128)(2,1)S(1)}, u32[]{:S(2)}, u32[]{:S(2)}) %collective-permute-start.17) | collective-permute-done | bytes 524320 | tf_op jit(solution)/shard_map/ppermute | solution.py:513
  254.1 10.6 %shard_map.271 = bf16[1024,2048]{1,0:T(8,128)(2,1)S(1)} custom-call(bf16[512,1024]{1,0:T(8,128)(2,1)S(1)} %copy-done.25, bf16[512,1024]{1,0:T(8,128)(2,1)S(1)} %collective-permute-done.13.normed_ref.refs_1_, bf16[512,1024]{1,0:T(8,128)(2,1)S(1)} %pad_maximum_fusion.9.normed_ref.refs_2_, bf16[512,1024]{1,0:T(8,128)(2,1)S(1)} %collective-permute-done.15.normed_ref.refs_3_, ...), custom_call_target="tpu_custom_call" | custom-call | flops 11000000512 | bytes 1000000 | tf_op jit(solution)/shard_map/pallas_call | solution.py:337
  281.1 22.6 %shard_map.273 = (f32[512,1024]{1,0:T(8,128)S(1)}, bf16[512,1024]{1,0:T(8,128)(2,1)}, bf16[1024,768]{1,0:T(8,128)(2,1)S(1)}, f32[1,768]{1,0:T(1,128)S(1)}) custom-call(bf16[512,1024]{1,0:T(8,128)(2,1)S(1)} %pad_maximum_fusion.10.near_ref.refs_0_, bf16[512,1024]{1,0:T(8,128)(2,1)} %collective-permute-done.21.far_ref.refs_1_, ...), custom_call_target="tpu_custom_call" | custom-call | flops 20000000000 | bytes 1000000 | tf_op jit(solution)/shard_map/pallas_call | solution.py:244
  313.6 11.2 %collective-permute-done.25 = bf16[256,1024]{1,0:T(8,128)(2,1)} collective-permute-done((bf16[256,1024]{1,0:T(8,128)(2,1)}, bf16[256,1024]{1,0:T(8,128)(2,1)}, u32[]{:S(2)}, u32[]{:S(2)}) %collective-permute-start.25) | collective-permute-done | bytes 524320 | tf_op jit(solution)/shard_map/ppermute | solution.py:513
  329.3 4.6 all-to-all-start.2
  345.4 20.0 %shard_map.275 = (f32[512,1024]{1,0:T(8,128)S(1)}, bf16[512,1024]{1,0:T(8,128)(2,1)S(1)}, bf16[1024,768]{1,0:T(8,128)(2,1)S(1)}, f32[1,768]{1,0:T(1,128)S(1)}) custom-call(bf16[512,1024]{1,0:T(8,128)(2,1)S(1)} %pad_maximum_fusion.11.refs_2_.near_ref, bf16[512,1024]{1,0:T(8,128)(2,1)S(1)} %collective-permute-done.27.refs_3_.far_ref, ...), custom_call_target="tpu_custom_call" | custom-call | flops 20000000000 | bytes 1000000 | tf_op jit(solution)/shard_map/pallas_call | solution.py:244
  383.6 4.5 all-to-all-start.3
  394.6 8.5 %collective-permute-done.35 = bf16[256,1024]{1,0:T(8,128)(2,1)S(1)} collective-permute-done((bf16[256,1024]{1,0:T(8,128)(2,1)}, bf16[256,1024]{1,0:T(8,128)(2,1)S(1)}, u32[]{:S(2)}, u32[]{:S(2)}) %collective-permute-start.35) | collective-permute-done | bytes 524320 | tf_op jit(solution)/shard_map/ppermute | solution.py:513
  404.3 7.0 %collective-permute-done.34 = bf16[4,128,384]{2,1,0:T(8,128)(2,1)S(1)} collective-permute-done((bf16[4,128,384]{2,1,0:T(8,128)(2,1)S(1)}, bf16[4,128,384]{2,1,0:T(8,128)(2,1)S(1)}, u32[]{:S(2)}, u32[]{:S(2)}) %collective-permute-start.34) | collective-permute-done | bytes 393248 | tf_op jit(solution)/shard_map/ppermute | solution.py:513
  411.4 7.6 %collective-permute-done.33 = bf16[4,128,384]{2,1,0:T(8,128)(2,1)S(1)} collective-permute-done((bf16[4,128,384]{2,1,0:T(8,128)(2,1)S(1)}, bf16[4,128,384]{2,1,0:T(8,128)(2,1)S(1)}, u32[]{:S(2)}, u32[]{:S(2)}) %collective-permute-start.33) | collective-permute-done | bytes 393248 | tf_op jit(solution)/shard_map/ppermute | solution.py:513
  469.3 4.9 shard_map.278.refs_0_
  474.3 4.9 shard_map.280.refs_0_
  479.2 5.2 shard_map.279
  485.1 6.2 %all-to-all-start.5 = ((bf16[8,32,1024]{2,1,0:T(8,128)(2,1)}), bf16[8,32,1024]{2,1,0:T(8,128)(2,1)S(1)}, u32[]{:S(2)}, u32[]{:S(2)}) async-start(bf16[8,32,1024]{2,1,0:T(8,128)(2,1)} %bitcast.86), calls=%async_computation.6 | async-start | bytes 1048576 | tf_op jit(solution)/shard_map/all_to_all | solution.py:588
  495.7 13.3 %collective-permute-done.49 = bf16[1,8,256,256]{3,2,1,0:T(8,128)(2,1)S(1)} collective-permute-done((bf16[1,8,256,256]{3,2,1,0:T(8,128)(2,1)}, bf16[1,8,256,256]{3,2,1,0:T(8,128)(2,1)S(1)}, u32[]{:S(2)}, u32[]{:S(2)}) %collective-permute-start.49) | collective-permute-done | bytes 1048608 | tf_op jit(solution)/shard_map/ppermute | solution.py:513
  516.2 11.9 %shard_map.281 = (f32[2,256,1024]{2,1,0:T(8,128)}, f32[2,256,1024]{2,1,0:T(8,128)}, f32[2,1024,256]{2,1,0:T(8,128)}, f32[2,1,256]{2,1,0:T(1,128)}) custom-call(s32[1]{0:T(128)} %bitcast.91.place_ref, bf16[2,8,256,256]{3,2,1,0:T(8,128)(2,1)} %pad_maximum_fusion.near_ref, bf16[2,8,256,256]{3,2,1,0:T(8,128)(2,1)} %collective-permute-done.50.far_ref, ...), custom_call_target="tpu_custom_call" | custom-call | flops 11000000512 | bytes 1000000 | tf_op jit(solution)/shard_map/pallas_call | solution.py:454
  534.4 12.2 %collective-permute-done.53 = bf16[256,1024]{1,0:T(8,128)(2,1)S(1)} collective-permute-done((bf16[256,1024]{1,0:T(8,128)(2,1)S(1)}, bf16[256,1024]{1,0:T(8,128)(2,1)S(1)}, u32[]{:S(2)}, u32[]{:S(2)}) %collective-permute-start.53) | collective-permute-done | bytes 524320 | tf_op jit(solution)/shard_map/ppermute | solution.py:513
  (551 shorter events, 232.1 us)
Async XLA Ops:
  16.1 42.6 %all-to-all-start = ((bf16[8,64,1024]{2,1,0:T(8,128)(2,1)}), bf16[8,64,1024]{2,1,0:T(8,128)(2,1)S(1)}, u32[]{:S(2)}, u32[]{:S(2)}) async-start(bf16[8,64,1024]{2,1,0:T(8,128)(2,1)} %pad_maximum_fusion.3), calls=%async_computation | async-start | bytes 2097152 | tf_op jit(solution)/shard_map/all_to_all | solution.py:588
  23.4 89.4 %all-gather.3.cloned.1.call-start = ((), (), s32[]{:S(2)}) async-start(), calls=%async_computation.7 | async-start | bytes 2654208 | tf_op jit(solution)/shard_map/all_gather | solution.py:745
  69.8 38.7 %all-to-all-start.1 = ((bf16[8,64,1024]{2,1,0:T(8,128)(2,1)}), bf16[8,64,1024]{2,1,0:T(8,128)(2,1)}, u32[]{:S(2)}, u32[]{:S(2)}) async-start(bf16[8,64,1024]{2,1,0:T(8,128)(2,1)} %pad_maximum_fusion.2), calls=%async_computation.1 | async-start | bytes 2097152 | tf_op jit(solution)/shard_map/all_to_all | solution.py:588
  75.2 131.7 %all-gather.5.cloned.1.call-start = ((), (), s32[]{:S(2)}) async-start(), calls=%async_computation.8 | async-start | bytes 4718592 | tf_op jit(solution)/shard_map/all_gather | solution.py:764
  88.1 23.7 %collective-permute-start.3 = (bf16[512,1024]{1,0:T(8,128)(2,1)S(1)}, bf16[512,1024]{1,0:T(8,128)(2,1)S(1)}, u32[]{:S(2)}, u32[]{:S(2)}) collective-permute-start(bf16[512,1024]{1,0:T(8,128)(2,1)S(1)} %pad_maximum_fusion.5.near_ref), channel_id=1, source_target_pairs={{0,1},{1,0},{2,3},{3,2},{4,5},{5,4},{6,7},{7,6},{8,9},{9,8},{10,11... | collective-permute-start | bytes 3145736 | tf_op jit(solution)/shard_map/ppermute | solution.py:513
  88.2 24.6 %collective-permute-start.2 = (bf16[512,1024]{1,0:T(8,128)(2,1)S(1)}, bf16[512,1024]{1,0:T(8,128)(2,1)}, u32[]{:S(2)}, u32[]{:S(2)}) collective-permute-start(bf16[512,1024]{1,0:T(8,128)(2,1)S(1)} %pad_maximum_fusion.4.near_ref), channel_id=1, source_target_pairs={{0,1},{1,0},{2,3},{3,2},{4,5},{5,4},{6,7},{7,6},{8,9},{9,8},{10,11... | collective-permute-start | bytes 3145736 | tf_op jit(solution)/shard_map/ppermute | solution.py:513
  112.8 263.1 %reduce-scatter.2.cloned.1.call-start = ((), (), s32[]{:S(2)}) async-start(), calls=%async_computation.9 | async-start | bytes 4718592 | tf_op jit(solution)/shard_map/reduce_scatter | solution.py:807
  114.2 28.3 %collective-permute-start.4 = (bf16[256,1024]{1,0:T(8,128)(2,1)}, bf16[256,1024]{1,0:T(8,128)(2,1)S(1)}, u32[]{:S(2)}, u32[]{:S(2)}) collective-permute-start(bf16[256,1024]{1,0:T(8,128)(2,1)} %bitcast_select_fusion), channel_id=1, source_target_pairs={{0,2},{1,3},{2,0},{3,1},{4,6},{5,7},{6,4},{7,5},{8,10},{9,11},{10,... | collective-permute-start | bytes 1572872 | tf_op jit(solution)/shard_map/ppermute | solution.py:513
  149.1 25.4 %collective-permute-start.7 = (bf16[256,1024]{1,0:T(8,128)(2,1)S(1)}, bf16[256,1024]{1,0:T(8,128)(2,1)S(1)}, u32[]{:S(2)}, u32[]{:S(2)}) collective-permute-start(bf16[256,1024]{1,0:T(8,128)(2,1)S(1)} %add_convert_fusion.11), channel_id=1, source_target_pairs={{0,2},{1,3},{2,0},{3,1},{4,6},{5,7},{6,4},{7,5},{8,10},{9,11},{10,... | collective-permute-start | bytes 1572872 | tf_op jit(solution)/shard_map/ppermute | solution.py:513
  149.7 24.7 %collective-permute-start.8 = (bf16[256,1024]{1,0:T(8,128)(2,1)}, bf16[256,1024]{1,0:T(8,128)(2,1)S(1)}, u32[]{:S(2)}, u32[]{:S(2)}) collective-permute-start(bf16[256,1024]{1,0:T(8,128)(2,1)} %bitcast_select_fusion.1), channel_id=1, source_target_pairs={{0,2},{1,3},{2,0},{3,1},{4,6},{5,7},{6,4},{7,5},{8,10},{9,11},{10,... | collective-permute-start | bytes 1572872 | tf_op jit(solution)/shard_map/ppermute | solution.py:513
  181.2 24.5 %collective-permute-start.12 = (bf16[256,1024]{1,0:T(8,128)(2,1)S(1)}, bf16[256,1024]{1,0:T(8,128)(2,1)S(1)}, u32[]{:S(2)}, u32[]{:S(2)}) collective-permute-start(bf16[256,1024]{1,0:T(8,128)(2,1)S(1)} %add_convert_fusion.9), channel_id=1, source_target_pairs={{0,2},{1,3},{2,0},{3,1},{4,6},{5,7},{6,4},{7,5},{8,10},{9,11},{10,... | collective-permute-start | bytes 1572872 | tf_op jit(solution)/shard_map/ppermute | solution.py:513
  230.0 21.5 %collective-permute-start.18 = (bf16[512,1024]{1,0:T(8,128)(2,1)S(1)}, bf16[512,1024]{1,0:T(8,128)(2,1)S(1)}, u32[]{:S(2)}, u32[]{:S(2)}) collective-permute-start(bf16[512,1024]{1,0:T(8,128)(2,1)S(1)} %get-tuple-element.257), channel_id=1, source_target_pairs={{0,1},{1,0},{2,3},{3,2},{4,5},{5,4},{6,7},{7,6},{8,9},{9,8},{10,11... | collective-permute-start | bytes 3145736 | tf_op jit(solution)/shard_map/ppermute | solution.py:513
  273.9 32.8 %collective-permute-start.24 = (bf16[512,1024]{1,0:T(8,128)(2,1)}, bf16[512,1024]{1,0:T(8,128)(2,1)}, u32[]{:S(2)}, u32[]{:S(2)}) collective-permute-start(bf16[512,1024]{1,0:T(8,128)(2,1)} %get-tuple-element.287), channel_id=1, source_target_pairs={{0,1},{1,0},{2,3},{3,2},{4,5},{5,4},{6,7},{7,6},{8,9},{9,8},{10,11... | collective-permute-start | bytes 3145736 | tf_op jit(solution)/shard_map/ppermute | solution.py:513
  276.2 27.6 %collective-permute-start.23 = (bf16[256,1024]{1,0:T(8,128)(2,1)S(1)}, bf16[256,1024]{1,0:T(8,128)(2,1)S(1)}, u32[]{:S(2)}, u32[]{:S(2)}) collective-permute-start(bf16[256,1024]{1,0:T(8,128)(2,1)S(1)} %add_convert_fusion.5), channel_id=1, source_target_pairs={{0,2},{1,3},{2,0},{3,1},{4,6},{5,7},{6,4},{7,5},{8,10},{9,11},{10,... | collective-permute-start | bytes 1572872 | tf_op jit(solution)/shard_map/ppermute | solution.py:513
  278.3 26.9 %collective-permute-start.22 = (bf16[256,1024]{1,0:T(8,128)(2,1)S(1)}, bf16[256,1024]{1,0:T(8,128)(2,1)S(1)}, u32[]{:S(2)}, u32[]{:S(2)}) collective-permute-start(bf16[256,1024]{1,0:T(8,128)(2,1)S(1)} %add_convert_fusion.6), channel_id=1, source_target_pairs={{0,2},{1,3},{2,0},{3,1},{4,6},{5,7},{6,4},{7,5},{8,10},{9,11},{10,... | collective-permute-start | bytes 1572872 | tf_op jit(solution)/shard_map/ppermute | solution.py:513
  309.7 16.3 %collective-permute-start.26 = (bf16[512,1024]{1,0:T(8,128)(2,1)}, bf16[512,1024]{1,0:T(8,128)(2,1)}, u32[]{:S(2)}, u32[]{:S(2)}) collective-permute-start(bf16[512,1024]{1,0:T(8,128)(2,1)} %get-tuple-element.293), channel_id=1, source_target_pairs={{0,1},{1,0},{2,3},{3,2},{4,5},{5,4},{6,7},{7,6},{8,9},{9,8},{10,11... | collective-permute-start | bytes 3145736 | tf_op jit(solution)/shard_map/ppermute | solution.py:513
  329.3 46.6 %all-to-all-start.2 = ((bf16[8,32,1024]{2,1,0:T(8,128)(2,1)}), bf16[8,32,1024]{2,1,0:T(8,128)(2,1)}, u32[]{:S(2)}, u32[]{:S(2)}) async-start(bf16[8,32,1024]{2,1,0:T(8,128)(2,1)} %bitcast.248), calls=%async_computation.2 | async-start | bytes 1048576 | tf_op jit(solution)/shard_map/all_to_all | solution.py:588
  338.8 31.6 %collective-permute-start.30 = (bf16[4,128,256]{2,1,0:T(8,128)(2,1)S(1)}, bf16[4,128,256]{2,1,0:T(8,128)(2,1)S(1)}, u32[]{:S(2)}, u32[]{:S(2)}) collective-permute-start(bf16[4,128,256]{2,1,0:T(8,128)(2,1)S(1)} %dynamic-slice_bitcast_fusion.2), channel_id=1, source_target_pairs={{0,4},{4,0},{8,12},{12,8},{16,20},{20,16},{24,28},{28,24},{1,5},{5... | collective-permute-start | bytes 786440 | tf_op jit(solution)/shard_map/ppermute | solution.py:513
  342.0 29.3 %collective-permute-start.29 = (bf16[256,1024]{1,0:T(8,128)(2,1)S(1)}, bf16[256,1024]{1,0:T(8,128)(2,1)S(1)}, u32[]{:S(2)}, u32[]{:S(2)}) collective-permute-start(bf16[256,1024]{1,0:T(8,128)(2,1)S(1)} %add_convert_fusion.2), channel_id=1, source_target_pairs={{0,2},{1,3},{2,0},{3,1},{4,6},{5,7},{6,4},{7,5},{8,10},{9,11},{10,... | collective-permute-start | bytes 1572872 | tf_op jit(solution)/shard_map/ppermute | solution.py:513
  344.0 29.5 %collective-permute-start.28 = (bf16[256,1024]{1,0:T(8,128)(2,1)S(1)}, bf16[256,1024]{1,0:T(8,128)(2,1)S(1)}, u32[]{:S(2)}, u32[]{:S(2)}) collective-permute-start(bf16[256,1024]{1,0:T(8,128)(2,1)S(1)} %add_convert_fusion.3), channel_id=1, source_target_pairs={{0,2},{1,3},{2,0},{3,1},{4,6},{5,7},{6,4},{7,5},{8,10},{9,11},{10,... | collective-permute-start | bytes 1572872 | tf_op jit(solution)/shard_map/ppermute | solution.py:513
  383.6 37.7 %all-to-all-start.3 = ((bf16[8,64,1024]{2,1,0:T(8,128)(2,1)}), bf16[8,64,1024]{2,1,0:T(8,128)(2,1)}, u32[]{:S(2)}, u32[]{:S(2)}) async-start(bf16[8,64,1024]{2,1,0:T(8,128)(2,1)} %bitcast.239), calls=%async_computation.4 | async-start | bytes 2097152 | tf_op jit(solution)/shard_map/all_to_all | solution.py:588
  389.7 21.6 %collective-permute-start.34 = (bf16[4,128,384]{2,1,0:T(8,128)(2,1)S(1)}, bf16[4,128,384]{2,1,0:T(8,128)(2,1)S(1)}, u32[]{:S(2)}, u32[]{:S(2)}) collective-permute-start(bf16[4,128,384]{2,1,0:T(8,128)(2,1)S(1)} %dynamic-slice_bitcast_fusion), channel_id=1, source_target_pairs={{0,4},{4,0},{8,12},{12,8},{16,20},{20,16},{24,28},{28,24},{1,5},{5... | collective-permute-start | bytes 1179656 | tf_op jit(solution)/shard_map/ppermute | solution.py:513
  391.8 27.2 %collective-permute-start.33 = (bf16[4,128,384]{2,1,0:T(8,128)(2,1)S(1)}, bf16[4,128,384]{2,1,0:T(8,128)(2,1)S(1)}, u32[]{:S(2)}, u32[]{:S(2)}) collective-permute-start(bf16[4,128,384]{2,1,0:T(8,128)(2,1)S(1)} %dynamic-slice_bitcast_fusion.1), channel_id=1, source_target_pairs={{0,4},{4,0},{8,12},{12,8},{16,20},{20,16},{24,28},{28,24},{1,5},{5... | collective-permute-start | bytes 1179656 | tf_op jit(solution)/shard_map/ppermute | solution.py:513
  393.1 26.8 %collective-permute-start.32 = (bf16[256,1024]{1,0:T(8,128)(2,1)S(1)}, bf16[256,1024]{1,0:T(8,128)(2,1)S(1)}, u32[]{:S(2)}, u32[]{:S(2)}) collective-permute-start(bf16[256,1024]{1,0:T(8,128)(2,1)S(1)} %add_convert_fusion.1), channel_id=1, source_target_pairs={{0,2},{1,3},{2,0},{3,1},{4,6},{5,7},{6,4},{7,5},{8,10},{9,11},{10,... | collective-permute-start | bytes 1572872 | tf_op jit(solution)/shard_map/ppermute | solution.py:513
  429.0 28.5 %collective-permute-start.42 = (bf16[256,1024]{1,0:T(8,128)(2,1)}, bf16[256,1024]{1,0:T(8,128)(2,1)}, u32[]{:S(2)}, u32[]{:S(2)}) collective-permute-start(bf16[256,1024]{1,0:T(8,128)(2,1)} %bitcast.54), channel_id=1, source_target_pairs={{0,2},{1,3},{2,0},{3,1},{4,6},{5,7},{6,4},{7,5},{8,10},{9,11},{10,... | collective-permute-start | bytes 1572872 | tf_op jit(solution)/shard_map/ppermute | solution.py:513
  429.6 26.2 %collective-permute-start.45 = (bf16[256,1024]{1,0:T(8,128)(2,1)}, bf16[256,1024]{1,0:T(8,128)(2,1)}, u32[]{:S(2)}, u32[]{:S(2)}) collective-permute-start(bf16[256,1024]{1,0:T(8,128)(2,1)} %bitcast.53), channel_id=1, source_target_pairs={{0,2},{1,3},{2,0},{3,1},{4,6},{5,7},{6,4},{7,5},{8,10},{9,11},{10,... | collective-permute-start | bytes 1572872 | tf_op jit(solution)/shard_map/ppermute | solution.py:513
  447.7 36.7 %all-to-all-start.4 = ((bf16[8,256,256]{2,1,0:T(8,128)(2,1)}), bf16[8,256,256]{2,1,0:T(8,128)(2,1)}, u32[]{:S(2)}, u32[]{:S(2)}) async-start(bf16[8,256,256]{2,1,0:T(8,128)(2,1)} %shard_map.277), calls=%async_computation.5 | async-start | bytes 2097152 | tf_op jit(solution)/shard_map/all_to_all | solution.py:588
  452.8 16.5 %collective-permute-start.44 = (bf16[512,1024]{1,0:T(8,128)(2,1)S(1)}, bf16[512,1024]{1,0:T(8,128)(2,1)}, u32[]{:S(2)}, u32[]{:S(2)}) collective-permute-start(bf16[512,1024]{1,0:T(8,128)(2,1)S(1)} %pad_maximum_fusion.13.near_ref), channel_id=1, source_target_pairs={{0,1},{1,0},{2,3},{3,2},{4,5},{5,4},{6,7},{7,6},{8,9},{9,8},{10,11... | collective-permute-start | bytes 3145736 | tf_op jit(solution)/shard_map/ppermute | solution.py:513
  456.9 17.3 %collective-permute-start.46 = (bf16[512,1024]{1,0:T(8,128)(2,1)S(1)}, bf16[512,1024]{1,0:T(8,128)(2,1)}, u32[]{:S(2)}, u32[]{:S(2)}) collective-permute-start(bf16[512,1024]{1,0:T(8,128)(2,1)S(1)} %constant_dynamic-update-slice_fusion.2.near_ref), channel_id=1, source_target_pairs={{0,1},{1,0},{2,3},{3,2},{4,5},{5,4},{6,7},{7,6},{8,9},{9,8},{10,11... | collective-permute-start | bytes 3145736 | tf_op jit(solution)/shard_map/ppermute | solution.py:513
  459.4 19.8 %collective-permute-start.43 = (bf16[512,1024]{1,0:T(8,128)(2,1)}, bf16[512,1024]{1,0:T(8,128)(2,1)}, u32[]{:S(2)}, u32[]{:S(2)}) collective-permute-start(bf16[512,1024]{1,0:T(8,128)(2,1)} %constant_dynamic-update-slice_fusion.near_ref), channel_id=1, source_target_pairs={{0,1},{1,0},{2,3},{3,2},{4,5},{5,4},{6,7},{7,6},{8,9},{9,8},{10,11... | collective-permute-start | bytes 3145736 | tf_op jit(solution)/shard_map/ppermute | solution.py:513
  484.4 24.5 %collective-permute-start.49 = (bf16[1,8,256,256]{3,2,1,0:T(8,128)(2,1)}, bf16[1,8,256,256]{3,2,1,0:T(8,128)(2,1)S(1)}, u32[]{:S(2)}, u32[]{:S(2)}) collective-permute-start(bf16[1,8,256,256]{3,2,1,0:T(8,128)(2,1)} %bitcast.85), channel_id=1, source_target_pairs={{0,2},{1,3},{2,0},{3,1},{4,6},{5,7},{6,4},{7,5},{8,10},{9,11},{10,... | collective-permute-start | bytes 3145736 | tf_op jit(solution)/shard_map/ppermute | solution.py:513
  485.1 26.6 %all-to-all-start.5 = ((bf16[8,32,1024]{2,1,0:T(8,128)(2,1)}), bf16[8,32,1024]{2,1,0:T(8,128)(2,1)S(1)}, u32[]{:S(2)}, u32[]{:S(2)}) async-start(bf16[8,32,1024]{2,1,0:T(8,128)(2,1)} %bitcast.86), calls=%async_computation.6 | async-start | bytes 1048576 | tf_op jit(solution)/shard_map/all_to_all | solution.py:588
  (145 other events, 1013.3 us)
Sparse Core Ops, SparseCore 0:
  27.0 77.8 all-gather.2
  112.9 72.1 all-gather.4
  274.6 92.8 reduce-scatter.1
